TPU v7x, 32 devices: a whole 2x2x4 slice. The times are simulated.
32 devices in a mesh: dp: 8 (over z, y), rep: 4 (over x, core).
Axes of the slice: x: 2, y: 2, z: 4, core: 2. Of those that a mesh axis runs over, the one named last changes fastest.
Arguments:
- latents: float32 [2, 32, 4096], P(None, ('dp', 'rep')), may hold values from -5 to 5
- noise_field: float32 [2, 32, 4096], P(None, ('dp', 'rep')), may hold values from -12 to 12
- timesteps: int32 [2, 32], P(None, ('dp', 'rep')), may hold values from 0 to 999
- labels: int32 [2, 32], P(None, ('dp', 'rep')), may hold values from 0 to 31
- drop_mask: int32 [2, 32], P(None, ('dp', 'rep')), may hold values 0 or 1
- roster: float32 [2, 1000], replicated, may hold values from 0.1 to 1
- w_qkv: float32 [2, 768, 2304], P(None, 'dp'), may hold values from -1 to 1
- w_proj: float32 [2, 768, 768], P(None, 'dp'), may hold values from -2 to 2
- w_fc1: float32 [2, 768, 3072], P(None, 'dp'), may hold values from -1 to 1
- w_fc2: float32 [2, 3072, 768], P(None, 'dp'), may hold values from -1 to 1
- w_mod: float32 [768, 10752], P('dp'), may hold values from -1 to 1
- row_qkv: float32 [2, 768], P(None, 'dp'), may hold values from 1.8119812e-07 to 7.2479247e-07
- col_qkv: float32 [2, 2304], replicated, may hold values from 1.8119812e-07 to 7.2479247e-07
- row_proj: float32 [2, 768], P(None, 'dp'), may hold values from 1.8119812e-07 to 7.2479247e-07
- col_proj: float32 [2, 768], replicated, may hold values from 1.8119812e-07 to 7.2479247e-07
- row_fc1: float32 [2, 768], P(None, 'dp'), may hold values from 1.8119812e-07 to 7.2479247e-07
- col_fc1: float32 [2, 3072], replicated, may hold values from 1.8119812e-07 to 7.2479247e-07
- row_fc2: float32 [2, 3072], P(None, 'dp'), may hold values from 1.8119812e-07 to 7.2479247e-07
- col_fc2: float32 [2, 768], replicated, may hold values from 1.8119812e-07 to 7.2479247e-07
- row_mod: float32 [768], P('dp'), may hold values from 1.8119812e-07 to 7.2479247e-07
- col_mod: float32 [10752], replicated, may hold values from 1.8119812e-07 to 7.2479247e-07
- small: float32 [861712], replicated, may hold values from -8 to 8
- small_second: float32 [861712], replicated, may hold values from 1.8119812e-07 to 7.2479247e-07
Outputs:
- loss_total: float32 [], replicated
- qkv_new: float32 [2, 768, 2304], P(None, 'dp')
- qkv_grad: float32 [2, 768, 2304], P(None, 'dp')
- qkv_row: float32 [2, 768], P(None, 'dp')
- qkv_col: float32 [2, 2304], replicated
- qkv_low: bfloat16 [2, 768, 2304], P(None, 'dp')
- proj_new: float32 [2, 768, 768], P(None, 'dp')
- proj_grad: float32 [2, 768, 768], P(None, 'dp')
- proj_row: float32 [2, 768], P(None, 'dp')
- proj_col: float32 [2, 768], replicated
- proj_low: bfloat16 [2, 768, 768], P(None, 'dp')
- fc1_new: float32 [2, 768, 3072], P(None, 'dp')
- fc1_grad: float32 [2, 768, 3072], P(None, 'dp')
- fc1_row: float32 [2, 768], P(None, 'dp')
- fc1_col: float32 [2, 3072], replicated
- fc1_low: bfloat16 [2, 768, 3072], P(None, 'dp')
- fc2_new: float32 [2, 3072, 768], P(None, 'dp')
- fc2_grad: float32 [2, 3072, 768], P(None, 'dp')
- fc2_row: float32 [2, 3072], P(None, 'dp')
- fc2_col: float32 [2, 768], replicated
- fc2_low: bfloat16 [2, 3072, 768], P(None, 'dp')
- mod_new: float32 [768, 10752], P('dp')
- mod_grad: float32 [768, 10752], P('dp')
- mod_row: float32 [768], P('dp')
- mod_col: float32 [10752], replicated
- mod_low: bfloat16 [768, 10752], P('dp')
- small_grad: float32 [861712], replicated
- small_second_new: float32 [861712], replicated
- small_new: float32 [861712], replicated
- small_low: bfloat16 [861712], replicated
All inputs are finite; a program needn't handle non-finite values. No bound on the sum of `drop_mask` on one device may be relied on, other than what follows from the above.
Results may differ from a plain program's by a relative error of at most 0.0039.
The roundings to bfloat16 on the way count: a program that leaves them out, or rounds other values in their place, can miss the bound.
Values may be sent and summed in bfloat16 or wider, within the bound.
A program may use at most 384 MiB of HBM per device.

v0:
```python
from functools import partial
import math

import jax
import jax.numpy as jnp
from jax import lax
from jax.sharding import PartitionSpec as P

D = 768
HEADS = 12
FF = 3072
FREQ = 256
CLASSES = 32
GRID = 16
PATCH = 2
CHAN = 4
LAYERS = 2
MICRO = 2
STEPS_T = 1000
STEP = 10
PDIM = 16
MOD = 10752


HIGHEST = lax.Precision.HIGHEST
EPS_NORM = 1e-06
EPS_ONE = 1e-30
CLIP = 0.5
RATE = 0.6


def product(left, right):
    return jnp.dot(left, right, preferred_element_type=jnp.float32)


def layout():
    return [
        ("patch_w", (PDIM, D)),
        ("patch_b", (D,)),
        ("time1_w", (FREQ, D)),
        ("time1_b", (D,)),
        ("time2_w", (D, D)),
        ("time2_b", (D,)),
        ("class_tab", (CLASSES + 1, D)),
        ("mod_b", (MOD,)),
        ("head_w", (D, PDIM)),
        ("head_b", (PDIM,)),
        ("block_b", (LAYERS, 4 * D + FF)),
    ]


def unpack(small):
    pieces = {}
    offset = 0
    for piece_name, piece_dims in layout():
        piece_size = math.prod(piece_dims)
        pieces[piece_name] = small[offset : offset + piece_size].reshape(piece_dims)
        offset += piece_size
    return pieces


def position_table():
    quarter = D // 4
    omega = jnp.exp(-math.log(10000.0) * jnp.arange(quarter, dtype=jnp.float32) / quarter)
    places = jnp.arange(GRID * GRID, dtype=jnp.int32)
    across = (places // GRID).astype(jnp.float32)[:, None] * omega
    downward = (places % GRID).astype(jnp.float32)[:, None] * omega
    return jnp.concatenate(
        [jnp.sin(across), jnp.cos(across), jnp.sin(downward), jnp.cos(downward)], axis=1
    )


def time_features(timesteps):
    half_count = FREQ // 2
    frequency = jnp.exp(-math.log(10000.0) * jnp.arange(half_count, dtype=jnp.float32) / half_count)
    angles = timesteps.astype(jnp.float32)[:, None] * frequency
    return jnp.concatenate([jnp.cos(angles), jnp.sin(angles)], axis=1)


def patchify(flat):
    number = flat.shape[0]
    blocks = flat.reshape(number, GRID, PATCH, GRID, PATCH, CHAN).transpose(0, 1, 3, 2, 4, 5)
    return blocks.reshape(number, GRID * GRID, PDIM)


def norm_rows(values):
    centered = values - jnp.mean(values, axis=-1, keepdims=True)
    inverse = lax.rsqrt(jnp.mean(centered * centered, axis=-1, keepdims=True) + EPS_NORM)
    return (centered * inverse, inverse)


def norm_back(grad, normed, inverse):
    return inverse * (
        grad
        - jnp.mean(grad, axis=-1, keepdims=True)
        - normed * jnp.mean(grad * normed, axis=-1, keepdims=True)
    )


def layer_forward(residual, spans, weights, biases):
    number, seq_tokens = (residual.shape[0], residual.shape[1])
    scaling = 1.0 / math.sqrt(D // HEADS)
    blank_bias = jnp.zeros((D,), jnp.float32)
    qkv_bias = jnp.concatenate([biases[:D], blank_bias, biases[D : 2 * D]])
    normed_a, inverse_a = norm_rows(residual)
    mixed_a = (normed_a * (1.0 + spans[1]) + spans[0]).astype(jnp.bfloat16)
    projected = (product(mixed_a.reshape(-1, D), weights[0]) + qkv_bias).astype(jnp.bfloat16)
    projected = projected.reshape(number, seq_tokens, 3, HEADS, D // HEADS)
    scores = (
        jnp.einsum(
            "bqhd,bkhd->bhqk",
            projected[:, :, 0],
            projected[:, :, 1],
            preferred_element_type=jnp.float32,
        )
        * scaling
    )
    total_lse = jax.nn.logsumexp(scores, axis=-1, keepdims=True)
    attention = jnp.exp(scores - total_lse).astype(jnp.bfloat16)
    attended = jnp.einsum(
        "bhqk,bkhd->bqhd", attention, projected[:, :, 2], preferred_element_type=jnp.float32
    )
    attended = attended.astype(jnp.bfloat16).reshape(-1, D)
    branch_a = product(attended, weights[1]) + biases[2 * D : 3 * D]
    middle = residual + spans[2] * branch_a.reshape(number, seq_tokens, D)
    normed_b, inverse_b = norm_rows(middle)
    mixed_b = (normed_b * (1.0 + spans[4]) + spans[3]).astype(jnp.bfloat16)
    hidden = product(mixed_b.reshape(-1, D), weights[2]) + biases[3 * D : 3 * D + FF]
    activated = jax.nn.gelu(hidden, approximate=True).astype(jnp.bfloat16)
    branch_b = product(activated, weights[3]) + biases[3 * D + FF :]
    result = middle + spans[5] * branch_b.reshape(number, seq_tokens, D)
    kept = (
        normed_a,
        inverse_a,
        mixed_a,
        projected,
        total_lse,
        attended,
        branch_a,
        normed_b,
        inverse_b,
        mixed_b,
        hidden,
        activated,
        branch_b,
    )
    return (result, kept)


def layer_backward(grad_out, spans, weights, kept):
    (
        normed_a,
        inverse_a,
        mixed_a,
        projected,
        total_lse,
        attended,
        branch_a,
        normed_b,
        inverse_b,
        mixed_b,
        hidden,
        activated,
        branch_b,
    ) = kept
    number, seq_tokens = (grad_out.shape[0], grad_out.shape[1])
    scaling = 1.0 / math.sqrt(D // HEADS)
    grad_b = (spans[5] * grad_out).reshape(-1, D).astype(jnp.bfloat16)
    gate_b = jnp.sum(grad_out * branch_b.reshape(number, seq_tokens, D), axis=1)
    grad_fc2 = product(activated.T, grad_b)
    bias_fc2 = jnp.sum(grad_b.astype(jnp.float32), axis=0)
    _, gelu_pull = jax.vjp(partial(jax.nn.gelu, approximate=True), hidden)
    grad_hidden = gelu_pull(product(grad_b, weights[3].T))[0].astype(jnp.bfloat16)
    grad_fc1 = product(mixed_b.reshape(-1, D).T, grad_hidden)
    bias_fc1 = jnp.sum(grad_hidden.astype(jnp.float32), axis=0)
    grad_mixed = product(grad_hidden, weights[2].T).reshape(number, seq_tokens, D)
    shift_b = jnp.sum(grad_mixed, axis=1)
    scale_b = jnp.sum(grad_mixed * normed_b, axis=1)
    grad_mid = grad_out + norm_back(grad_mixed * (1.0 + spans[4]), normed_b, inverse_b)
    grad_a = (spans[2] * grad_mid).reshape(-1, D).astype(jnp.bfloat16)
    gate_a = jnp.sum(grad_mid * branch_a.reshape(number, seq_tokens, D), axis=1)
    grad_proj = product(attended.T, grad_a)
    bias_proj = jnp.sum(grad_a.astype(jnp.float32), axis=0)
    grad_att = (
        product(grad_a, weights[1].T)
        .astype(jnp.bfloat16)
        .reshape(number, seq_tokens, HEADS, D // HEADS)
    )
    query, keys, values = (projected[:, :, 0], projected[:, :, 1], projected[:, :, 2])
    scores = (
        jnp.einsum("bqhd,bkhd->bhqk", query, keys, preferred_element_type=jnp.float32) * scaling
    )
    attention = jnp.exp(scores - total_lse)
    grad_values = jnp.einsum(
        "bhqk,bqhd->bkhd",
        attention.astype(jnp.bfloat16),
        grad_att,
        preferred_element_type=jnp.float32,
    )
    grad_weights = jnp.einsum(
        "bqhd,bkhd->bhqk", grad_att, values, preferred_element_type=jnp.float32
    )
    inner = jnp.sum(attention * grad_weights, axis=-1, keepdims=True)
    grad_scores = (attention * (grad_weights - inner)).astype(jnp.bfloat16)
    grad_query = (
        jnp.einsum("bhqk,bkhd->bqhd", grad_scores, keys, preferred_element_type=jnp.float32)
        * scaling
    )
    grad_keys = (
        jnp.einsum("bhqk,bqhd->bkhd", grad_scores, query, preferred_element_type=jnp.float32)
        * scaling
    )
    grad_projected = (
        jnp.stack([grad_query, grad_keys, grad_values], axis=2)
        .reshape(-1, 3 * D)
        .astype(jnp.bfloat16)
    )
    grad_qkv = product(mixed_a.reshape(-1, D).T, grad_projected)
    bias_sums = jnp.sum(grad_projected.astype(jnp.float32), axis=0)
    grad_mixed_a = product(grad_projected, weights[0].T).reshape(number, seq_tokens, D)
    shift_a = jnp.sum(grad_mixed_a, axis=1)
    scale_a = jnp.sum(grad_mixed_a * normed_a, axis=1)
    grad_in = grad_mid + norm_back(grad_mixed_a * (1.0 + spans[1]), normed_a, inverse_a)
    grad_spans = jnp.concatenate([shift_a, scale_a, gate_a, shift_b, scale_b, gate_b], axis=-1)
    grad_bias = jnp.concatenate([bias_sums[:D], bias_sums[2 * D :], bias_proj, bias_fc1, bias_fc2])
    return (grad_in, (grad_qkv, grad_proj, grad_fc1, grad_fc2), grad_bias, grad_spans)


def local(
    latents,
    noise_field,
    timesteps,
    labels,
    drop_mask,
    roster,
    w_qkv,
    w_proj,
    w_fc1,
    w_fc2,
    w_mod,
    row_qkv,
    col_qkv,
    row_proj,
    col_proj,
    row_fc1,
    col_fc1,
    row_fc2,
    col_fc2,
    row_mod,
    col_mod,
    small,
    small_second,
):
    pieces = unpack(small)
    count_all = (
        latents.shape[0]
        * latents.shape[1]
        * lax.axis_size("dp")
        * lax.axis_size("rep")
        * GRID
        * GRID
        * PDIM
    )
    places = position_table()
    shard_low = (
        w_qkv.astype(jnp.bfloat16),
        w_proj.astype(jnp.bfloat16),
        w_fc1.astype(jnp.bfloat16),
        w_fc2.astype(jnp.bfloat16),
    )
    mod_shard = w_mod.astype(jnp.bfloat16)
    patch_low = pieces["patch_w"].astype(jnp.bfloat16)
    time1_low = pieces["time1_w"].astype(jnp.bfloat16)
    time2_low = pieces["time2_w"].astype(jnp.bfloat16)
    head_low = pieces["head_w"].astype(jnp.bfloat16)
    block_acc = [None] * LAYERS
    mod_acc = None
    small_acc = jnp.zeros_like(small)
    loss_acc = jnp.zeros((), jnp.float32)
    for micro in range(MICRO):
        mod_full = lax.all_gather(mod_shard, "dp", axis=0, tiled=True)
        picker = (timesteps[micro][:, None] == jnp.arange(STEPS_T)[None, :]).astype(jnp.float32)
        factors = jnp.dot(picker, roster.T, precision=HIGHEST)
        noised = factors[:, 0:1] * latents[micro] + factors[:, 1:2] * noise_field[micro]
        tokens = patchify(noised).astype(jnp.bfloat16)
        target = patchify(noise_field[micro]).reshape(-1, PDIM)
        number = tokens.shape[0]
        residual = (product(tokens.reshape(-1, PDIM), patch_low) + pieces["patch_b"]).reshape(
            number, GRID * GRID, D
        ) + places
        features = time_features(timesteps[micro]).astype(jnp.bfloat16)
        hidden_t = product(features, time1_low) + pieces["time1_b"]
        silu_t = jax.nn.silu(hidden_t).astype(jnp.bfloat16)
        chosen = jnp.where(drop_mask[micro] == 1, CLASSES, labels[micro])
        onehot = (chosen[:, None] == jnp.arange(CLASSES + 1)[None, :]).astype(jnp.float32)
        condition = (
            product(silu_t, time2_low)
            + pieces["time2_b"]
            + jnp.dot(onehot, pieces["class_tab"], precision=HIGHEST)
        )
        silu_c = jax.nn.silu(condition).astype(jnp.bfloat16)
        modulation = product(silu_c, mod_full) + pieces["mod_b"]
        kept_all = []
        gathered_all = []
        spans_all = []
        for layer_index in range(LAYERS):
            weights = (
                lax.all_gather(shard_low[0][layer_index], "dp", axis=0, tiled=True),
                lax.all_gather(shard_low[1][layer_index], "dp", axis=0, tiled=True),
                lax.all_gather(shard_low[2][layer_index], "dp", axis=0, tiled=True),
                lax.all_gather(shard_low[3][layer_index], "dp", axis=0, tiled=True),
            )
            spans = [
                modulation[:, None, D * (6 * layer_index + i) : D * (6 * layer_index + i + 1)]
                for i in range(6)
            ]
            residual, kept = layer_forward(residual, spans, weights, pieces["block_b"][layer_index])
            kept_all.append(kept)
            gathered_all.append(weights)
            spans_all.append(spans)
        final_shift = modulation[:, None, 6 * D * LAYERS : 6 * D * LAYERS + D]
        final_scale = modulation[:, None, 6 * D * LAYERS + D :]
        normed_f, inverse_f = norm_rows(residual)
        final_in = (
            (normed_f * (1.0 + final_scale) + final_shift).astype(jnp.bfloat16).reshape(-1, D)
        )
        output = product(final_in, head_low) + pieces["head_b"]
        error = output - target
        loss_acc = loss_acc + jnp.sum(error * error)
        grad_output = (error * (2.0 / count_all)).astype(jnp.bfloat16)
        grad_head = product(final_in.T, grad_output)
        grad_head_b = jnp.sum(grad_output.astype(jnp.float32), axis=0)
        grad_final = product(grad_output, head_low.T).reshape(number, GRID * GRID, D)
        final_grads = [jnp.sum(grad_final, axis=1), jnp.sum(grad_final * normed_f, axis=1)]
        grad_res = norm_back(grad_final * (1.0 + final_scale), normed_f, inverse_f)
        layer_spans = [None] * LAYERS
        bias_grads = [None] * LAYERS
        for layer_index in reversed(range(LAYERS)):
            weights = (
                lax.all_gather(shard_low[0][layer_index], "dp", axis=0, tiled=True),
                lax.all_gather(shard_low[1][layer_index], "dp", axis=0, tiled=True),
                lax.all_gather(shard_low[2][layer_index], "dp", axis=0, tiled=True),
                lax.all_gather(shard_low[3][layer_index], "dp", axis=0, tiled=True),
            )
            grad_res, grads, grad_bias, grad_spans = layer_backward(
                grad_res, spans_all[layer_index], weights, kept_all[layer_index]
            )
            layer_spans[layer_index] = grad_spans
            bias_grads[layer_index] = grad_bias
            shards = (
                lax.psum_scatter(grads[0], "dp", scatter_dimension=0, tiled=True),
                lax.psum_scatter(grads[1], "dp", scatter_dimension=0, tiled=True),
                lax.psum_scatter(grads[2], "dp", scatter_dimension=0, tiled=True),
                lax.psum_scatter(grads[3], "dp", scatter_dimension=0, tiled=True),
            )
            if micro == 0:
                block_acc[layer_index] = shards
            else:
                block_acc[layer_index] = tuple(
                    (a + b for a, b in zip(block_acc[layer_index], shards))
                )
        grad_mod = jnp.concatenate(layer_spans + final_grads, axis=-1).astype(jnp.bfloat16)
        grad_wmod = product(silu_c.T, grad_mod)
        grad_mod_b = jnp.sum(grad_mod.astype(jnp.float32), axis=0)
        mod_back = lax.all_gather(mod_shard, "dp", axis=0, tiled=True)
        _, silu_pull = jax.vjp(jax.nn.silu, condition)
        grad_cond = silu_pull(product(grad_mod, mod_back.T))[0].astype(jnp.bfloat16)
        grad_class = jnp.dot(onehot.T, grad_cond.astype(jnp.float32), precision=HIGHEST)
        grad_time2 = product(silu_t.T, grad_cond)
        grad_time2_b = jnp.sum(grad_cond.astype(jnp.float32), axis=0)
        _, silu_time_pull = jax.vjp(jax.nn.silu, hidden_t)
        grad_hidden_t = silu_time_pull(product(grad_cond, time2_low.T))[0].astype(jnp.bfloat16)
        grad_time1 = product(features.T, grad_hidden_t)
        grad_time1_b = jnp.sum(grad_hidden_t.astype(jnp.float32), axis=0)
        grad_start = grad_res.reshape(-1, D).astype(jnp.bfloat16)
        grad_patch = product(tokens.reshape(-1, PDIM).T, grad_start)
        grad_patch_b = jnp.sum(grad_start.astype(jnp.float32), axis=0)
        mod_part = lax.psum_scatter(grad_wmod, "dp", scatter_dimension=0, tiled=True)
        mod_acc = mod_part if micro == 0 else mod_acc + mod_part
        small_acc = small_acc + jnp.concatenate(
            [
                grad_patch.reshape(-1),
                grad_patch_b,
                grad_time1.reshape(-1),
                grad_time1_b,
                grad_time2.reshape(-1),
                grad_time2_b,
                grad_class.reshape(-1),
                grad_mod_b,
                grad_head.reshape(-1),
                grad_head_b,
                jnp.stack(bias_grads).reshape(-1),
            ]
        )
    grad_qkv = jnp.stack([block_acc[i][0] for i in range(LAYERS)])
    grad_proj = jnp.stack([block_acc[i][1] for i in range(LAYERS)])
    grad_fc1 = jnp.stack([block_acc[i][2] for i in range(LAYERS)])
    grad_fc2 = jnp.stack([block_acc[i][3] for i in range(LAYERS)])
    grad_qkv, grad_proj, grad_fc1, grad_fc2, grad_wmod = lax.psum(
        (grad_qkv, grad_proj, grad_fc1, grad_fc2, mod_acc), "rep"
    )
    small_grad, loss_total = lax.psum((small_acc, loss_acc), ("dp", "rep"))
    beta = 1.0 - STEP ** (-0.8)
    rows_dp = lax.axis_size("dp")
    kinds = [
        (w_qkv, grad_qkv, row_qkv, col_qkv),
        (w_proj, grad_proj, row_proj, col_proj),
        (w_fc1, grad_fc1, row_fc1, col_fc1),
        (w_fc2, grad_fc2, row_fc2, col_fc2),
        (w_mod[None], grad_wmod[None], row_mod[None], col_mod[None]),
    ]
    firsts = []
    for weight, grad, row, col in kinds:
        square = grad * grad + EPS_ONE
        row_new = beta * row + (1.0 - beta) * jnp.mean(square, axis=-1)
        firsts.append(
            (
                row_new,
                jnp.sum(square, axis=-2),
                jnp.sum(row_new, axis=-1),
                jnp.sum(weight * weight, axis=(-2, -1)),
            )
        )
    col_flat = jnp.concatenate([entry[1].reshape(-1) for entry in firsts])
    row_flat = jnp.concatenate([entry[2] for entry in firsts])
    weight_flat = jnp.concatenate([entry[3] for entry in firsts])
    col_flat, row_flat, weight_flat = lax.psum((col_flat, row_flat, weight_flat), "dp")
    seconds = []
    col_offset = 0
    lay_offset = 0
    for kind, first in zip(kinds, firsts):
        weight, grad, row, col = kind
        stacked, col_count = (weight.shape[0], weight.shape[2])
        rows_all = weight.shape[1] * rows_dp
        col_sum = col_flat[col_offset : col_offset + stacked * col_count].reshape(
            stacked, col_count
        )
        row_mean = row_flat[lay_offset : lay_offset + stacked] / rows_all
        weight_rms = jnp.sqrt(
            weight_flat[lay_offset : lay_offset + stacked] / (rows_all * col_count)
        )
        col_offset += stacked * col_count
        lay_offset += stacked
        col_new = beta * col + (1.0 - beta) * col_sum / rows_all
        estimate = first[0][:, :, None] * col_new[:, None, :] / row_mean[:, None, None]
        update = grad * lax.rsqrt(estimate)
        seconds.append((update, col_new, weight_rms, rows_all * col_count))
    update_sq = lax.psum(
        jnp.concatenate([jnp.sum(entry[0] * entry[0], axis=(-2, -1)) for entry in seconds]), "dp"
    )
    results = []
    lay_offset = 0
    for kind, first, second in zip(kinds, firsts, seconds):
        weight, grad = (kind[0], kind[1])
        update, col_new, weight_rms, entries = second
        stacked = weight.shape[0]
        update_rms = jnp.sqrt(update_sq[lay_offset : lay_offset + stacked] / entries)
        lay_offset += stacked
        update = update / jnp.maximum(1.0, update_rms / CLIP)[:, None, None]
        new_weight = weight - (RATE * jnp.maximum(0.001, weight_rms))[:, None, None] * update
        results.append((new_weight, grad, first[0], col_new, new_weight.astype(jnp.bfloat16)))
    square = small_grad * small_grad + EPS_ONE
    small_second_new = beta * small_second + (1.0 - beta) * square
    update = small_grad * lax.rsqrt(small_second_new)
    update = update / jnp.maximum(1.0, jnp.sqrt(jnp.mean(update * update)) / CLIP)
    small_new = small - RATE * jnp.maximum(0.001, jnp.sqrt(jnp.mean(small * small))) * update
    mod_result = results[4]
    return (
        loss_total,
        results[0][0],
        results[0][1],
        results[0][2],
        results[0][3],
        results[0][4],
        results[1][0],
        results[1][1],
        results[1][2],
        results[1][3],
        results[1][4],
        results[2][0],
        results[2][1],
        results[2][2],
        results[2][3],
        results[2][4],
        results[3][0],
        results[3][1],
        results[3][2],
        results[3][3],
        results[3][4],
        mod_result[0][0],
        mod_result[1][0],
        mod_result[2][0],
        mod_result[3][0],
        mod_result[4][0],
        small_grad,
        small_second_new,
        small_new,
        small_new.astype(jnp.bfloat16),
    )


def solution(mesh):
    in_specs = (
        P(None, ("dp", "rep"), None),
        P(None, ("dp", "rep"), None),
        P(None, ("dp", "rep")),
        P(None, ("dp", "rep")),
        P(None, ("dp", "rep")),
        P(),
        P(None, "dp", None),
        P(None, "dp", None),
        P(None, "dp", None),
        P(None, "dp", None),
        P("dp", None),
        P(None, "dp"),
        P(),
        P(None, "dp"),
        P(),
        P(None, "dp"),
        P(),
        P(None, "dp"),
        P(),
        P("dp"),
        P(),
        P(),
        P(),
    )
    out_specs = (
        P(),
        P(None, "dp", None),
        P(None, "dp", None),
        P(None, "dp"),
        P(),
        P(None, "dp", None),
        P(None, "dp", None),
        P(None, "dp", None),
        P(None, "dp"),
        P(),
        P(None, "dp", None),
        P(None, "dp", None),
        P(None, "dp", None),
        P(None, "dp"),
        P(),
        P(None, "dp", None),
        P(None, "dp", None),
        P(None, "dp", None),
        P(None, "dp"),
        P(),
        P(None, "dp", None),
        P("dp", None),
        P("dp", None),
        P("dp"),
        P(),
        P("dp", None),
        P(),
        P(),
        P(),
        P(),
    )
    return jax.shard_map(local, mesh=mesh, in_specs=in_specs, out_specs=out_specs, check_vma=False)
```

profile of v0, /device:TPU:0, one launch (start us, length us, event | category | flops | bytes accessed | tf_op | source)
XLA Modules:
  0.0 3043.5 jit_solution(11602530351059204021)
XLA Ops:
  7.3 6.4 multiply_reduce_fusion.1
  13.8 3.0 multiply_reduce_fusion.17
  38.9 2.8 slice_reduce_fusion
  56.7 3.1 convert_element_type.569
  79.0 161.9 %all-gather.18.cloned.1.call-done = bf16[768,10752]{1,0:T(8,128)(2,1)} async-done(((bf16[96,10752]{1,0:T(8,128)(2,1)}), bf16[768,10752]{1,0:T(8,128)(2,1)}) %all-gather.18.cloned.1.call-update) | async-done | bytes 16515088 | tf_op jit(solution)/shard_map/all_gather | solution.py:281
  240.9 7.9 convolution_reduce_fusion
  250.5 56.6 %all-gather.20.cloned.1.call-done = bf16[1,768,2304]{2,1,0:T(8,128)(2,1)} async-done(((bf16[1,96,2304]{2,1,0:T(8,128)(2,1)}), bf16[1,768,2304]{2,1,0:T(8,128)(2,1)}) %all-gather.20.cloned.1.call-update) | async-done | bytes 3538960 | tf_op jit(solution)/shard_map/all_gather | solution.py:308
  307.1 3.2 fusion.46
  316.5 32.9 %all-gather.22.cloned.1.call-done = bf16[1,768,768]{2,1,0:T(8,128)(2,1)} async-done(((bf16[1,96,768]{2,1,0:T(8,128)(2,1)}), bf16[1,768,768]{2,1,0:T(8,128)(2,1)}) %all-gather.22.cloned.1.call-update) | async-done | bytes 1179664 | tf_op jit(solution)/shard_map/all_gather | solution.py:309
  349.4 2.9 fusion.243
  354.0 76.7 %all-gather.24.cloned.1.call-done = bf16[1,768,3072]{2,1,0:T(8,128)(2,1)} async-done(((bf16[1,96,3072]{2,1,0:T(8,128)(2,1)}), bf16[1,768,3072]{2,1,0:T(8,128)(2,1)}) %all-gather.24.cloned.1.call-update) | async-done | bytes 4718608 | tf_op jit(solution)/shard_map/all_gather | solution.py:310
  430.7 5.7 fusion.35
  436.4 74.9 %all-gather.26.cloned.1.call-done = bf16[1,3072,768]{2,1,0:T(8,128)(2,1)} async-done(((bf16[1,384,768]{2,1,0:T(8,128)(2,1)}), bf16[1,3072,768]{2,1,0:T(8,128)(2,1)}) %all-gather.26.cloned.1.call-update) | async-done | bytes 4718608 | tf_op jit(solution)/shard_map/all_gather | solution.py:311
  511.4 6.3 fusion.242
  518.8 58.5 %all-gather.28.cloned.1.call-done = bf16[1,768,2304]{2,1,0:T(8,128)(2,1)} async-done(((bf16[1,96,2304]{2,1,0:T(8,128)(2,1)}), bf16[1,768,2304]{2,1,0:T(8,128)(2,1)}) %all-gather.28.cloned.1.call-update) | async-done | bytes 3538960 | tf_op jit(solution)/shard_map/all_gather | solution.py:308
  577.3 4.4 fusion.47
  590.0 29.6 all-gather.30.cloned.1.call-done
  619.6 2.9 fusion.241
  624.2 76.8 %all-gather.32.cloned.1.call-done = bf16[1,768,3072]{2,1,0:T(8,128)(2,1)} async-done(((bf16[1,96,3072]{2,1,0:T(8,128)(2,1)}), bf16[1,768,3072]{2,1,0:T(8,128)(2,1)}) %all-gather.32.cloned.1.call-update) | async-done | bytes 4718608 | tf_op jit(solution)/shard_map/all_gather | solution.py:310
  701.1 5.7 fusion.41
  706.8 75.1 %all-gather.34.cloned.1.call-done = bf16[1,3072,768]{2,1,0:T(8,128)(2,1)} async-done(((bf16[1,384,768]{2,1,0:T(8,128)(2,1)}), bf16[1,3072,768]{2,1,0:T(8,128)(2,1)}) %all-gather.34.cloned.1.call-update) | async-done | bytes 4718608 | tf_op jit(solution)/shard_map/all_gather | solution.py:311
  781.9 5.6 fusion.240
  791.8 3.7 convert_reduce_fusion
  815.1 3.7 convert_reduce_fusion.1
  838.9 10.1 convolution_reduce_fusion.7
  852.6 8.1 convolution_reduce_fusion.1
  872.8 2.9 fusion.246
  883.8 3.1 convolution_convert_fusion.6
  895.9 3.7 convert_reduce_fusion.2
  908.8 5.3 multiply_reduce_fusion.7
  916.5 3.6 multiply_convert_fusion.3
  927.8 5.8 convert_reduce_fusion.3
  940.8 2.9 fusion.215
  943.8 4.2 convolution_add_fusion
  961.2 4.3 convolution_add_fusion.1
  969.7 5.8 convolution_add_fusion.2
  979.7 5.8 convolution_add_fusion.3
  988.9 5.2 convolution_add_fusion.4
  997.4 5.2 convolution_add_fusion.5
  1004.2 4.9 multiply_reduce_fusion.19
  1018.1 11.4 multiply_add_fusion
  1031.0 10.2 convolution_reduce_fusion.9
  1055.3 30.4 concatenate.120
  1085.8 38.0 %concatenate.123 = f32[861712]{0:T(1024)} concatenate(f32[12288]{0:T(1024)} %reshape.2459, f32[768]{0:T(1024)} %get-tuple-element.149, f32[196608]{0:T(1024)} %reshape.2460, f32[768]{0:T(1024)S(1)} %copy-done.175, f32[589824]{0:T(1024)} %reshape.2461, bf16[768]{0:T(1024)(128)(2,1)} %copy-done.229, f32[25344]{0:T(1024)} %reshape.2462, bf16[10752]{0:T(1024)(128)(2,1)S(1)} %copy-done.139, ...), dimensions={0} | concatenate | bytes 6870656 | tf_op jit(solution)/shard_map/concatenate | solution.py:380
  1123.8 4.5 add.1019
  1130.3 57.1 %reduce-scatter.12.cloned.1.call-done = f32[96,2304]{1,0:T(8,128)} async-done(((f32[768,2304]{1,0:T(8,128)}), f32[96,2304]{1,0:T(8,128)}) %reduce-scatter.12.cloned.1.call-update) | async-done | bytes 884752 | tf_op jit(solution)/shard_map/reduce_scatter | solution.py:351
  1187.4 132.2 %reduce-scatter.10.cloned.1.call-done = f32[96,2304]{1,0:T(8,128)} async-done(((f32[768,2304]{1,0:T(8,128)}), f32[96,2304]{1,0:T(8,128)}) %reduce-scatter.10.cloned.1.call-update) | async-done | bytes 884752 | tf_op jit(solution)/shard_map/reduce_scatter | solution.py:351
  1322.3 163.3 %reduce-scatter.24.cloned.1.call-done = f32[384,768]{1,0:T(8,128)} async-done(((f32[3072,768]{1,0:T(8,128)}), f32[384,768]{1,0:T(8,128)}) %reduce-scatter.24.cloned.1.call-update) | async-done | bytes 1179664 | tf_op jit(solution)/shard_map/reduce_scatter | solution.py:354
  1485.6 166.0 %reduce-scatter.22.cloned.1.call-done = f32[384,768]{1,0:T(8,128)} async-done(((f32[3072,768]{1,0:T(8,128)}), f32[384,768]{1,0:T(8,128)}) %reduce-scatter.22.cloned.1.call-update) | async-done | bytes 1179664 | tf_op jit(solution)/shard_map/reduce_scatter | solution.py:354
  1651.6 3.2 pad_maximum_fusion.1
  1654.8 162.9 %reduce-scatter.20.cloned.1.call-done = f32[96,3072]{1,0:T(8,128)} async-done(((f32[768,3072]{1,0:T(8,128)}), f32[96,3072]{1,0:T(8,128)}) %reduce-scatter.20.cloned.1.call-update) | async-done | bytes 1179664 | tf_op jit(solution)/shard_map/reduce_scatter | solution.py:353
  1817.7 166.0 %reduce-scatter.18.cloned.1.call-done = f32[96,3072]{1,0:T(8,128)} async-done(((f32[768,3072]{1,0:T(8,128)}), f32[96,3072]{1,0:T(8,128)}) %reduce-scatter.18.cloned.1.call-update) | async-done | bytes 1179664 | tf_op jit(solution)/shard_map/reduce_scatter | solution.py:353
  1983.7 3.3 pad_maximum_fusion
  1987.0 533.3 %reduce-scatter.26.cloned.1.call-done = f32[96,10752]{1,0:T(8,128)} async-done(((f32[768,10752]{1,0:T(8,128)}), f32[96,10752]{1,0:T(8,128)}) %reduce-scatter.26.cloned.1.call-update) | async-done | bytes 4128784 | tf_op jit(solution)/shard_map/reduce_scatter | solution.py:378
  2524.5 39.5 %psum.77 = f32[]{:T(128)} all-reduce(f32[]{:T(128)S(6)} %add.981), channel_id=1, replica_groups=mesh['dp'=8,'rep'=4] {'dp','rep'}, use_global_device_ids=true, to_apply=%region_30.31 | all-reduce | flops 1 | bytes 8 | tf_op jit(solution)/shard_map/psum | solution.py:402
  2563.9 100.4 %all-reduce.8.cloned.1.call-done = f32[861712]{0:T(1024)} async-done(((f32[861712]{0:T(1024)}), f32[861712]{0:T(1024)}) %all-reduce.8.cloned.1.call-update) | async-done | bytes 3446864 | tf_op jit(solution)/shard_map/psum | solution.py:402
  2664.4 5.4 multiply_reduce_fusion.2
  2670.5 197.9 %all-reduce.10.cloned.1.call-done = (f32[2,96,2304]{2,1,0:T(8,128)}, f32[2,96,768]{2,1,0:T(8,128)}, f32[2,96,3072]{2,1,0:T(8,128)}, f32[2,384,768]{2,1,0:T(8,128)}, f32[96,10752]{1,0:T(8,128)}) async-done(((f32[2,96,2304]{2,1,0:T(8,128)}, f32[2,96,768]{2,1,0:T(8,128)}, f32[2,96,3072]{2,1,0:T(8,128)}, f32[2,384,768]{2,1,0:T(8,128)}, f32[96,10752]{1,0:T(8,128)}), (f32[2,96,2304]{2,1,0:T(8,128)}, ...) | async-done | bytes 11206672 | tf_op jit(solution)/shard_map/psum | solution.py:399
  2877.3 21.6 psum.85
  2900.9 64.7 %all-reduce.6.cloned.1.call-done = f32[24576]{0:T(1024)} async-done(((f32[24576]{0:T(1024)}), f32[24576]{0:T(1024)}) %all-reduce.6.cloned.1.call-update) | async-done | bytes 98320 | tf_op jit(solution)/shard_map/psum | solution.py:427
  2976.7 7.1 fusion.219
  2983.7 20.1 all-reduce
  3009.6 4.2 fusion.232
  3022.4 3.8 fusion.228
  (1163 shorter events, 277.5 us)
Async XLA Ops:
  7.2 28.9 copy-start
  7.2 233.7 %all-gather.18.cloned.1.call-start = ((), (), s32[]{:S(2)}) async-start(), calls=%async_computation.9 | async-start | bytes 18579456 | tf_op jit(solution)/shard_map/all_gather | solution.py:281
  13.7 293.4 %all-gather.20.cloned.1.call-start = ((), (), s32[]{:S(2)}) async-start(), calls=%async_computation.12 | async-start | bytes 3981312 | tf_op jit(solution)/shard_map/all_gather | solution.py:308
  17.7 331.7 %all-gather.22.cloned.1.call-start = ((), (), s32[]{:S(2)}) async-start(), calls=%async_computation.13 | async-start | bytes 1327104 | tf_op jit(solution)/shard_map/all_gather | solution.py:309
  19.3 411.4 %all-gather.24.cloned.1.call-start = ((), (), s32[]{:S(2)}) async-start(), calls=%async_computation.14 | async-start | bytes 5308416 | tf_op jit(solution)/shard_map/all_gather | solution.py:310
  21.5 489.8 %all-gather.26.cloned.1.call-start = ((), (), s32[]{:S(2)}) async-start(), calls=%async_computation.15 | async-start | bytes 5308416 | tf_op jit(solution)/shard_map/all_gather | solution.py:311
  24.6 552.7 %all-gather.28.cloned.1.call-start = ((), (), s32[]{:S(2)}) async-start(), calls=%async_computation.16 | async-start | bytes 3981312 | tf_op jit(solution)/shard_map/all_gather | solution.py:308
  25.2 594.4 %all-gather.30.cloned.1.call-start = ((), (), s32[]{:S(2)}) async-start(), calls=%async_computation.17 | async-start | bytes 1327104 | tf_op jit(solution)/shard_map/all_gather | solution.py:309
  25.9 675.1 %all-gather.32.cloned.1.call-start = ((), (), s32[]{:S(2)}) async-start(), calls=%async_computation.18 | async-start | bytes 5308416 | tf_op jit(solution)/shard_map/all_gather | solution.py:310
  26.7 755.2 %all-gather.34.cloned.1.call-start = ((), (), s32[]{:S(2)}) async-start(), calls=%async_computation.19 | async-start | bytes 5308416 | tf_op jit(solution)/shard_map/all_gather | solution.py:311
  27.4 1100.9 %reduce-scatter.16.cloned.1.call-start = ((), (), s32[]{:S(2)}) async-start(), calls=%async_computation.23 | async-start | bytes 2654208 | tf_op jit(solution)/shard_map/reduce_scatter | solution.py:352
  73.4 175.5 %copy-start.29 = (f32[256,768]{1,0:T(8,128)}, f32[256,768]{1,0:T(8,128)S(1)}, u32[]{:S(2)}) copy-start(f32[256,768]{1,0:T(8,128)S(1)} %get-tuple-element.319) | copy-start | bytes 2359300
  73.8 233.3 %copy-start.37 = (f32[256,768]{1,0:T(8,128)}, f32[256,768]{1,0:T(8,128)S(1)}, u32[]{:S(2)}) copy-start(f32[256,768]{1,0:T(8,128)S(1)} %get-tuple-element.300) | copy-start | bytes 2359300
  73.8 233.3 %copy-start.251 = (f32[256]{0:T(256)}, f32[256]{0:T(256)S(1)}, u32[]{:S(2)}) copy-start(f32[256]{0:T(256)S(1)} %broadcast_multiply_fusion.30) | copy-start | bytes 3076
  74.1 233.0 %copy-start.291 = (f32[256]{0:T(256)}, f32[256]{0:T(256)S(1)}, u32[]{:S(2)}) copy-start(f32[256]{0:T(256)S(1)} %add_rsqrt_fusion.4) | copy-start | bytes 3076
  77.6 171.3 %copy-start.211 = (f32[256]{0:T(256)}, f32[256]{0:T(256)S(1)}, u32[]{:S(2)}) copy-start(f32[256]{0:T(256)S(1)} %broadcast_multiply_fusion.35) | copy-start | bytes 3076
  79.0 228.1 %copy-start.284 = (f32[2304]{0:T(1024)}, f32[2304]{0:T(1024)S(1)}, u32[]{:S(2)}) copy-start(f32[2304]{0:T(1024)S(1)} %get-tuple-element.270) | copy-start | bytes 27652
  250.4 59.8 %copy-start.199 = (f32[768]{0:T(1024)}, f32[768]{0:T(1024)S(1)}, u32[]{:S(2)}) copy-start(f32[768]{0:T(1024)S(1)} %get-tuple-element.92) | copy-start | bytes 9220
  250.4 59.8 %copy-start.257 = (f32[768]{0:T(1024)}, f32[768]{0:T(1024)S(1)}, u32[]{:S(2)}) copy-start(f32[768]{0:T(1024)S(1)} %get-tuple-element.91) | copy-start | bytes 9220
  250.5 180.2 %copy-start.149 = (f32[768]{0:T(1024)}, f32[768]{0:T(1024)S(1)}, u32[]{:S(2)}) copy-start(f32[768]{0:T(1024)S(1)} %get-tuple-element.88) | copy-start | bytes 9220
  250.5 450.6 %copy-start.151 = (f32[768]{0:T(1024)}, f32[768]{0:T(1024)S(1)}, u32[]{:S(2)}) copy-start(f32[768]{0:T(1024)S(1)} %get-tuple-element.82) | copy-start | bytes 9220
  250.5 547.2 %copy-start.147 = (f32[768]{0:T(1024)}, f32[768]{0:T(1024)S(1)}, u32[]{:S(2)}) copy-start(f32[768]{0:T(1024)S(1)} %get-tuple-element.83) | copy-start | bytes 9220
  250.5 570.6 %copy-start.145 = (f32[768]{0:T(1024)}, f32[768]{0:T(1024)S(1)}, u32[]{:S(2)}) copy-start(f32[768]{0:T(1024)S(1)} %get-tuple-element.89) | copy-start | bytes 9220
  316.5 119.9 %copy-start.83 = (bf16[12,64,256]{2,1,0:T(8,128)(2,1)}, bf16[12,64,256]{2,1,0:T(8,128)(2,1)S(1)}, u32[]{:S(2)}) copy-start(bf16[12,64,256]{2,1,0:T(8,128)(2,1)S(1)} %convolution_convert_fusion.5) | copy-start | bytes 1179652
  511.3 66.0 %copy-start.202 = (f32[768]{0:T(1024)S(1)}, f32[768]{0:T(1024)}, u32[]{:S(2)}) copy-start(f32[768]{0:T(1024)} %get-tuple-element.86) | copy-start | bytes 9220
  511.3 66.0 %copy-start.259 = (f32[768]{0:T(1024)S(1)}, f32[768]{0:T(1024)}, u32[]{:S(2)}) copy-start(f32[768]{0:T(1024)} %get-tuple-element.85) | copy-start | bytes 9220
  511.3 66.0 %copy-start.282 = (f32[2304]{0:T(1024)S(1)}, f32[2304]{0:T(1024)}, u32[]{:S(2)}) copy-start(f32[2304]{0:T(1024)} %get-tuple-element.269) | copy-start | bytes 27652
  517.7 64.1 %copy-start.254 = (f32[256]{0:T(256)}, f32[256]{0:T(256)S(1)}, u32[]{:S(2)}) copy-start(f32[256]{0:T(256)S(1)} %broadcast_multiply_fusion.28) | copy-start | bytes 3076
  518.8 63.0 %copy-start.294 = (f32[256]{0:T(256)}, f32[256]{0:T(256)S(1)}, u32[]{:S(2)}) copy-start(f32[256]{0:T(256)S(1)} %add_rsqrt_fusion.2) | copy-start | bytes 3076
  586.1 33.6 %copy-start.191 = (f32[768]{0:T(1024)S(1)}, f32[768]{0:T(1024)}, u32[]{:S(2)}) copy-start(f32[768]{0:T(1024)} %get-tuple-element.223) | copy-start | bytes 9220
  590.0 116.8 %copy-start.85 = (bf16[12,64,256]{2,1,0:T(8,128)(2,1)}, bf16[12,64,256]{2,1,0:T(8,128)(2,1)S(1)}, u32[]{:S(2)}) copy-start(bf16[12,64,256]{2,1,0:T(8,128)(2,1)S(1)} %convolution_convert_fusion.4) | copy-start | bytes 1179652
  622.6 175.1 %copy-start.226 = (f32[256]{0:T(256)}, f32[256]{0:T(256)S(1)}, u32[]{:S(2)}) copy-start(f32[256]{0:T(256)S(1)} %broadcast_multiply_fusion.27) | copy-start | bytes 3076
  888.4 13.4 copy-start.46
  888.4 13.4 copy-start.218
  916.0 212.4 %reduce-scatter.14.cloned.1.call-start = ((), (), s32[]{:S(2)}) async-start(), calls=%async_computation.22 | async-start | bytes 2654208 | tf_op jit(solution)/shard_map/reduce_scatter | solution.py:352
  940.5 246.9 %reduce-scatter.12.cloned.1.call-start = ((), (), s32[]{:S(2)}) async-start(), calls=%async_computation.21 | async-start | bytes 7962624 | tf_op jit(solution)/shard_map/reduce_scatter | solution.py:351
  948.0 371.6 %reduce-scatter.10.cloned.1.call-start = ((), (), s32[]{:S(2)}) async-start(), calls=%async_computation.20 | async-start | bytes 7962624 | tf_op jit(solution)/shard_map/reduce_scatter | solution.py:351
  965.5 520.1 %reduce-scatter.24.cloned.1.call-start = ((), (), s32[]{:S(2)}) async-start(), calls=%async_computation.27 | async-start | bytes 10616832 | tf_op jit(solution)/shard_map/reduce_scatter | solution.py:354
  975.5 676.1 %reduce-scatter.22.cloned.1.call-start = ((), (), s32[]{:S(2)}) async-start(), calls=%async_computation.26 | async-start | bytes 10616832 | tf_op jit(solution)/shard_map/reduce_scatter | solution.py:354
  985.6 832.1 %reduce-scatter.20.cloned.1.call-start = ((), (), s32[]{:S(2)}) async-start(), calls=%async_computation.25 | async-start | bytes 10616832 | tf_op jit(solution)/shard_map/reduce_scatter | solution.py:353
  994.2 989.5 %reduce-scatter.18.cloned.1.call-start = ((), (), s32[]{:S(2)}) async-start(), calls=%async_computation.24 | async-start | bytes 10616832 | tf_op jit(solution)/shard_map/reduce_scatter | solution.py:353
  1002.7 1517.5 %reduce-scatter.26.cloned.1.call-start = ((), (), s32[]{:S(2)}) async-start(), calls=%async_computation.28 | async-start | bytes 37158912 | tf_op jit(solution)/shard_map/reduce_scatter | solution.py:378
  1029.5 1634.8 %all-reduce.8.cloned.1.call-start = ((), (), s32[]{:S(2)}) async-start(), calls=%async_computation.11 | async-start | bytes 6897664 | tf_op jit(solution)/shard_map/psum | solution.py:402
  1055.3 30.4 copy-start.139
  1128.3 1740.0 %all-reduce.10.cloned.1.call-start = ((), (), s32[]{:S(2)}) async-start(), calls=%async_computation.29 | async-start | bytes 22413312 | tf_op jit(solution)/shard_map/psum | solution.py:399
  2520.2 144.1 %copy-start.91 = (f32[861712]{0:T(1024)S(1)}, f32[861712]{0:T(1024)}, u32[]{:S(2)}) copy-start(f32[861712]{0:T(1024)} %param.45) | copy-start | bytes 10340548
  2520.3 445.4 %all-reduce.6.cloned.1.call-start = ((), (), s32[]{:S(2)}) async-start(), calls=%async_computation.10 | async-start | bytes 196608 | tf_op jit(solution)/shard_map/psum | solution.py:427
  2874.2 93.7 %copy-start.231 = (f32[2,2304]{1,0:T(2,128)S(1)}, f32[2,2304]{1,0:T(2,128)}, u32[]{:S(2)}) copy-start(f32[2,2304]{1,0:T(2,128)} %param.35) | copy-start | bytes 55300
  2874.2 93.7 %copy-start.301 = (f32[2,768]{1,0:T(2,128)S(1)}, f32[2,768]{1,0:T(2,128)}, u32[]{:S(2)}) copy-start(f32[2,768]{1,0:T(2,128)} %param.37) | copy-start | bytes 18436
  2874.3 93.7 %copy-start.228 = (f32[2,3072]{1,0:T(2,128)S(1)}, f32[2,3072]{1,0:T(2,128)}, u32[]{:S(2)}) copy-start(f32[2,3072]{1,0:T(2,128)} %param.39) | copy-start | bytes 73732
  2874.3 93.8 %copy-start.302 = (f32[2,768]{1,0:T(2,128)S(1)}, f32[2,768]{1,0:T(2,128)}, u32[]{:S(2)}) copy-start(f32[2,768]{1,0:T(2,128)} %param.41) | copy-start | bytes 18436
  2874.7 96.0 %copy-start.56 = (f32[2,96,768]{2,1,0:T(8,128)S(1)}, f32[2,96,768]{2,1,0:T(8,128)}, u32[]{:S(2)}) copy-start(f32[2,96,768]{2,1,0:T(8,128)} %get-tuple-element.362) | copy-start | bytes 1769476
  2875.5 97.1 %copy-start.290 = (f32[2,96]{1,0:T(2,128)}, f32[2,96]{1,0:T(2,128)S(1)}, u32[]{:S(2)}) copy-start(f32[2,96]{1,0:T(2,128)S(1)} %get-tuple-element.358) | copy-start | bytes 2308
  2875.6 96.9 %copy-start.286 = (f32[2,96]{1,0:T(2,128)}, f32[2,96]{1,0:T(2,128)S(1)}, u32[]{:S(2)}) copy-start(f32[2,96]{1,0:T(2,128)S(1)} %get-tuple-element.363) | copy-start | bytes 2308
  2875.8 96.8 %copy-start.288 = (f32[2,96]{1,0:T(2,128)}, f32[2,96]{1,0:T(2,128)S(1)}, u32[]{:S(2)}) copy-start(f32[2,96]{1,0:T(2,128)S(1)} %get-tuple-element.368) | copy-start | bytes 2308
  2875.9 96.7 %copy-start.209 = (f32[2,384]{1,0:T(2,128)}, f32[2,384]{1,0:T(2,128)S(1)}, u32[]{:S(2)}) copy-start(f32[2,384]{1,0:T(2,128)S(1)} %get-tuple-element.373) | copy-start | bytes 9220
  2876.5 96.9 %copy-start.303 = (f32[96]{0:T(128)}, f32[96]{0:T(128)S(1)}, u32[]{:S(2)}) copy-start(f32[96]{0:T(128)S(1)} %get-tuple-element.378) | copy-start | bytes 1156
  2899.7 72.9 %copy-start.305 = (f32[2]{0:T(128)}, f32[2]{0:T(128)S(1)}, u32[]{:S(2)}) copy-start(f32[2]{0:T(128)S(1)} %get-tuple-element.287) | copy-start | bytes 28
  2899.7 72.9 %copy-start.307 = (f32[2]{0:T(128)}, f32[2]{0:T(128)S(1)}, u32[]{:S(2)}) copy-start(f32[2]{0:T(128)S(1)} %get-tuple-element.288) | copy-start | bytes 28
  2899.7 72.9 %copy-start.308 = (f32[2]{0:T(128)}, f32[2]{0:T(128)S(1)}, u32[]{:S(2)}) copy-start(f32[2]{0:T(128)S(1)} %get-tuple-element.285) | copy-start | bytes 28
  2899.7 72.9 %copy-start.310 = (f32[2]{0:T(128)}, f32[2]{0:T(128)S(1)}, u32[]{:S(2)}) copy-start(f32[2]{0:T(128)S(1)} %get-tuple-element.286) | copy-start | bytes 28
  2968.0 45.8 %copy-start.172 = (f32[2,768]{1,0:T(2,128)}, f32[2,768]{1,0:T(2,128)S(1)}, u32[]{:S(2)}) copy-start(f32[2,768]{1,0:T(2,128)S(1)} %multiply_add_fusion.24) | copy-start | bytes 18436
  2968.1 49.6 %copy-start.173 = (f32[2,768]{1,0:T(2,128)}, f32[2,768]{1,0:T(2,128)S(1)}, u32[]{:S(2)}) copy-start(f32[2,768]{1,0:T(2,128)S(1)} %multiply_add_fusion.23) | copy-start | bytes 18436
  2983.7 30.0 copy-start.101
  (324 other events, 1275.9 us)
Sparse Core Ops, SparseCore 0:
  13.8 227.0 all-gather.17
  243.7 63.3 all-gather.19
  309.9 39.4 all-gather.21
  352.0 78.6 all-gather.23
  433.3 78.0 all-gather.25
  514.0 63.3 all-gather.27
  580.1 39.5 all-gather.29
  622.4 78.6 all-gather.31
  703.8 78.0 all-gather.33
  916.1 67.1 reduce-scatter.15
  987.3 68.3 reduce-scatter.13
  1059.2 128.0 reduce-scatter.11
  1191.5 128.0 reduce-scatter.9
  1323.0 162.5 reduce-scatter.23
  1489.0 162.5 reduce-scatter.21
  1655.1 162.5 reduce-scatter.19
  1821.1 162.5 reduce-scatter.17
  1987.5 532.6 reduce-scatter.25
  2526.4 137.8 all-reduce.7
  2668.6 199.6 all-reduce.9
  2899.7 65.8 all-reduce.5
where the time goes:
time: 3050 us; the launch traced here: 3040 us
  waiting for transfers between devices  2390 us (78%)
  matrix products  224 us (7%)
  local copies, waits for them, and re-layouts  177 us (6%)
  other arithmetic  141 us (5%)
  blocking collectives  81.2 us (3%)
    reduce_scatter x1, waiting for transfers between devices, local(): lax.psum_scatter(grad_wmod, 'dp', scatter_dimension=0, tiled=True)  533 us
    reduce_scatter x2, waiting for transfers between devices, local(): lax.psum_scatter(grads[3], 'dp', scatter_dimension=0, tiled=True)  329 us
    reduce_scatter x2, waiting for transfers between devices, local(): lax.psum_scatter(grads[2], 'dp', scatter_dimension=0, tiled=True)  329 us
    psum x1, waiting for transfers between devices, local(): lax.psum((grad_qkv, grad_proj, grad_fc1, grad_fc2, mod_acc), 'rep')  198 us
    reduce_scatter x2, waiting for transfers between devices, local(): lax.psum_scatter(grads[0], 'dp', scatter_dimension=0, tiled=True)  189 us
    dot_general x68, matrix products, product(): return jnp.dot(left, right, preferred_element_type=jnp.float32)  187 us
    all_gather x1, waiting for transfers between devices, local(): mod_full = lax.all_gather(mod_shard, 'dp', axis=0, tiled=True)  162 us
    all_gather x2, waiting for transfers between devices, local(): lax.all_gather(shard_low[2][layer_index], 'dp', axis=0, tiled=True)  154 us
  transfers between devices with their start and end apart: 21, of which 19 were waited for; matrix products, arithmetic and copies ran while one was open for 11% of the time, Pallas kernels for 0%

commit v1 on v0

--- a/solution.py
+++ b/solution.py
@@ -252,154 +252,147 @@
     small_second,
 ):
     pieces = unpack(small)
-    count_all = (
-        latents.shape[0]
-        * latents.shape[1]
-        * lax.axis_size("dp")
-        * lax.axis_size("rep")
-        * GRID
-        * GRID
-        * PDIM
-    )
+    dp_size, rep_size = lax.axis_size("dp"), lax.axis_size("rep")
+    everyone = dp_size * rep_size
+    number = latents.shape[0] * latents.shape[1]
+    count_all = number * everyone * GRID * GRID * PDIM
+    rows_mod = w_mod.shape[0]
+    first_row = lax.axis_index("dp") * rows_mod
     places = position_table()
-    shard_low = (
-        w_qkv.astype(jnp.bfloat16),
-        w_proj.astype(jnp.bfloat16),
-        w_fc1.astype(jnp.bfloat16),
-        w_fc2.astype(jnp.bfloat16),
-    )
-    mod_shard = w_mod.astype(jnp.bfloat16)
     patch_low = pieces["patch_w"].astype(jnp.bfloat16)
     time1_low = pieces["time1_w"].astype(jnp.bfloat16)
     time2_low = pieces["time2_w"].astype(jnp.bfloat16)
     head_low = pieces["head_w"].astype(jnp.bfloat16)
-    block_acc = [None] * LAYERS
-    mod_acc = None
-    small_acc = jnp.zeros_like(small)
-    loss_acc = jnp.zeros((), jnp.float32)
-    for micro in range(MICRO):
-        mod_full = lax.all_gather(mod_shard, "dp", axis=0, tiled=True)
-        picker = (timesteps[micro][:, None] == jnp.arange(STEPS_T)[None, :]).astype(jnp.float32)
-        factors = jnp.dot(picker, roster.T, precision=HIGHEST)
-        noised = factors[:, 0:1] * latents[micro] + factors[:, 1:2] * noise_field[micro]
-        tokens = patchify(noised).astype(jnp.bfloat16)
-        target = patchify(noise_field[micro]).reshape(-1, PDIM)
-        number = tokens.shape[0]
-        residual = (product(tokens.reshape(-1, PDIM), patch_low) + pieces["patch_b"]).reshape(
-            number, GRID * GRID, D
-        ) + places
-        features = time_features(timesteps[micro]).astype(jnp.bfloat16)
-        hidden_t = product(features, time1_low) + pieces["time1_b"]
-        silu_t = jax.nn.silu(hidden_t).astype(jnp.bfloat16)
-        chosen = jnp.where(drop_mask[micro] == 1, CLASSES, labels[micro])
-        onehot = (chosen[:, None] == jnp.arange(CLASSES + 1)[None, :]).astype(jnp.float32)
-        condition = (
-            product(silu_t, time2_low)
-            + pieces["time2_b"]
-            + jnp.dot(onehot, pieces["class_tab"], precision=HIGHEST)
+    mod_shard = w_mod.astype(jnp.bfloat16)
+
+    own_ids = jnp.stack([timesteps, labels, drop_mask]).reshape(3, number)
+    all_ids = lax.all_gather(own_ids, ("dp", "rep"), axis=0, tiled=False)
+    all_ids = all_ids.transpose(1, 0, 2).reshape(3, everyone * number)
+    features = time_features(all_ids[0]).astype(jnp.bfloat16)
+    hidden_t = product(features, time1_low) + pieces["time1_b"]
+    silu_t = jax.nn.silu(hidden_t).astype(jnp.bfloat16)
+    chosen = jnp.where(all_ids[2] == 1, CLASSES, all_ids[1])
+    onehot = (chosen[:, None] == jnp.arange(CLASSES + 1)[None, :]).astype(jnp.float32)
+    condition = (
+        product(silu_t, time2_low)
+        + pieces["time2_b"]
+        + jnp.dot(onehot, pieces["class_tab"], precision=HIGHEST)
+    )
+    silu_c = jax.nn.silu(condition).astype(jnp.bfloat16)
+    silu_rows = lax.dynamic_slice_in_dim(silu_c, first_row, rows_mod, axis=1)
+    group_rows = lax.dynamic_index_in_dim(
+        silu_rows.reshape(dp_size, rep_size, number, rows_mod),
+        lax.axis_index("rep"),
+        axis=1,
+        keepdims=False,
+    ).reshape(dp_size * number, rows_mod)
+    modulation = (
+        lax.psum_scatter(product(group_rows, mod_shard), "dp", scatter_dimension=0, tiled=True)
+        + pieces["mod_b"]
+    )
+
+    picker = (timesteps.reshape(-1)[:, None] == jnp.arange(STEPS_T)[None, :]).astype(jnp.float32)
+    factors = jnp.dot(picker, roster.T, precision=HIGHEST)
+    noise_flat = noise_field.reshape(number, -1)
+    noised = factors[:, 0:1] * latents.reshape(number, -1) + factors[:, 1:2] * noise_flat
+    tokens = patchify(noised).astype(jnp.bfloat16)
+    target = patchify(noise_flat).reshape(-1, PDIM)
+    residual = (product(tokens.reshape(-1, PDIM), patch_low) + pieces["patch_b"]).reshape(
+        number, GRID * GRID, D
+    ) + places
+    kept_all = []
+    gathered_all = []
+    spans_all = []
+    for layer_index in range(LAYERS):
+        weights = tuple(
+            lax.all_gather(w[layer_index].astype(jnp.bfloat16), "dp", axis=0, tiled=True)
+            for w in (w_qkv, w_proj, w_fc1, w_fc2)
         )
-        silu_c = jax.nn.silu(condition).astype(jnp.bfloat16)
-        modulation = product(silu_c, mod_full) + pieces["mod_b"]
-        kept_all = []
-        gathered_all = []
-        spans_all = []
-        for layer_index in range(LAYERS):
-            weights = (
-                lax.all_gather(shard_low[0][layer_index], "dp", axis=0, tiled=True),
-                lax.all_gather(shard_low[1][layer_index], "dp", axis=0, tiled=True),
-                lax.all_gather(shard_low[2][layer_index], "dp", axis=0, tiled=True),
-                lax.all_gather(shard_low[3][layer_index], "dp", axis=0, tiled=True),
-            )
-            spans = [
-                modulation[:, None, D * (6 * layer_index + i) : D * (6 * layer_index + i + 1)]
-                for i in range(6)
-            ]
-            residual, kept = layer_forward(residual, spans, weights, pieces["block_b"][layer_index])
-            kept_all.append(kept)
-            gathered_all.append(weights)
-            spans_all.append(spans)
-        final_shift = modulation[:, None, 6 * D * LAYERS : 6 * D * LAYERS + D]
-        final_scale = modulation[:, None, 6 * D * LAYERS + D :]
-        normed_f, inverse_f = norm_rows(residual)
-        final_in = (
-            (normed_f * (1.0 + final_scale) + final_shift).astype(jnp.bfloat16).reshape(-1, D)
+        spans = [
+            modulation[:, None, D * (6 * layer_index + i) : D * (6 * layer_index + i + 1)]
+            for i in range(6)
+        ]
+        residual, kept = layer_forward(residual, spans, weights, pieces["block_b"][layer_index])
+        kept_all.append(kept)
+        gathered_all.append(weights)
+        spans_all.append(spans)
+    final_shift = modulation[:, None, 6 * D * LAYERS : 6 * D * LAYERS + D]
+    final_scale = modulation[:, None, 6 * D * LAYERS + D :]
+    normed_f, inverse_f = norm_rows(residual)
+    final_in = (normed_f * (1.0 + final_scale) + final_shift).astype(jnp.bfloat16).reshape(-1, D)
+    output = product(final_in, head_low) + pieces["head_b"]
+    error = output - target
+    loss_own = jnp.sum(error * error)
+    grad_output = (error * (2.0 / count_all)).astype(jnp.bfloat16)
+    grad_head = product(final_in.T, grad_output)
+    grad_head_b = jnp.sum(grad_output.astype(jnp.float32), axis=0)
+    grad_final = product(grad_output, head_low.T).reshape(number, GRID * GRID, D)
+    final_grads = [jnp.sum(grad_final, axis=1), jnp.sum(grad_final * normed_f, axis=1)]
+    grad_res = norm_back(grad_final * (1.0 + final_scale), normed_f, inverse_f)
+    layer_spans = [None] * LAYERS
+    bias_grads = [None] * LAYERS
+    block_grads = [None] * LAYERS
+    for layer_index in reversed(range(LAYERS)):
+        grad_res, grads, grad_bias, grad_spans = layer_backward(
+            grad_res, spans_all[layer_index], gathered_all[layer_index], kept_all[layer_index]
         )
-        output = product(final_in, head_low) + pieces["head_b"]
-        error = output - target
-        loss_acc = loss_acc + jnp.sum(error * error)
-        grad_output = (error * (2.0 / count_all)).astype(jnp.bfloat16)
-        grad_head = product(final_in.T, grad_output)
-        grad_head_b = jnp.sum(grad_output.astype(jnp.float32), axis=0)
-        grad_final = product(grad_output, head_low.T).reshape(number, GRID * GRID, D)
-        final_grads = [jnp.sum(grad_final, axis=1), jnp.sum(grad_final * normed_f, axis=1)]
-        grad_res = norm_back(grad_final * (1.0 + final_scale), normed_f, inverse_f)
-        layer_spans = [None] * LAYERS
-        bias_grads = [None] * LAYERS
-        for layer_index in reversed(range(LAYERS)):
-            weights = (
-                lax.all_gather(shard_low[0][layer_index], "dp", axis=0, tiled=True),
-                lax.all_gather(shard_low[1][layer_index], "dp", axis=0, tiled=True),
-                lax.all_gather(shard_low[2][layer_index], "dp", axis=0, tiled=True),
-                lax.all_gather(shard_low[3][layer_index], "dp", axis=0, tiled=True),
-            )
-            grad_res, grads, grad_bias, grad_spans = layer_backward(
-                grad_res, spans_all[layer_index], weights, kept_all[layer_index]
-            )
-            layer_spans[layer_index] = grad_spans
-            bias_grads[layer_index] = grad_bias
-            shards = (
-                lax.psum_scatter(grads[0], "dp", scatter_dimension=0, tiled=True),
-                lax.psum_scatter(grads[1], "dp", scatter_dimension=0, tiled=True),
-                lax.psum_scatter(grads[2], "dp", scatter_dimension=0, tiled=True),
-                lax.psum_scatter(grads[3], "dp", scatter_dimension=0, tiled=True),
-            )
-            if micro == 0:
-                block_acc[layer_index] = shards
-            else:
-                block_acc[layer_index] = tuple(
-                    (a + b for a, b in zip(block_acc[layer_index], shards))
-                )
-        grad_mod = jnp.concatenate(layer_spans + final_grads, axis=-1).astype(jnp.bfloat16)
-        grad_wmod = product(silu_c.T, grad_mod)
-        grad_mod_b = jnp.sum(grad_mod.astype(jnp.float32), axis=0)
-        mod_back = lax.all_gather(mod_shard, "dp", axis=0, tiled=True)
-        _, silu_pull = jax.vjp(jax.nn.silu, condition)
-        grad_cond = silu_pull(product(grad_mod, mod_back.T))[0].astype(jnp.bfloat16)
-        grad_class = jnp.dot(onehot.T, grad_cond.astype(jnp.float32), precision=HIGHEST)
-        grad_time2 = product(silu_t.T, grad_cond)
-        grad_time2_b = jnp.sum(grad_cond.astype(jnp.float32), axis=0)
-        _, silu_time_pull = jax.vjp(jax.nn.silu, hidden_t)
-        grad_hidden_t = silu_time_pull(product(grad_cond, time2_low.T))[0].astype(jnp.bfloat16)
-        grad_time1 = product(features.T, grad_hidden_t)
-        grad_time1_b = jnp.sum(grad_hidden_t.astype(jnp.float32), axis=0)
-        grad_start = grad_res.reshape(-1, D).astype(jnp.bfloat16)
-        grad_patch = product(tokens.reshape(-1, PDIM).T, grad_start)
-        grad_patch_b = jnp.sum(grad_start.astype(jnp.float32), axis=0)
-        mod_part = lax.psum_scatter(grad_wmod, "dp", scatter_dimension=0, tiled=True)
-        mod_acc = mod_part if micro == 0 else mod_acc + mod_part
-        small_acc = small_acc + jnp.concatenate(
+        layer_spans[layer_index] = grad_spans
+        bias_grads[layer_index] = grad_bias
+        block_grads[layer_index] = tuple(
+            lax.psum_scatter(g, "dp", scatter_dimension=0, tiled=True) for g in grads
+        )
+    grad_qkv, grad_proj, grad_fc1, grad_fc2 = lax.psum(
+        tuple(jnp.stack([block_grads[i][k] for i in range(LAYERS)]) for k in range(4)), "rep"
+    )
+
+    own_mod = jnp.concatenate(layer_spans + final_grads, axis=-1).astype(jnp.bfloat16)
+    grad_mod = lax.all_gather(own_mod, ("dp", "rep"), axis=0, tiled=True)
+    grad_wmod = product(silu_rows.T, grad_mod)
+    grad_mod_b = jnp.sum(grad_mod.astype(jnp.float32), axis=0)
+    cond_rows = lax.all_gather(product(grad_mod, mod_shard.T), "dp", axis=1, tiled=True)
+    _, silu_pull = jax.vjp(jax.nn.silu, condition)
+    grad_cond = silu_pull(cond_rows)[0].astype(jnp.bfloat16)
+    grad_class = jnp.dot(onehot.T, grad_cond.astype(jnp.float32), precision=HIGHEST)
+    grad_time2 = product(silu_t.T, grad_cond)
+    grad_time2_b = jnp.sum(grad_cond.astype(jnp.float32), axis=0)
+    _, silu_time_pull = jax.vjp(jax.nn.silu, hidden_t)
+    grad_hidden_t = silu_time_pull(product(grad_cond, time2_low.T))[0].astype(jnp.bfloat16)
+    grad_time1 = product(features.T, grad_hidden_t)
+    grad_time1_b = jnp.sum(grad_hidden_t.astype(jnp.float32), axis=0)
+    grad_start = grad_res.reshape(-1, D).astype(jnp.bfloat16)
+    grad_patch = product(tokens.reshape(-1, PDIM).T, grad_start)
+    grad_patch_b = jnp.sum(grad_start.astype(jnp.float32), axis=0)
+    summed = lax.psum(
+        jnp.concatenate(
             [
                 grad_patch.reshape(-1),
                 grad_patch_b,
-                grad_time1.reshape(-1),
-                grad_time1_b,
-                grad_time2.reshape(-1),
-                grad_time2_b,
-                grad_class.reshape(-1),
-                grad_mod_b,
                 grad_head.reshape(-1),
+                jnp.stack(bias_grads).reshape(-1),
                 grad_head_b,
-                jnp.stack(bias_grads).reshape(-1),
+                loss_own[None],
             ]
-        )
-    grad_qkv = jnp.stack([block_acc[i][0] for i in range(LAYERS)])
-    grad_proj = jnp.stack([block_acc[i][1] for i in range(LAYERS)])
-    grad_fc1 = jnp.stack([block_acc[i][2] for i in range(LAYERS)])
-    grad_fc2 = jnp.stack([block_acc[i][3] for i in range(LAYERS)])
-    grad_qkv, grad_proj, grad_fc1, grad_fc2, grad_wmod = lax.psum(
-        (grad_qkv, grad_proj, grad_fc1, grad_fc2, mod_acc), "rep"
-    )
-    small_grad, loss_total = lax.psum((small_acc, loss_acc), ("dp", "rep"))
+        ),
+        ("dp", "rep"),
+    )
+    cut_patch = (PDIM + 1) * D
+    cut_head = cut_patch + D * PDIM
+    cut_bias = cut_head + LAYERS * (4 * D + FF)
+    loss_total = summed[cut_bias + PDIM]
+    small_grad = jnp.concatenate(
+        [
+            summed[:cut_patch],
+            grad_time1.reshape(-1),
+            grad_time1_b,
+            grad_time2.reshape(-1),
+            grad_time2_b,
+            grad_class.reshape(-1),
+            grad_mod_b,
+            summed[cut_patch:cut_head],
+            summed[cut_bias : cut_bias + PDIM],
+            summed[cut_head:cut_bias],
+        ]
+    )
     beta = 1.0 - STEP ** (-0.8)
     rows_dp = lax.axis_size("dp")
     kinds = [
@@ -411,51 +404,44 @@
     ]
     firsts = []
     for weight, grad, row, col in kinds:
-        square = grad * grad + EPS_ONE
-        row_new = beta * row + (1.0 - beta) * jnp.mean(square, axis=-1)
+        square = grad * grad
+        row_new = beta * row + (1.0 - beta) * jnp.mean(square + EPS_ONE, axis=-1)
         firsts.append(
             (
                 row_new,
-                jnp.sum(square, axis=-2),
+                jnp.sum(square + EPS_ONE, axis=-2),
+                jnp.sum(square / row_new[:, :, None], axis=-2),
                 jnp.sum(row_new, axis=-1),
                 jnp.sum(weight * weight, axis=(-2, -1)),
             )
         )
-    col_flat = jnp.concatenate([entry[1].reshape(-1) for entry in firsts])
-    row_flat = jnp.concatenate([entry[2] for entry in firsts])
-    weight_flat = jnp.concatenate([entry[3] for entry in firsts])
-    col_flat, row_flat, weight_flat = lax.psum((col_flat, row_flat, weight_flat), "dp")
+    shared = lax.psum(
+        jnp.concatenate([entry[k].reshape(-1) for k in range(1, 5) for entry in firsts]), "dp"
+    )
+    parts = []
+    offset = 0
+    for k in range(1, 5):
+        for entry in firsts:
+            parts.append(shared[offset : offset + entry[k].size].reshape(entry[k].shape))
+            offset += entry[k].size
     seconds = []
-    col_offset = 0
-    lay_offset = 0
-    for kind, first in zip(kinds, firsts):
+    for index, kind in enumerate(kinds):
         weight, grad, row, col = kind
-        stacked, col_count = (weight.shape[0], weight.shape[2])
         rows_all = weight.shape[1] * rows_dp
-        col_sum = col_flat[col_offset : col_offset + stacked * col_count].reshape(
-            stacked, col_count
-        )
-        row_mean = row_flat[lay_offset : lay_offset + stacked] / rows_all
-        weight_rms = jnp.sqrt(
-            weight_flat[lay_offset : lay_offset + stacked] / (rows_all * col_count)
-        )
-        col_offset += stacked * col_count
-        lay_offset += stacked
+        col_count = weight.shape[2]
+        col_sum, over_rows, row_sum, weight_sq = (parts[index + len(kinds) * k] for k in range(4))
+        row_mean = row_sum / rows_all
+        weight_rms = jnp.sqrt(weight_sq / (rows_all * col_count))
         col_new = beta * col + (1.0 - beta) * col_sum / rows_all
-        estimate = first[0][:, :, None] * col_new[:, None, :] / row_mean[:, None, None]
+        update_sq = row_mean * jnp.sum(over_rows / col_new, axis=-1)
+        estimate = firsts[index][0][:, :, None] * col_new[:, None, :] / row_mean[:, None, None]
         update = grad * lax.rsqrt(estimate)
-        seconds.append((update, col_new, weight_rms, rows_all * col_count))
-    update_sq = lax.psum(
-        jnp.concatenate([jnp.sum(entry[0] * entry[0], axis=(-2, -1)) for entry in seconds]), "dp"
-    )
+        seconds.append((update, col_new, weight_rms, update_sq / (rows_all * col_count)))
     results = []
-    lay_offset = 0
     for kind, first, second in zip(kinds, firsts, seconds):
         weight, grad = (kind[0], kind[1])
-        update, col_new, weight_rms, entries = second
-        stacked = weight.shape[0]
-        update_rms = jnp.sqrt(update_sq[lay_offset : lay_offset + stacked] / entries)
-        lay_offset += stacked
+        update, col_new, weight_rms, update_ms = second
+        update_rms = jnp.sqrt(update_ms)
         update = update / jnp.maximum(1.0, update_rms / CLIP)[:, None, None]
         new_weight = weight - (RATE * jnp.maximum(0.001, weight_rms))[:, None, None] * update
         results.append((new_weight, grad, first[0], col_new, new_weight.astype(jnp.bfloat16)))

time: 3050 us -> 2330 us (0.76)
  waiting for transfers between devices: 2390 us -> 1770 us
  matrix products: 224 us -> 184 us
    reduce_scatter x9 -> x8, waiting for transfers between devices: 1380 us -> 1060 us  [local(): lax.psum_scatter(g, 'dp', scatter_dimension=0, tiled=True)]
    psum x3, waiting for transfers between devices: 363 us -> 161 us  [the longest x1 63.1 us: local(): lax.psum(jnp.concatenate([entry[k].reshape(-1) for k in range(1, 5) for e...]
    all_gather x9, waiting for transfers between devices: 643 us -> 498 us  [the longest x8 441 us: local(): lax.all_gather(w[layer_index].astype(jnp.bfloat16), 'dp', axis=0, tiled=T...]
    psum x3 -> x0, blocking collectives: 81.2 us -> none  [the longest x1 39.5 us: local(): small_grad, loss_total = lax.psum((small_acc, loss_acc), ('dp', 'rep'))]
    all_gather x0 -> x2, blocking collectives: none -> 74.2 us  [the longest x1 43.4 us: local(): all_ids = lax.all_gather(own_ids, ('dp', 'rep'), axis=0, tiled=False)]
    unnamed x21 -> x22, waiting for transfers between devices: 2.87 us -> 44.9 us
    concatenate x8 -> x3, local copies, waits for them, and re-layouts: 72.4 us -> 32.3 us  [the longest x1 28.9 us: local(): jnp.concatenate([summed[:cut_patch], grad_time1.reshape(-1), grad_time1_b...]
    dot_general x68 -> x37, matrix products: 187 us -> 157 us  [product(): return jnp.dot(left, right, preferred_element_type=jnp.float32)]
  transfers between devices with their start and end apart: 21 -> 21, of which waited for: 19 -> 21; matrix products, arithmetic and copies ran while one was open for 11% -> 11% of each run, Pallas kernels for 0% -> 0%
where the time goes in v1:
time: 2330 us; the launch traced here: 2320 us
  waiting for transfers between devices  1770 us (76%)
  matrix products  184 us (8%)
  local copies, waits for them, and re-layouts  155 us (7%)
  other arithmetic  116 us (5%)
  blocking collectives  74.2 us (3%)
    reduce_scatter x8, waiting for transfers between devices, local(): lax.psum_scatter(g, 'dp', scatter_dimension=0, tiled=True)  1060 us
    all_gather x8, waiting for transfers between devices, local(): lax.all_gather(w[layer_index].astype(jnp.bfloat16), 'dp', axis=0, tiled=T...  441 us
    dot_general x37, matrix products, product(): return jnp.dot(left, right, preferred_element_type=jnp.float32)  157 us
    psum x1, waiting for transfers between devices, local(): lax.psum(jnp.concatenate([entry[k].reshape(-1) for k in range(1, 5) for e...  63.1 us
    all_gather x1, waiting for transfers between devices, local(): grad_mod = lax.all_gather(own_mod, ('dp', 'rep'), axis=0, tiled=True)  56.5 us
    psum x1, waiting for transfers between devices, local(): lax.psum(jnp.concatenate([grad_patch.reshape(-1), grad_patch_b, grad_head...  50.1 us
    psum x1, waiting for transfers between devices, local(): lax.psum(tuple((jnp.stack([block_grads[i][k] for i in range(LAYERS)]) for...  48 us
  transfers between devices with their start and end apart: 21, of which 21 were waited for; matrix products, arithmetic and copies ran while one was open for 11% of the time, Pallas kernels for 0%

profile of v1, /device:TPU:0, one launch (start us, length us, event | category | flops | bytes accessed | tf_op | source)
XLA Modules:
  0.0 2320.5 jit_solution(9341782011903536567)
XLA Ops:
  9.7 4.5 multiply_reduce_fusion.6
  15.8 43.4 %all-gather = s32[96,2,1]{1,2,0:T(1,128)S(1)} all-gather(s32[3,2,1]{1,2,0:T(1,128)S(1)} %pad_add_fusion), channel_id=2, replica_groups=mesh['dp'=8,'rep'=4] {'dp','rep'}, dimensions={0}, use_global_device_ids=true | all-gather | bytes 792 | tf_op jit(solution)/shard_map/all_gather | solution.py:269
  63.5 3.5 fusion.74
  94.8 42.1 %all-reduce.11.cloned.1.call-done = f32[16,10752]{1,0:T(8,128)} async-done(((f32[16,10752]{1,0:T(8,128)}), f32[16,10752]{1,0:T(8,128)}) %all-reduce.11.cloned.1.call-update) | async-done | bytes 688144
  139.3 64.8 %all-gather.21.cloned.1.call-done = bf16[1,768,2304]{2,1,0:T(8,128)(2,1)} async-done(((bf16[1,96,2304]{2,1,0:T(8,128)(2,1)}), bf16[1,768,2304]{2,1,0:T(8,128)(2,1)}) %all-gather.21.cloned.1.call-update) | async-done | bytes 3538960 | tf_op jit(solution)/shard_map/all_gather | solution.py:308
  204.1 5.7 fusion.30
  209.8 4.3 copy.158
  214.1 6.0 reshape.798
  220.1 3.4 fusion.164
  230.4 16.3 all-gather.23.cloned.1.call-done
  246.7 4.1 fusion.159
  255.2 73.0 %all-gather.25.cloned.1.call-done = bf16[1,768,3072]{2,1,0:T(8,128)(2,1)} async-done(((bf16[1,96,3072]{2,1,0:T(8,128)(2,1)}), bf16[1,768,3072]{2,1,0:T(8,128)(2,1)}) %all-gather.25.cloned.1.call-update) | async-done | bytes 4718608 | tf_op jit(solution)/shard_map/all_gather | solution.py:308
  328.2 7.9 fusion.28
  336.1 73.0 %all-gather.27.cloned.1.call-done = bf16[1,3072,768]{2,1,0:T(8,128)(2,1)} async-done(((bf16[1,384,768]{2,1,0:T(8,128)(2,1)}), bf16[1,3072,768]{2,1,0:T(8,128)(2,1)}) %all-gather.27.cloned.1.call-update) | async-done | bytes 4718608 | tf_op jit(solution)/shard_map/all_gather | solution.py:308
  409.1 10.3 fusion.157
  423.8 51.7 %all-gather.29.cloned.1.call-done = bf16[1,768,2304]{2,1,0:T(8,128)(2,1)} async-done(((bf16[1,96,2304]{2,1,0:T(8,128)(2,1)}), bf16[1,768,2304]{2,1,0:T(8,128)(2,1)}) %all-gather.29.cloned.1.call-update) | async-done | bytes 3538960 | tf_op jit(solution)/shard_map/all_gather | solution.py:308
  475.5 5.7 fusion.31
  481.1 4.3 copy.164
  485.4 6.0 reshape.800
  501.3 16.6 all-gather.31.cloned.1.call-done
  517.9 4.5 fusion.155
  526.8 72.7 %all-gather.33.cloned.1.call-done = bf16[1,768,3072]{2,1,0:T(8,128)(2,1)} async-done(((bf16[1,96,3072]{2,1,0:T(8,128)(2,1)}), bf16[1,768,3072]{2,1,0:T(8,128)(2,1)}) %all-gather.33.cloned.1.call-update) | async-done | bytes 4718608 | tf_op jit(solution)/shard_map/all_gather | solution.py:308
  599.6 7.8 fusion.20
  607.4 73.2 %all-gather.35.cloned.1.call-done = bf16[1,3072,768]{2,1,0:T(8,128)(2,1)} async-done(((bf16[1,384,768]{2,1,0:T(8,128)(2,1)}), bf16[1,3072,768]{2,1,0:T(8,128)(2,1)}) %all-gather.35.cloned.1.call-update) | async-done | bytes 4718608 | tf_op jit(solution)/shard_map/all_gather | solution.py:308
  680.6 10.3 fusion.153
  696.4 5.4 multiply_reduce_fusion.10
  703.6 6.5 convert_reduce_fusion
  710.2 3.8 fusion.58
  714.1 3.2 fusion.49
  726.4 5.3 convolution_bitcast_fusion.1
  747.4 6.7 convert_reduce_fusion.1
  754.2 3.8 fusion.57
  758.1 3.5 fusion.50
  770.6 5.3 convolution_bitcast_fusion
  788.7 5.0 multiply_reduce_fusion.16
  799.4 3.5 fusion.178
  806.7 4.9 fusion.177
  816.9 4.9 fusion.176
  823.0 10.1 fusion.138
  834.2 10.2 fusion.137
  846.2 6.4 fusion.180
  854.5 6.2 fusion.181
  861.5 3.9 multiply_reduce_fusion.4
  865.3 50.1 %all-reduce.7.cloned.1.call-done = f32[37649]{0:T(1024)} async-done(((f32[37649]{0:T(1024)}), f32[37649]{0:T(1024)}) %all-reduce.7.cloned.1.call-update) | async-done | bytes 150612 | tf_op jit(solution)/shard_map/psum | solution.py:365
  919.4 56.5 %all-gather.37.cloned.1.call-done = bf16[32,2,10752]{2,1,0:T(2,128)(2,1)} async-done(((bf16[1,2,10752]{2,1,0:T(2,128)(2,1)}), bf16[32,2,10752]{2,1,0:T(2,128)(2,1)}) %all-gather.37.cloned.1.call-update) | async-done | bytes 1376272 | tf_op jit(solution)/shard_map/all_gather | solution.py:349
  977.6 70.6 %reduce-scatter.15.cloned.1.call-done = f32[96,768]{1,0:T(8,128)} async-done(((f32[768,768]{1,0:T(8,128)}), f32[96,768]{1,0:T(8,128)}) %reduce-scatter.15.cloned.1.call-update) | async-done | bytes 294928 | tf_op jit(solution)/shard_map/reduce_scatter | solution.py:342
  1048.2 72.7 %reduce-scatter.13.cloned.1.call-done = f32[96,768]{1,0:T(8,128)} async-done(((f32[768,768]{1,0:T(8,128)}), f32[96,768]{1,0:T(8,128)}) %reduce-scatter.13.cloned.1.call-update) | async-done | bytes 294928 | tf_op jit(solution)/shard_map/reduce_scatter | solution.py:342
  1122.8 130.2 %reduce-scatter.11.cloned.1.call-done = f32[96,2304]{1,0:T(8,128)} async-done(((f32[768,2304]{1,0:T(8,128)}), f32[96,2304]{1,0:T(8,128)}) %reduce-scatter.11.cloned.1.call-update) | async-done | bytes 884752 | tf_op jit(solution)/shard_map/reduce_scatter | solution.py:342
  1253.0 131.6 %reduce-scatter.9.cloned.1.call-done = f32[96,2304]{1,0:T(8,128)} async-done(((f32[768,2304]{1,0:T(8,128)}), f32[96,2304]{1,0:T(8,128)}) %reduce-scatter.9.cloned.1.call-update) | async-done | bytes 884752 | tf_op jit(solution)/shard_map/reduce_scatter | solution.py:342
  1387.4 163.5 %reduce-scatter.23.cloned.1.call-done = f32[384,768]{1,0:T(8,128)} async-done(((f32[3072,768]{1,0:T(8,128)}), f32[384,768]{1,0:T(8,128)}) %reduce-scatter.23.cloned.1.call-update) | async-done | bytes 1179664 | tf_op jit(solution)/shard_map/reduce_scatter | solution.py:342
  1550.9 166.3 %reduce-scatter.21.cloned.1.call-done = f32[384,768]{1,0:T(8,128)} async-done(((f32[3072,768]{1,0:T(8,128)}), f32[384,768]{1,0:T(8,128)}) %reduce-scatter.21.cloned.1.call-update) | async-done | bytes 1179664 | tf_op jit(solution)/shard_map/reduce_scatter | solution.py:342
  1717.2 3.2 pad_maximum_fusion.1
  1720.3 163.1 %reduce-scatter.17.cloned.1.call-done = f32[96,3072]{1,0:T(8,128)} async-done(((f32[768,3072]{1,0:T(8,128)}), f32[96,3072]{1,0:T(8,128)}) %reduce-scatter.17.cloned.1.call-update) | async-done | bytes 1179664 | tf_op jit(solution)/shard_map/reduce_scatter | solution.py:342
  1883.5 166.5 %reduce-scatter.19.cloned.1.call-done = f32[96,3072]{1,0:T(8,128)} async-done(((f32[768,3072]{1,0:T(8,128)}), f32[96,3072]{1,0:T(8,128)}) %reduce-scatter.19.cloned.1.call-update) | async-done | bytes 1179664 | tf_op jit(solution)/shard_map/reduce_scatter | solution.py:342
  2049.9 3.3 pad_maximum_fusion
  2056.5 30.8 %all-gather.10 = f32[8,96,64]{1,2,0:T(8,128)S(1)} all-gather(f32[1,96,64]{1,2,0:T(8,128)S(1)} %convolution_bitcast_fusion.2), channel_id=1, replica_groups=mesh['dp'=8,'rep'=4] {'dp'}, dimensions={0}, use_global_device_ids=true | all-gather | bytes 221184 | tf_op jit(solution)/shard_map/all_gather | solution.py:352
  2092.3 3.5 reshape.827
  2096.0 28.9 %concatenate.41 = f32[861712]{0:T(1024)S(1)} concatenate(f32[13056]{0:T(1024)S(1)} %slice-done.17, f32[196608]{0:T(1024)} %reshape.826, f32[768]{0:T(1024)S(1)} %get-tuple-element.72, f32[589824]{0:T(1024)} %reshape.827, f32[768]{0:T(1024)S(1)} %get-tuple-element.70, f32[25344]{0:T(1024)} %reshape.828, f32[10752]{0:T(1024)S(1)} %convert_reduce_fusion.4, ...), dimensions={0} | concatenate | bytes 6893696 | tf_op jit(solution)/shard_map/concatenate | solution.py:382
  2124.9 7.1 multiply_reduce_fusion.5
  2137.8 48.0 %all-reduce.13.cloned.1.call-done = (f32[2,96,2304]{2,1,0:T(8,128)}, f32[2,96,768]{2,1,0:T(8,128)}, f32[2,96,3072]{2,1,0:T(8,128)}, f32[2,384,768]{2,1,0:T(8,128)}) async-done(((f32[2,96,2304]{2,1,0:T(8,128)}, f32[2,96,768]{2,1,0:T(8,128)}, f32[2,96,3072]{2,1,0:T(8,128)}, f32[2,384,768]{2,1,0:T(8,128)}), (f32[2,96,2304]{2,1,0:T(8,128)}, f32[2,96,768]{2,1,0:T(8,128)}, f32[2,96,3072]{2,1,0:T(8,128)}, ...) | async-done | bytes 7077904 | tf_op jit(solution)/shard_map/psum | solution.py:344
  2197.4 7.1 fusion.139
  2204.6 63.1 %all-reduce.9.cloned.1.call-done = f32[49170]{0:T(1024)} async-done(((f32[49170]{0:T(1024)}), f32[49170]{0:T(1024)}) %all-reduce.9.cloned.1.call-update) | async-done | bytes 196696 | tf_op jit(solution)/shard_map/psum | solution.py:418
  2292.5 3.7 fusion.147
  2304.6 3.8 fusion.142
  (607 shorter events, 212.2 us)
Async XLA Ops:
  7.2 74.2 %copy-start = (f32[2,1000]{1,0:T(2,128)S(1)}, f32[2,1000]{1,0:T(2,128)}, u32[]{:S(2)}) copy-start(f32[2,1000]{1,0:T(2,128)} %param.28) | copy-start | bytes 24004
  7.2 129.7 %all-reduce.11.cloned.1.call-start = ((), (), s32[]{:S(2)}) async-start(), calls=%async_computation.27 | async-start | bytes 1376256
  67.0 137.1 %all-gather.21.cloned.1.call-start = ((), (), s32[]{:S(2)}) async-start(), calls=%async_computation.18 | async-start | bytes 3981312 | tf_op jit(solution)/shard_map/all_gather | solution.py:308
  69.0 177.7 %all-gather.23.cloned.1.call-start = ((), (), s32[]{:S(2)}) async-start(), calls=%async_computation.19 | async-start | bytes 1327104 | tf_op jit(solution)/shard_map/all_gather | solution.py:308
  70.5 257.7 %all-gather.25.cloned.1.call-start = ((), (), s32[]{:S(2)}) async-start(), calls=%async_computation.20 | async-start | bytes 5308416 | tf_op jit(solution)/shard_map/all_gather | solution.py:308
  72.7 336.4 %all-gather.27.cloned.1.call-start = ((), (), s32[]{:S(2)}) async-start(), calls=%async_computation.21 | async-start | bytes 5308416 | tf_op jit(solution)/shard_map/all_gather | solution.py:308
  74.6 7.8 copy-start.88
  74.6 7.9 copy-start.89
  75.8 399.7 %all-gather.29.cloned.1.call-start = ((), (), s32[]{:S(2)}) async-start(), calls=%async_computation.22 | async-start | bytes 3981312 | tf_op jit(solution)/shard_map/all_gather | solution.py:308
  76.3 441.5 %all-gather.31.cloned.1.call-start = ((), (), s32[]{:S(2)}) async-start(), calls=%async_computation.23 | async-start | bytes 1327104 | tf_op jit(solution)/shard_map/all_gather | solution.py:308
  77.1 522.5 %all-gather.33.cloned.1.call-start = ((), (), s32[]{:S(2)}) async-start(), calls=%async_computation.24 | async-start | bytes 5308416 | tf_op jit(solution)/shard_map/all_gather | solution.py:308
  77.8 602.8 %all-gather.35.cloned.1.call-start = ((), (), s32[]{:S(2)}) async-start(), calls=%async_computation.25 | async-start | bytes 5308416 | tf_op jit(solution)/shard_map/all_gather | solution.py:308
  78.6 836.9 %all-reduce.7.cloned.1.call-start = ((), (), s32[]{:S(2)}) async-start(), calls=%async_computation.8 | async-start | bytes 303104 | tf_op jit(solution)/shard_map/psum | solution.py:365
  91.9 45.0 %slice-start.12 = ((f32[861712]{0:T(1024)}), f32[10752]{0:T(1024)S(1)}, s32[]{:S(2)}) async-start(f32[861712]{0:T(1024)} %param.44), calls=%async_computation.41 | async-start | bytes 90112 | tf_op jit(solution)/shard_map/slice | solution.py:57
  92.4 604.0 %copy-start.4 = (f32[512,768]{1,0:T(8,128)}, f32[512,768]{1,0:T(8,128)S(1)}, u32[]{:S(2)}) copy-start(f32[512,768]{1,0:T(8,128)S(1)} %get-tuple-element.240) | copy-start | bytes 4718596
  255.2 153.9 %copy-start.102 = (f32[768]{0:T(1024)S(1)}, f32[768]{0:T(1024)}, u32[]{:S(2)}) copy-start(f32[768]{0:T(1024)} %get-tuple-element.147) | copy-start | bytes 9220
  499.4 18.5 copy-start.100
  526.8 153.8 %copy-start.101 = (f32[768]{0:T(1024)S(1)}, f32[768]{0:T(1024)}, u32[]{:S(2)}) copy-start(f32[768]{0:T(1024)} %get-tuple-element.143) | copy-start | bytes 9220
  696.0 7.6 slice-start.6
  696.0 7.6 slice-start.15
  696.4 7.1 slice-start.7
  696.4 7.1 slice-start.16
  702.4 7.7 slice-start.10
  702.6 7.5 copy-start.70
  703.6 6.6 copy-start.8
  703.6 6.6 slice-start.11
  719.5 12.2 slice-start.2
  739.5 7.8 slice-start.4
  739.5 7.8 slice-start.13
  745.5 8.6 slice-start.8
  746.4 7.7 copy-start.72
  747.4 6.8 copy-start.9
  747.4 6.8 slice-start.9
  763.7 12.2 slice-start
  770.6 5.3 copy-start.55
  796.1 179.9 %all-gather.37.cloned.1.call-start = ((), (), s32[]{:S(2)}) async-start(), calls=%async_computation.26 | async-start | bytes 1419264 | tf_op jit(solution)/shard_map/all_gather | solution.py:349
  797.0 251.2 %reduce-scatter.15.cloned.1.call-start = ((), (), s32[]{:S(2)}) async-start(), calls=%async_computation.12 | async-start | bytes 2654208 | tf_op jit(solution)/shard_map/reduce_scatter | solution.py:342
  799.3 321.6 %reduce-scatter.13.cloned.1.call-start = ((), (), s32[]{:S(2)}) async-start(), calls=%async_computation.11 | async-start | bytes 2654208 | tf_op jit(solution)/shard_map/reduce_scatter | solution.py:342
  802.9 450.1 %reduce-scatter.11.cloned.1.call-start = ((), (), s32[]{:S(2)}) async-start(), calls=%async_computation.10 | async-start | bytes 7962624 | tf_op jit(solution)/shard_map/reduce_scatter | solution.py:342
  811.6 573.0 %reduce-scatter.9.cloned.1.call-start = ((), (), s32[]{:S(2)}) async-start(), calls=%async_computation.9 | async-start | bytes 7962624 | tf_op jit(solution)/shard_map/reduce_scatter | solution.py:342
  821.9 729.0 %reduce-scatter.23.cloned.1.call-start = ((), (), s32[]{:S(2)}) async-start(), calls=%async_computation.16 | async-start | bytes 10616832 | tf_op jit(solution)/shard_map/reduce_scatter | solution.py:342
  833.1 884.1 %reduce-scatter.21.cloned.1.call-start = ((), (), s32[]{:S(2)}) async-start(), calls=%async_computation.15 | async-start | bytes 10616832 | tf_op jit(solution)/shard_map/reduce_scatter | solution.py:342
  844.4 1039.1 %reduce-scatter.17.cloned.1.call-start = ((), (), s32[]{:S(2)}) async-start(), calls=%async_computation.13 | async-start | bytes 10616832 | tf_op jit(solution)/shard_map/reduce_scatter | solution.py:342
  852.6 1197.3 %reduce-scatter.19.cloned.1.call-start = ((), (), s32[]{:S(2)}) async-start(), calls=%async_computation.14 | async-start | bytes 10616832 | tf_op jit(solution)/shard_map/reduce_scatter | solution.py:342
  860.7 1325.0 %all-reduce.13.cloned.1.call-start = ((), (), s32[]{:S(2)}) async-start(), calls=%async_computation.28 | async-start | bytes 14155776 | tf_op jit(solution)/shard_map/psum | solution.py:344
  977.6 1118.1 %copy-start.17 = (bf16[64,10752]{1,0:T(8,128)(2,1)}, bf16[64,10752]{1,0:T(8,128)(2,1)S(1)}, u32[]{:S(2)}) copy-start(bf16[64,10752]{1,0:T(8,128)(2,1)S(1)} %reshape.839) | copy-start | bytes 4128772
  2053.2 34.3 %copy-start.77 = (f32[64,768]{1,0:T(8,128)S(1)}, f32[64,768]{1,0:T(8,128)}, u32[]{:S(2)}) copy-start(f32[64,768]{1,0:T(8,128)} %copy-done.76) | copy-start | bytes 589828
  2053.2 34.4 %copy-start.120 = (s32[64]{0:T(128)S(1)}, s32[64]{0:T(128)}, u32[]{:S(2)}) copy-start(s32[64]{0:T(128)} %copy-done.119) | copy-start | bytes 772
  2053.2 35.4 %copy-start.67 = (bf16[768,768]{1,0:T(8,128)(2,1)S(1)}, bf16[768,768]{1,0:T(8,128)(2,1)}, u32[]{:S(2)}) copy-start(bf16[768,768]{1,0:T(8,128)(2,1)} %copy-done.66) | copy-start | bytes 3538948
  2053.2 35.4 %copy-start.75 = (f32[64,768]{1,0:T(8,128)S(1)}, f32[64,768]{1,0:T(8,128)}, u32[]{:S(2)}) copy-start(f32[64,768]{1,0:T(8,128)} %copy-done.74) | copy-start | bytes 589828
  2053.3 214.4 %all-reduce.9.cloned.1.call-start = ((), (), s32[]{:S(2)}) async-start(), calls=%async_computation.17 | async-start | bytes 401408 | tf_op jit(solution)/shard_map/psum | solution.py:418
  2056.4 32.7 %copy-start.80 = (bf16[64,128]{1,0:T(8,128)(2,1)S(1)}, bf16[64,128]{1,0:T(8,128)(2,1)}, u32[]{:S(2)}) copy-start(bf16[64,128]{1,0:T(8,128)(2,1)} %copy-done.79) | copy-start | bytes 49156
  2056.4 32.7 %copy-start.82 = (bf16[64,128]{1,0:T(8,128)(2,1)S(1)}, bf16[64,128]{1,0:T(8,128)(2,1)}, u32[]{:S(2)}) copy-start(bf16[64,128]{1,0:T(8,128)(2,1)} %copy-done.81) | copy-start | bytes 49156
  2124.9 7.2 copy-start.15
  2124.9 7.8 copy-start.85
  2135.7 52.0 %copy-start.109 = (f32[96]{0:T(128)}, f32[96]{0:T(128)S(1)}, u32[]{:S(2)}) copy-start(f32[96]{0:T(128)S(1)} %get-tuple-element.289) | copy-start | bytes 1156
  2197.4 93.1 %copy-start.65 = (f32[2,96,768]{2,1,0:T(8,128)S(1)}, f32[2,96,768]{2,1,0:T(8,128)}, u32[]{:S(2)}) copy-start(f32[2,96,768]{2,1,0:T(8,128)} %param.30) | copy-start | bytes 1769476
  2274.2 18.3 copy-start.107
  2285.8 6.7 copy-start.16
  2286.8 9.5 copy-start.92
  2287.6 8.6 copy-start.93
  2288.5 7.7 copy-start.86
  2289.5 9.3 copy-start.83
  2296.3 6.3 copy-start.78
  (109 other events, 287.6 us)
Sparse Core Ops, SparseCore 0:
  67.1 69.7 all-reduce.10
  139.9 64.1 all-gather.20
  207.1 39.5 all-gather.22
  249.5 78.6 all-gather.24
  331.1 78.0 all-gather.26
  412.0 63.3 all-gather.28
  478.3 39.5 all-gather.30
  520.9 78.6 all-gather.32
  602.6 78.0 all-gather.34
  796.2 119.2 all-reduce.6
  919.4 56.5 all-gather.36
  980.3 67.8 reduce-scatter.14
  1052.7 68.1 reduce-scatter.12
  1124.9 128.0 reduce-scatter.10
  1256.5 128.0 reduce-scatter.8
  1388.5 162.3 reduce-scatter.22
  1554.7 162.3 reduce-scatter.20
  1721.0 162.3 reduce-scatter.16
  1887.5 162.4 reduce-scatter.18
  2053.7 132.0 all-reduce.12
  2197.5 70.0 all-reduce.8

commit v2 on v1

--- a/solution.py
+++ b/solution.py
@@ -4,6 +4,8 @@
 import jax
 import jax.numpy as jnp
 from jax import lax
+from jax.experimental import pallas as pl
+from jax.experimental.pallas import tpu as pltpu
 from jax.sharding import PartitionSpec as P
 
 D = 768
@@ -226,6 +228,514 @@
     return (grad_in, (grad_qkv, grad_proj, grad_fc1, grad_fc2), grad_bias, grad_spans)
 
 
+MESH_IDS = pl.DeviceIdType.MESH
+Z_SIZE, Y_SIZE, X_SIZE, C_SIZE = 4, 2, 2, 2
+LANES = 128
+
+
+def place():
+    dp, rep = lax.axis_index("dp"), lax.axis_index("rep")
+    return (dp // Y_SIZE, dp % Y_SIZE, rep // C_SIZE, rep % C_SIZE)
+
+
+def device(z, y, x, c):
+    return (z * Y_SIZE + y, x * C_SIZE + c)
+
+
+def meet(peers):
+    barrier = pltpu.get_barrier_semaphore()
+    for peer in peers:
+        pl.semaphore_signal(barrier, inc=1, device_id=peer, device_id_type=MESH_IDS)
+    pl.semaphore_wait(barrier, len(peers))
+
+
+def push(source, target, send, receive, peer):
+    return pltpu.make_async_remote_copy(
+        src_ref=source,
+        dst_ref=target,
+        send_sem=send,
+        recv_sem=receive,
+        device_id=peer,
+        device_id_type=MESH_IDS,
+    )
+
+
+def ids_kernel(own, full, send, receive, local):
+    dp, rep = lax.axis_index("dp"), lax.axis_index("rep")
+    dps, reps = Z_SIZE * Y_SIZE, X_SIZE * C_SIZE
+    offsets = [(i, j) for i in range(dps) for j in range(reps) if i or j]
+    peers = [((dp + i) % dps, (rep + j) % reps) for i, j in offsets]
+    meet(peers)
+    mine = dp * reps + rep
+    copies = [
+        push(own, full.at[mine], send.at[n], receive.at[n], peer) for n, peer in enumerate(peers)
+    ]
+    for copy in copies:
+        copy.start()
+    keep = pltpu.make_async_copy(own, full.at[mine], local)
+    keep.start()
+    keep.wait()
+    for copy in copies:
+        copy.wait()
+
+
+def gather_ids(own):
+    count = Z_SIZE * Y_SIZE * X_SIZE * C_SIZE
+    return pl.pallas_call(
+        ids_kernel,
+        out_shape=jax.ShapeDtypeStruct((count,) + own.shape, own.dtype),
+        in_specs=[pl.BlockSpec(memory_space=pltpu.VMEM)],
+        out_specs=pl.BlockSpec(memory_space=pltpu.VMEM),
+        scratch_shapes=[
+            pltpu.SemaphoreType.DMA((count - 1,)),
+            pltpu.SemaphoreType.DMA((count - 1,)),
+            pltpu.SemaphoreType.DMA,
+        ],
+        compiler_params=pltpu.CompilerParams(collective_id=1, has_side_effects=True),
+        name="gather_ids",
+    )(own)
+
+
+def gather_kernel(groups, packed, parts, full, summed, part_in, z_s, z_r, y_s, y_r, x_s, x_r, c_s, c_r, p_s, p_r, local):
+    z, y, x, c = place()
+    dp = z * Y_SIZE + y
+    dps = Z_SIZE * Y_SIZE
+    part_peers = [((dp + k) % dps, x * C_SIZE + c) for k in range(1, dps)]
+    across_y, across_x, sibling = device(z, 1 - y, x, c), device(z, y, 1 - x, c), device(z, y, x, 1 - c)
+    meet(part_peers + [across_x, sibling])
+    part_copies = [
+        push(parts.at[peer[0]], part_in.at[dp], p_s.at[k], p_r.at[k], peer)
+        for k, peer in enumerate(part_peers)
+    ]
+    for copy in part_copies:
+        copy.start()
+    keeps = []
+    for layer in range(LAYERS):
+        keep = pltpu.make_async_copy(packed.at[layer], full.at[layer, dp], local.at[layer])
+        keep.start()
+        keeps.append(keep)
+    started = []
+
+    def rows(group, third, count):
+        layer, first, size = groups[group]
+        step = size // 6
+        return pl.ds(pl.multiple_of(first + c * 3 * step + third * step, 16), count * step)
+
+    def source(k, other):
+        return ((z - k) % Z_SIZE) * Y_SIZE + (1 - y if other else y)
+
+    def piece(group, owner, third, count):
+        return full.at[groups[group][0], owner, rows(group, third, count)]
+
+    def go(source_ref, target_ref, send, receive, peer):
+        copy = push(source_ref, target_ref, send, receive, peer)
+        copy.start()
+        started.append(copy)
+
+    def first_hop(group):
+        own = packed.at[groups[group][0], rows(group, x, 2)]
+        target = piece(group, dp, x, 2)
+        go(own, target, y_s.at[group, 0], y_r.at[group, 0], across_y)
+        for k in range(1, Z_SIZE):
+            peer = device((z + k) % Z_SIZE, y, x, c)
+            go(own, target, z_s.at[group, k - 1], z_r.at[group, k - 1], peer)
+
+    def arrive(ref, send, receive, peer):
+        push(ref, ref, send, receive, peer).wait_recv()
+
+    def spread(group, index, owner):
+        third = piece(group, owner, 2 * x, 1)
+        go(third, third, x_s.at[group, index], x_r.at[group, index], across_x)
+        both = piece(group, owner, x, 2)
+        go(both, both, c_s.at[group, index], c_r.at[group, index], sibling)
+
+    def on_z(group, k):
+        ref = piece(group, source(k, False), x, 2)
+        arrive(ref, z_s.at[group, k - 1], z_r.at[group, k - 1], across_y)
+        go(ref, ref, y_s.at[group, k], y_r.at[group, k], across_y)
+        spread(group, k - 1, source(k, False))
+
+    def on_y(group, k):
+        ref = piece(group, source(k, True), x, 2)
+        arrive(ref, y_s.at[group, k], y_r.at[group, k], across_y)
+        spread(group, Z_SIZE - 1 + k, source(k, True))
+
+    def on_x(group, index):
+        owner = source(index + 1, False) if index < Z_SIZE - 1 else source(index - Z_SIZE + 1, True)
+        ref = piece(group, owner, 2 - 2 * x, 1)
+        arrive(ref, x_s.at[group, index], x_r.at[group, index], across_x)
+        slot = index + 2 * Z_SIZE - 1
+        go(ref, ref, c_s.at[group, slot], c_r.at[group, slot], sibling)
+
+    def on_c(group):
+        layer, first, size = groups[group]
+        step = size // 6
+        other = 1 - c
+        for index in range(2 * Z_SIZE - 1):
+            owner = source(index + 1, False) if index < Z_SIZE - 1 else source(index - Z_SIZE + 1, True)
+            for slot, third, count in ((index, x, 2), (index + 2 * Z_SIZE - 1, 2 - 2 * x, 1)):
+                start = pl.multiple_of(first + other * 3 * step + third * step, 16)
+                ref = full.at[layer, owner, pl.ds(start, count * step)]
+                arrive(ref, c_s.at[group, slot], c_r.at[group, slot], sibling)
+
+    first_hop(0)
+    count = len(groups)
+    for group in range(count + 1):
+        if group + 1 < count:
+            first_hop(group + 1)
+        events = []
+        if group < count:
+            events = [(on_y, group, 0)]
+            for k in range(1, Z_SIZE):
+                events += [(on_z, group, k), (on_y, group, k)]
+        for index in range(2 * Z_SIZE - 1):
+            if events:
+                step, *where = events[index]
+                step(*where)
+            if group > 0:
+                on_x(group - 1, index)
+        if group == 0:
+            for copy in part_copies:
+                copy.wait()
+            total = jnp.where(dp == 0, parts[0], part_in[0])
+            for k in range(1, dps):
+                total = total + jnp.where(dp == k, parts[k], part_in[k])
+            summed[...] = total
+    for group in range(count):
+        on_c(group)
+    for copy in started:
+        copy.wait_send()
+    for keep in keeps:
+        keep.wait()
+
+
+def gather_weights(packed, parts, groups):
+    layers, height, width = packed.shape
+    dps = Z_SIZE * Y_SIZE
+    count = len(groups)
+    dma = pltpu.SemaphoreType.DMA
+    return pl.pallas_call(
+        partial(gather_kernel, groups),
+        out_shape=(
+            jax.ShapeDtypeStruct((layers, dps, height, width), packed.dtype),
+            jax.ShapeDtypeStruct(parts.shape[1:], parts.dtype),
+        ),
+        in_specs=[pl.BlockSpec(memory_space=pl.ANY), pl.BlockSpec(memory_space=pltpu.VMEM)],
+        out_specs=(pl.BlockSpec(memory_space=pl.ANY), pl.BlockSpec(memory_space=pltpu.VMEM)),
+        scratch_shapes=[
+            pltpu.VMEM(parts.shape, parts.dtype),
+            dma((count, Z_SIZE - 1)),
+            dma((count, Z_SIZE - 1)),
+            dma((count, Z_SIZE)),
+            dma((count, Z_SIZE)),
+            dma((count, 2 * Z_SIZE - 1)),
+            dma((count, 2 * Z_SIZE - 1)),
+            dma((count, 4 * Z_SIZE - 2)),
+            dma((count, 4 * Z_SIZE - 2)),
+            dma((dps - 1,)),
+            dma((dps - 1,)),
+            dma((layers,)),
+        ],
+        compiler_params=pltpu.CompilerParams(
+            collective_id=2, has_side_effects=True, vmem_limit_bytes=16 * 2**20
+        ),
+        name="gather_weights",
+    )(packed, parts)
+
+
+def scatter_kernel(
+    groups, grads, mods, smalls, finals, mods_all, small_out,
+    held, from_c, from_x, from_y, from_z, to_x, from_fin, small_c, small_x, small_y, small_z,
+    c_s, c_r, x_s, x_r, y_s, y_r, z_s, z_r, e_s, e_r, f_s, f_r, m_s, m_r, v_s, v_r, local,
+):
+    z, y, x, c = place()
+    dps = Z_SIZE * Y_SIZE
+    z_peers = [device((z + k) % Z_SIZE, y, x, c) for k in range(1, Z_SIZE)]
+    across_y, across_x, sibling = device(z, 1 - y, x, c), device(z, y, 1 - x, c), device(z, y, x, 1 - c)
+    count = len(groups)
+    meet(z_peers + [across_y, across_x, sibling])
+    started = []
+
+    def go(source_ref, target_ref, send, receive, peer):
+        copy = push(source_ref, target_ref, send, receive, peer)
+        copy.start()
+        started.append(copy)
+
+    def arrive(ref, send, receive, peer):
+        push(ref, ref, send, receive, peer).wait_recv()
+
+    sizes = [size // 2 for _, _, size in groups]
+    starts = [sum(sizes[:g]) for g in range(count)]
+
+    def half(group):
+        return pl.ds(starts[group], sizes[group])
+
+    def two(group):
+        step = sizes[group] // 3
+        return pl.ds(pl.multiple_of(starts[group] + x * step, 16), 2 * step)
+
+    def tight(group):
+        return pl.ds(starts[group] // 3 * 2, sizes[group] // 3 * 2)
+
+    def third(group):
+        return pl.ds(starts[group] // 3, sizes[group] // 3)
+
+    def begin(group):
+        layer, first, size = groups[group]
+        theirs = pl.ds(pl.multiple_of(first + (1 - c) * (size // 2), 16), size // 2)
+        ours = pl.ds(pl.multiple_of(first + c * (size // 2), 16), size // 2)
+        for j in range(Y_SIZE):
+            side = y if j else 1 - y
+            go(grads.at[layer, :, side, theirs], from_c.at[:, side, half(group)], c_s.at[group, j], c_r.at[group, j], sibling)
+            pltpu.make_async_copy(grads.at[layer, :, side, ours], held.at[:, side, half(group)], local.at[group, j]).start()
+
+    def add(target, extra, send=None):
+        def body(owner, carry):
+            total = target[owner].astype(jnp.float32) + extra[owner].astype(jnp.float32)
+            total = total.astype(jnp.bfloat16)
+            if send is None:
+                target[owner] = total
+            else:
+                send[owner] = total
+            return carry
+        lax.fori_loop(0, Z_SIZE, body, 0)
+
+    def on_c(group):
+        layer, first, size = groups[group]
+        step = sizes[group] // 3
+        theirs = pl.ds(pl.multiple_of(starts[group] + (2 - 2 * x) * step, 16), step)
+        for j in range(Y_SIZE):
+            side = y if j else 1 - y
+            mine = held.at[:, side, half(group)]
+            pltpu.make_async_copy(mine, mine, local.at[group, j]).wait()
+            arrive(mine, c_s.at[group, j], c_r.at[group, j], sibling)
+            add(held.at[:, side, theirs], from_c.at[:, side, theirs], to_x.at[:, side, third(group)])
+            go(to_x.at[:, side, third(group)], from_x.at[:, side, third(group)], x_s.at[group, j], x_r.at[group, j], across_x)
+            add(held.at[:, side, two(group)], from_c.at[:, side, two(group)])
+
+    def on_x(group):
+        step = sizes[group] // 3
+        ours = pl.ds(pl.multiple_of(starts[group] + 2 * x * step, 16), step)
+        for j in range(Y_SIZE):
+            side = y if j else 1 - y
+            got = from_x.at[:, side, third(group)]
+            arrive(got, x_s.at[group, j], x_r.at[group, j], across_x)
+            add(held.at[:, side, ours], got)
+            if j == 0:
+                go(held.at[:, side, two(group)], from_y.at[:, tight(group)], y_s.at[group], y_r.at[group], across_y)
+
+    def on_y(group):
+        got = from_y.at[:, tight(group)]
+        arrive(got, y_s.at[group], y_r.at[group], across_y)
+        add(held.at[:, y, two(group)], got)
+        for k in range(1, Z_SIZE):
+            go(
+                held.at[(z + k) % Z_SIZE, y, two(group)], from_z.at[k - 1, tight(group)],
+                z_s.at[group, k - 1], z_r.at[group, k - 1], z_peers[k - 1],
+            )
+
+    def on_z(group):
+        total = held[z, y, two(group)].astype(jnp.float32)
+        for k in range(1, Z_SIZE):
+            arrive(from_z.at[k - 1, tight(group)], z_s.at[group, k - 1], z_r.at[group, k - 1], across_y)
+            total = total + from_z[k - 1, tight(group)].astype(jnp.float32)
+        held[z, y, two(group)] = total.astype(jnp.bfloat16)
+        go(held.at[z, y, two(group)], from_fin.at[tight(group)], e_s.at[group], e_r.at[group], across_x)
+
+    def on_fin(group):
+        layer, first, size = groups[group]
+        step = sizes[group] // 3
+        arrive(from_fin.at[tight(group)], e_s.at[group], e_r.at[group], across_x)
+        base = pl.multiple_of(starts[group] // 3 * 2, 16)
+        out = pl.multiple_of(first + c * (size // 2), 16)
+        mine = pl.multiple_of(starts[group] + 2 * x * step, 16)
+        middle = starts[group] + step
+        finals[layer, pl.ds(pl.multiple_of(out + 2 * x * step, 16), step)] = held[z, y, pl.ds(mine, step)].astype(jnp.float32)
+        finals[layer, pl.ds(pl.multiple_of(out + (2 - 2 * x) * step, 16), step)] = from_fin[
+            pl.ds(pl.multiple_of(base + (1 - x) * step, 16), step)
+        ].astype(jnp.float32)
+        finals[layer, pl.ds(pl.multiple_of(out + step, 16), step)] = held[z, y, pl.ds(middle, step)].astype(
+            jnp.float32
+        ) + from_fin[pl.ds(pl.multiple_of(base + x * step, 16), step)].astype(jnp.float32)
+        ref = finals.at[layer, pl.ds(out, size // 2)]
+        go(ref, ref, f_s.at[group], f_r.at[group], sibling)
+
+    def on_last(group):
+        layer, first, size = groups[group]
+        ref = finals.at[layer, pl.ds(pl.multiple_of(first + (1 - c) * (size // 2), 16), size // 2)]
+        arrive(ref, f_s.at[group], f_r.at[group], sibling)
+
+    slot = x * C_SIZE + c
+
+    def mods_first():
+        keep = pltpu.make_async_copy(mods, mods_all.at[z, y, slot], local.at[count, 0])
+        keep.start()
+        keep.wait()
+        own = mods_all.at[z, y, slot]
+        for k in range(1, Z_SIZE):
+            go(own, own, m_s.at[k - 1], m_r.at[k - 1], z_peers[k - 1])
+
+    def mods_y():
+        for k in range(1, Z_SIZE):
+            arrive(mods_all.at[(z - k) % Z_SIZE, y, slot], m_s.at[k - 1], m_r.at[k - 1], across_y)
+        ref = mods_all.at[:, y, slot]
+        go(ref, ref, m_s.at[3], m_r.at[3], across_y)
+
+    def mods_x():
+        arrive(mods_all.at[:, 1 - y, slot], m_s.at[3], m_r.at[3], across_y)
+        ref = mods_all.at[:, :, slot]
+        go(ref, ref, m_s.at[4], m_r.at[4], across_x)
+
+    def mods_c():
+        arrive(mods_all.at[:, :, (1 - x) * C_SIZE + c], m_s.at[4], m_r.at[4], across_x)
+        for k in range(X_SIZE):
+            ref = mods_all.at[:, :, k * C_SIZE + c]
+            go(ref, ref, m_s.at[5 + k], m_r.at[5 + k], sibling)
+
+    def mods_end():
+        for k in range(X_SIZE):
+            arrive(mods_all.at[:, :, k * C_SIZE + 1 - c], m_s.at[5 + k], m_r.at[5 + k], sibling)
+
+    span = small_c.shape[0]
+    mine_v = pl.ds(pl.multiple_of(c * span, 8), span)
+    other_v = pl.ds(pl.multiple_of((1 - c) * span, 8), span)
+
+    def small_first():
+        go(smalls.at[other_v], small_c, v_s.at[0], v_r.at[0], sibling)
+
+    def small_to_x():
+        arrive(small_c, v_s.at[0], v_r.at[0], sibling)
+        small_c[...] = small_c[...] + smalls[mine_v]
+        go(small_c, small_x, v_s.at[1], v_r.at[1], across_x)
+
+    def small_to_y():
+        arrive(small_x, v_s.at[1], v_r.at[1], across_x)
+        small_x[...] = small_x[...] + small_c[...]
+        go(small_x, small_y, v_s.at[2], v_r.at[2], across_y)
+
+    def small_to_z():
+        arrive(small_y, v_s.at[2], v_r.at[2], across_y)
+        small_z[z] = small_y[...] + small_x[...]
+        for k in range(1, Z_SIZE):
+            go(small_z.at[z], small_z.at[z], v_s.at[2 + k], v_r.at[2 + k], z_peers[k - 1])
+
+    def small_to_c():
+        for k in range(1, Z_SIZE):
+            arrive(small_z.at[(z - k) % Z_SIZE], v_s.at[2 + k], v_r.at[2 + k], across_y)
+        small_out[mine_v] = (small_z[0] + small_z[1]) + (small_z[2] + small_z[3])
+        go(small_out.at[mine_v], small_out.at[mine_v], v_s.at[6], v_r.at[6], sibling)
+
+    def small_end():
+        arrive(small_out.at[other_v], v_s.at[6], v_r.at[6], sibling)
+
+    extra = [
+        [small_first, mods_first], [small_to_x, mods_y], [small_to_y, mods_x], [small_to_z, mods_c],
+        [small_to_c, mods_end], [small_end],
+    ]
+    for group in range(count):
+        begin(group)
+    stages = [on_c, on_x, on_y, on_z, on_fin, on_last]
+    for step in range(max(count + len(stages) - 1, len(extra))):
+        for index, stage in enumerate(stages):
+            if 0 <= step - index < count:
+                stage(step - index)
+        if step < len(extra):
+            for stage in extra[step]:
+                stage()
+    for copy in started:
+        copy.wait_send()
+
+
+def scatter_grads(grads, mods, smalls, groups):
+    layers, owners, height, width = grads.shape
+    grads = grads.reshape(layers, Z_SIZE, Y_SIZE, height, width)
+    rows = sum(size for _, _, size in groups) // 2
+    count = len(groups)
+    dma = pltpu.SemaphoreType.DMA
+    low, wide = jnp.bfloat16, jnp.float32
+    span = smalls.shape[0] // 2
+    vmem = pl.BlockSpec(memory_space=pltpu.VMEM)
+    finals, mods_all, small_out = pl.pallas_call(
+        partial(scatter_kernel, groups),
+        out_shape=(
+            jax.ShapeDtypeStruct((layers, height, width), wide),
+            jax.ShapeDtypeStruct((Z_SIZE, Y_SIZE, X_SIZE * C_SIZE) + mods.shape, mods.dtype),
+            jax.ShapeDtypeStruct(smalls.shape, wide),
+        ),
+        in_specs=[pl.BlockSpec(memory_space=pl.ANY), vmem, vmem],
+        out_specs=(vmem, vmem, vmem),
+        scratch_shapes=[
+            pltpu.VMEM((Z_SIZE, Y_SIZE, rows, width), low),
+            pltpu.VMEM((Z_SIZE, Y_SIZE, rows, width), low),
+            pltpu.VMEM((Z_SIZE, Y_SIZE, rows // 3, width), low),
+            pltpu.VMEM((Z_SIZE, rows // 3 * 2, width), low),
+            pltpu.VMEM((Z_SIZE - 1, rows // 3 * 2, width), low),
+            pltpu.VMEM((Z_SIZE, Y_SIZE, rows // 3, width), low),
+            pltpu.VMEM((rows // 3 * 2, width), low),
+            pltpu.VMEM((span, LANES), wide),
+            pltpu.VMEM((span, LANES), wide),
+            pltpu.VMEM((span, LANES), wide),
+            pltpu.VMEM((Z_SIZE, span, LANES), wide),
+            dma((count, 2)), dma((count, 2)),
+            dma((count, 2)), dma((count, 2)),
+            dma((count,)), dma((count,)),
+            dma((count, Z_SIZE - 1)), dma((count, Z_SIZE - 1)),
+            dma((count,)), dma((count,)),
+            dma((count,)), dma((count,)),
+            dma((7,)), dma((7,)),
+            dma((7,)), dma((7,)),
+            dma((count + 1, 2)),
+        ],
+        compiler_params=pltpu.CompilerParams(
+            collective_id=3, has_side_effects=True, vmem_limit_bytes=62 * 2**20
+        ),
+        name="scatter_grads",
+    )(grads, mods, smalls)
+    return finals, mods_all, small_out
+
+
+def pack_shard(w_qkv, w_proj, w_fc1, w_fc2):
+    pieces = [w_qkv[:, D * i : D * (i + 1)] for i in range(3)] + [w_proj]
+    pieces += [w_fc1[:, D * i : D * (i + 1)] for i in range(FF // D)] + [w_fc2]
+    return jnp.concatenate(pieces, axis=0).astype(jnp.bfloat16)
+
+
+def square(full, index):
+    rows = D // full.shape[0]
+    return full[:, rows * index : rows * (index + 1)].reshape(D, D)
+
+
+def unpack_full(full):
+    rows = D // full.shape[0]
+    count = FF // D
+    return (
+        jnp.concatenate([square(full, i) for i in range(3)], axis=1),
+        square(full, 3),
+        jnp.concatenate([square(full, 4 + i) for i in range(count)], axis=1),
+        full[:, rows * (4 + count) :].reshape(FF, D),
+    )
+
+
+def pack_grads(grads, owners):
+    def split(block):
+        return block.astype(jnp.bfloat16).reshape(owners, -1, D)
+
+    pieces = [split(grads[0][:, D * i : D * (i + 1)]) for i in range(3)] + [split(grads[1])]
+    pieces += [split(grads[2][:, D * i : D * (i + 1)]) for i in range(FF // D)] + [split(grads[3])]
+    return jnp.concatenate(pieces, axis=1)
+
+
+def unpack_shard(packed, rows):
+    count = FF // D
+    blocks = [packed[:, rows * i : rows * (i + 1)] for i in range(4 + count)]
+    return (
+        jnp.concatenate(blocks[:3], axis=-1),
+        blocks[3],
+        jnp.concatenate(blocks[4:], axis=-1),
+        packed[:, rows * (4 + count) :],
+    )
+
+
 def local(
     latents,
     noise_field,
@@ -266,7 +776,12 @@
     mod_shard = w_mod.astype(jnp.bfloat16)
 
     own_ids = jnp.stack([timesteps, labels, drop_mask]).reshape(3, number)
-    all_ids = lax.all_gather(own_ids, ("dp", "rep"), axis=0, tiled=False)
+    direct = (dp_size, rep_size) == (Z_SIZE * Y_SIZE, X_SIZE * C_SIZE) and rows_mod % 96 == 0
+    if direct:
+        tile = jnp.pad(own_ids, ((0, 8 - 3), (0, LANES - number))).astype(jnp.float32)
+        all_ids = gather_ids(tile)[:, :3, :number].astype(jnp.int32)
+    else:
+        all_ids = lax.all_gather(own_ids, ("dp", "rep"), axis=0, tiled=False)
     all_ids = all_ids.transpose(1, 0, 2).reshape(3, everyone * number)
     features = time_features(all_ids[0]).astype(jnp.bfloat16)
     hidden_t = product(features, time1_low) + pieces["time1_b"]
@@ -286,10 +801,19 @@
         axis=1,
         keepdims=False,
     ).reshape(dp_size * number, rows_mod)
-    modulation = (
-        lax.psum_scatter(product(group_rows, mod_shard), "dp", scatter_dimension=0, tiled=True)
-        + pieces["mod_b"]
-    )
+    mod_part = product(group_rows, mod_shard)
+    if direct:
+        packed = jnp.stack(
+            [pack_shard(w_qkv[i], w_proj[i], w_fc1[i], w_fc2[i]) for i in range(LAYERS)]
+        )
+        heights = [(0, 384), (384, 384), (768, 384)]
+        groups = [(i, first, size) for i in range(LAYERS) for first, size in heights]
+        mod_part = mod_part.reshape(dp_size, -1, LANES)
+        packed_full, mod_sum = gather_weights(packed, mod_part, groups)
+        mod_sum = mod_sum.reshape(number, MOD)
+    else:
+        mod_sum = lax.psum_scatter(mod_part, "dp", scatter_dimension=0, tiled=True)
+    modulation = mod_sum + pieces["mod_b"]
 
     picker = (timesteps.reshape(-1)[:, None] == jnp.arange(STEPS_T)[None, :]).astype(jnp.float32)
     factors = jnp.dot(picker, roster.T, precision=HIGHEST)
@@ -304,10 +828,13 @@
     gathered_all = []
     spans_all = []
     for layer_index in range(LAYERS):
-        weights = tuple(
-            lax.all_gather(w[layer_index].astype(jnp.bfloat16), "dp", axis=0, tiled=True)
-            for w in (w_qkv, w_proj, w_fc1, w_fc2)
-        )
+        if direct:
+            weights = unpack_full(packed_full[layer_index])
+        else:
+            weights = tuple(
+                lax.all_gather(w[layer_index].astype(jnp.bfloat16), "dp", axis=0, tiled=True)
+                for w in (w_qkv, w_proj, w_fc1, w_fc2)
+            )
         spans = [
             modulation[:, None, D * (6 * layer_index + i) : D * (6 * layer_index + i + 1)]
             for i in range(6)
@@ -338,15 +865,43 @@
         )
         layer_spans[layer_index] = grad_spans
         bias_grads[layer_index] = grad_bias
-        block_grads[layer_index] = tuple(
-            lax.psum_scatter(g, "dp", scatter_dimension=0, tiled=True) for g in grads
+        if direct:
+            block_grads[layer_index] = pack_grads(grads, dp_size)
+        else:
+            block_grads[layer_index] = tuple(
+                lax.psum_scatter(g, "dp", scatter_dimension=0, tiled=True) for g in grads
+            )
+
+    grad_start = grad_res.reshape(-1, D).astype(jnp.bfloat16)
+    grad_patch = product(tokens.reshape(-1, PDIM).T, grad_start)
+    grad_patch_b = jnp.sum(grad_start.astype(jnp.float32), axis=0)
+    own_sums = jnp.concatenate(
+        [
+            grad_patch.reshape(-1),
+            grad_patch_b,
+            grad_head.reshape(-1),
+            jnp.stack(bias_grads).reshape(-1),
+            grad_head_b,
+            loss_own[None],
+        ]
+    )
+    own_mod = jnp.concatenate(layer_spans + final_grads, axis=-1).astype(jnp.bfloat16)
+    if direct:
+        order = [(i, first, size) for i in reversed(range(LAYERS)) for first, size in heights[::-1]]
+        mod_rows = number * MOD // LANES
+        mod_tile = jnp.pad(own_mod.reshape(mod_rows, LANES), ((0, -mod_rows % 16), (0, 0)))
+        sum_tile = jnp.pad(own_sums, (0, -own_sums.size % (16 * LANES))).reshape(-1, LANES)
+        finals, mod_all, sum_all = scatter_grads(jnp.stack(block_grads), mod_tile, sum_tile, order)
+        grad_qkv, grad_proj, grad_fc1, grad_fc2 = unpack_shard(finals, rows_mod)
+        grad_mod = mod_all.reshape(everyone, -1, LANES)[:, :mod_rows].reshape(-1, MOD)
+        summed = sum_all.reshape(-1)
+    else:
+        grad_qkv, grad_proj, grad_fc1, grad_fc2 = lax.psum(
+            tuple(jnp.stack([block_grads[i][k] for i in range(LAYERS)]) for k in range(4)), "rep"
         )
-    grad_qkv, grad_proj, grad_fc1, grad_fc2 = lax.psum(
-        tuple(jnp.stack([block_grads[i][k] for i in range(LAYERS)]) for k in range(4)), "rep"
-    )
-
-    own_mod = jnp.concatenate(layer_spans + final_grads, axis=-1).astype(jnp.bfloat16)
-    grad_mod = lax.all_gather(own_mod, ("dp", "rep"), axis=0, tiled=True)
+        grad_mod = lax.all_gather(own_mod, ("dp", "rep"), axis=0, tiled=True)
+        summed = lax.psum(own_sums, ("dp", "rep"))
+
     grad_wmod = product(silu_rows.T, grad_mod)
     grad_mod_b = jnp.sum(grad_mod.astype(jnp.float32), axis=0)
     cond_rows = lax.all_gather(product(grad_mod, mod_shard.T), "dp", axis=1, tiled=True)
@@ -359,22 +914,6 @@
     grad_hidden_t = silu_time_pull(product(grad_cond, time2_low.T))[0].astype(jnp.bfloat16)
     grad_time1 = product(features.T, grad_hidden_t)
     grad_time1_b = jnp.sum(grad_hidden_t.astype(jnp.float32), axis=0)
-    grad_start = grad_res.reshape(-1, D).astype(jnp.bfloat16)
-    grad_patch = product(tokens.reshape(-1, PDIM).T, grad_start)
-    grad_patch_b = jnp.sum(grad_start.astype(jnp.float32), axis=0)
-    summed = lax.psum(
-        jnp.concatenate(
-            [
-                grad_patch.reshape(-1),
-                grad_patch_b,
-                grad_head.reshape(-1),
-                jnp.stack(bias_grads).reshape(-1),
-                grad_head_b,
-                loss_own[None],
-            ]
-        ),
-        ("dp", "rep"),
-    )
     cut_patch = (PDIM + 1) * D
     cut_head = cut_patch + D * PDIM
     cut_bias = cut_head + LAYERS * (4 * D + FF)

time: 2330 us -> 908 us (0.39)
  waiting for transfers between devices: 1770 us -> 0.02 us
  Pallas kernels: 0 us -> 350 us
  local copies, waits for them, and re-layouts: 155 us -> 211 us
  blocking collectives: 74.2 us -> 33 us
  matrix products: 184 us -> 145 us
    reduce_scatter x8 -> x0, waiting for transfers between devices: 1060 us -> none  [local(): lax.psum_scatter(g, 'dp', scatter_dimension=0, tiled=True)]
    all_gather x9 -> x0, waiting for transfers between devices: 498 us -> none  [the longest x8 441 us: local(): lax.all_gather(w[layer_index].astype(jnp.bfloat16), 'dp', axis=0, tiled=T...]
    pallas_call x0 -> x3, Pallas kernels: none -> 350 us  [the longest x1 176 us: scatter_grads(): pl.pallas_call(partial(scatter_kernel, groups), out_shape=(jax.ShapeDtype...]
    psum x2 -> x0, waiting for transfers between devices: 98.1 us -> none  [the longest x1 50.1 us: local(): lax.psum(jnp.concatenate([grad_patch.reshape(-1), grad_patch_b, grad_head...]
    psum x1, waiting for transfers between devices: 63.1 us -> 0.01 us  [local(): lax.psum(jnp.concatenate([entry[k].reshape(-1) for k in range(1, 5) for e...]
    unnamed x22 -> x1, waiting for transfers between devices: 44.9 us -> 0.02 us
    dot_general x37, matrix products: 157 us -> 113 us  [product(): return jnp.dot(left, right, preferred_element_type=jnp.float32)]
    all_gather x1 -> x0, blocking collectives: 43.4 us -> none  [local(): all_ids = lax.all_gather(own_ids, ('dp', 'rep'), axis=0, tiled=False)]
  transfers between devices with their start and end apart: 21 -> 1, of which waited for: 21 -> 0; matrix products, arithmetic and copies ran while one was open for 11% -> 6% of each run, Pallas kernels for 0% -> 0%
where the time goes in v2:
time: 908 us; the launch traced here: 896 us
  Pallas kernels  350 us (39%)
  local copies, waits for them, and re-layouts  211 us (23%)
  matrix products  145 us (16%)
  other arithmetic  136 us (15%)
  blocking collectives  33 us (4%)
  between operations  21.4 us (2%)
    pallas_call x1, Pallas kernels, scatter_grads(): pl.pallas_call(partial(scatter_kernel, groups), out_shape=(jax.ShapeDtype...  176 us
    pallas_call x1, Pallas kernels, gather_weights(): pl.pallas_call(partial(gather_kernel, groups), out_shape=(jax.ShapeDtypeS...  161 us
    dot_general x37, matrix products, product(): return jnp.dot(left, right, preferred_element_type=jnp.float32)  113 us
    unnamed x466, local copies, waits for them, and re-layouts  47.8 us
    all_gather x1, blocking collectives, local(): lax.all_gather(product(grad_mod, mod_shard.T), 'dp', axis=1, tiled=True)  33 us
    concatenate x1, local copies, waits for them, and re-layouts, local(): jnp.concatenate([summed[:cut_patch], grad_time1.reshape(-1), grad_time1_b...  29.1 us
    another operation x1, other arithmetic, local(): jnp.stack(block_grads)  19.3 us
  transfers between devices with their start and end apart: 1, of which 0 were waited for; matrix products, arithmetic and copies ran while one was open for 6% of the time, Pallas kernels for 0%

profile of v2, /device:TPU:0, one launch (start us, length us, event | category | flops | bytes accessed | tf_op | source)
XLA Modules:
  0.0 895.7 jit_solution(16057920252323996465)
XLA Ops:
  16.7 12.1 %gather_ids.1 = f32[32,8,128]{2,1,0:T(8,128)} custom-call(f32[8,128]{1,0:T(8,128)} %pad_convert_fusion.own), custom_call_target="tpu_custom_call" | custom-call | tf_op jit(solution)/shard_map/gather_ids/pallas_call | solution.py:284
  41.1 4.1 multiply_reduce_fusion.4
  49.4 2.6 multiply_reduce_fusion.30
  57.7 2.6 fusion.42
  62.5 161.2 %gather_weights.1 = (bf16[2,8,1152,768]{3,2,1,0:T(8,128)(2,1)S(1)}, f32[168,128]{1,0:T(8,128)S(1)}) custom-call(bf16[2,1152,768]{2,1,0:T(8,128)(2,1)S(1)} %pad_maximum_fusion.3.packed, f32[8,168,128]{2,1,0:T(8,128)S(1)} %reshape.1179.parts), custom_call_target="tpu_custom_call" | custom-call | tf_op jit(solution)/shard_map/gather_weights/pallas_call | solution.py:417
  223.8 9.3 %copy-done.2 = bf16[2,8,1152,768]{3,2,1,0:T(8,128)(2,1)} copy-done((bf16[2,8,1152,768]{3,2,1,0:T(8,128)(2,1)}, bf16[2,8,1152,768]{3,2,1,0:T(8,128)(2,1)S(1)}, u32[]{:S(2)}) %copy-start.2) | copy-done | bytes 28311576
  233.1 16.2 %slice_bitcast_fusion = (bf16[8,1152,768]{2,1,0:T(8,128)(2,1)}, bf16[8,1152,768]{2,1,0:T(8,128)(2,1)S(1)}) fusion(bf16[2,8,1152,768]{3,2,1,0:T(8,128)(2,1)} %copy-done.2), kind=kLoop, calls=%fused_computation.1 | loop fusion | bytes 56623104 | tf_op jit(solution)/shard_map/squeeze | solution.py:832
  249.3 4.9 slice.727
  254.2 7.0 fusion.161
  261.1 2.6 slice.709
  263.7 3.7 fusion.162
  281.9 3.9 fusion.14
  285.8 4.3 copy.117
  290.1 6.0 reshape.1184
  296.1 3.3 fusion.171
  304.5 2.6 fusion.159
  310.7 5.6 fusion.47
  316.5 5.4 fusion.157
  326.4 4.7 fusion.15
  331.1 4.3 copy.123
  335.4 6.2 reshape.1195
  341.6 2.9 fusion.170
  356.1 5.7 fusion.45
  361.9 5.8 fusion.153
  372.8 5.3 multiply_reduce_fusion.11
  379.8 6.5 convert_reduce_fusion
  386.4 5.5 convolution_convert_fusion
  392.0 3.8 fusion.36
  395.8 4.3 fusion.27
  404.1 4.3 convolution_convert_fusion.1
  410.7 3.1 reshape.1209
  413.8 4.4 convolution_bitcast_fusion.1
  418.2 7.2 multiply_reduce_fusion.1
  425.5 4.5 multiply_convert_fusion.1
  432.1 3.9 copy.147
  436.4 2.6 multiply_reduce_fusion.14
  441.4 6.6 convert_reduce_fusion.1
  448.0 5.5 convolution_convert_fusion.3
  453.5 3.9 fusion.35
  457.4 4.5 fusion.28
  465.9 4.4 convolution_convert_fusion.4
  472.6 3.3 reshape.1211
  475.9 4.4 convolution_bitcast_fusion
  480.4 7.2 multiply_reduce_fusion
  487.6 4.5 multiply_convert_fusion
  495.8 3.9 copy.146
  499.8 4.6 fusion.165
  506.8 3.2 convolution_convert_fusion.2
  514.8 3.6 copy.174
  518.5 4.3 multiply_reduce_fusion.10
  525.6 4.0 convolution_convert_fusion.5
  548.2 2.6 constant_dynamic-update-slice_fusion.9
  550.8 19.3 %pad_maximum_fusion.grads = bf16[2,4,2,1152,768]{4,3,2,1,0:T(8,128)(2,1)} fusion(bf16[1,4,2,1152,768]{4,3,2,1,0:T(8,128)(2,1)} %constant_dynamic-update-slice_fusion.9, bf16[1,4,2,1152,768]{4,3,2,1,0:T(8,128)(2,1)} %copy-done.18), kind=kLoop, calls=%fused_computation | loop fusion | flops 14155776 | bytes 56623104 | tf_op jit(solution)/shard_map/stack | solution.py:894
  570.1 176.3 %scatter_grads.1 = (f32[2,1152,768]{2,1,0:T(8,128)}, bf16[4,2,4,176,128]{4,3,2,1,0:T(8,128)(2,1)}, f32[304,128]{1,0:T(8,128)}) custom-call(bf16[2,4,2,1152,768]{4,3,2,1,0:T(8,128)(2,1)} %pad_maximum_fusion.grads, bf16[176,128]{1,0:T(8,128)(2,1)} %pad.13.mods, f32[304,128]{1,0:T(8,128)} %pad_bitcast_fusion.smalls), custom_call_target="tpu_custom_call" | custom-call | tf_op jit(solution)/shard_map/scatter_grads/pallas_call | solution.py:658
  746.3 3.3 add_reduce_fusion.2
  749.6 4.5 fusion.163
  755.8 3.2 add_reduce_fusion.4
  772.3 3.0 convolution_bitcast_fusion.2
  776.3 33.0 %all-gather = f32[8,96,64]{1,2,0:T(8,128)S(1)} all-gather(f32[1,96,64]{1,2,0:T(8,128)S(1)} %convolution_bitcast_fusion.2), channel_id=1, replica_groups=mesh['dp'=8,'rep'=4] {'dp'}, dimensions={0}, use_global_device_ids=true | all-gather | bytes 221184 | tf_op jit(solution)/shard_map/all_gather | solution.py:907
  815.7 29.1 %concatenate.196 = f32[861712]{0:T(1024)S(1)} concatenate(f32[13056]{0:T(1024)S(1)} %slice_bitcast_fusion.16, f32[196608]{0:T(1024)} %reshape.1231, f32[768]{0:T(1024)S(1)} %get-tuple-element.78, f32[589824]{0:T(1024)} %reshape.1232, f32[768]{0:T(1024)S(1)} %get-tuple-element.76, f32[25344]{0:T(1024)} %reshape.1233, f32[10752]{0:T(1024)S(1)} %convert_reduce_fusion.4, ...), dimensions={0} | concatenate | bytes 6893696 | tf_op jit(solution)/shard_map/concatenate | solution.py:921
  844.7 6.6 multiply_reduce_fusion.5
  852.1 6.2 fusion.137
  872.5 3.7 fusion.145
  884.6 3.8 fusion.140
  (693 shorter events, 169.9 us)
Async XLA Ops:
  7.2 260.2 %copy-start = (f32[2,1000]{1,0:T(2,128)S(1)}, f32[2,1000]{1,0:T(2,128)}, u32[]{:S(2)}) copy-start(f32[2,1000]{1,0:T(2,128)} %param.28) | copy-start | bytes 24004
  7.2 28.6 %copy-start.21 = (f32[2,96,3072]{2,1,0:T(8,128)S(1)}, f32[2,96,3072]{2,1,0:T(8,128)}, u32[]{:S(2)}) copy-start(f32[2,96,3072]{2,1,0:T(8,128)} %param.31) | copy-start | bytes 7077892
  7.2 852.5 %all-reduce.5.cloned.1.call-start = ((), (), s32[]{:S(2)}) async-start(), calls=%async_computation | async-start | bytes 401408 | tf_op jit(solution)/shard_map/psum | solution.py:957
  41.1 10.9 %copy-start.26 = (f32[2,384,768]{2,1,0:T(8,128)S(1)}, f32[2,384,768]{2,1,0:T(8,128)}, u32[]{:S(2)}) copy-start(f32[2,384,768]{2,1,0:T(8,128)} %param.32) | copy-start | bytes 7077892
  223.8 9.3 %copy-start.2 = (bf16[2,8,1152,768]{3,2,1,0:T(8,128)(2,1)}, bf16[2,8,1152,768]{3,2,1,0:T(8,128)(2,1)S(1)}, u32[]{:S(2)}) copy-start(bf16[2,8,1152,768]{3,2,1,0:T(8,128)(2,1)S(1)} %get-tuple-element.36) | copy-start | bytes 84934656
  279.8 6.0 copy-start.129
  310.7 5.7 copy-start.106
  310.7 5.7 slice-start.4
  310.7 5.7 copy-start.8
  310.7 5.7 slice-start.5
  310.7 5.7 copy-start.131
  310.7 5.7 copy-start.151
  356.1 5.7 copy-start.108
  356.1 5.7 slice-start.8
  356.1 5.7 copy-start.6
  356.1 5.7 slice-start.9
  356.1 5.7 copy-start.132
  356.1 5.7 copy-start.150
  361.8 5.8 copy-start.43
  369.4 10.4 %slice-start.10 = ((s8[4718592]{0:T(1024)(128)(4,1)}), s8[4194304]{0:T(1024)(128)(4,1)S(1)}, s32[]{:S(2)}) async-start(s8[4718592]{0:T(1024)(128)(4,1)} %bitcast.472), calls=%async_computation.11 | async-start | bytes 8388608
  372.3 7.5 slice-start.15
  372.8 7.1 slice-start.11
  372.8 7.1 slice-start.16
  386.4 5.5 copy-start.72
  386.4 5.5 copy-start.7
  386.4 5.5 copy-start.52
  386.4 5.5 copy-start.53
  386.4 5.5 copy-start.54
  386.4 5.5 copy-start.55
  413.8 11.7 %slice-start.2 = ((s8[6291456]{0:T(1024)(128)(4,1)}), s8[4194304]{0:T(1024)(128)(4,1)S(1)}, s32[]{:S(2)}) async-start(s8[6291456]{0:T(1024)(128)(4,1)} %bitcast.459), calls=%async_computation.3 | async-start | bytes 8388608
  418.2 7.2 slice-start.3
  432.1 9.2 %slice-start.6 = ((s8[4718592]{0:T(1024)(128)(4,1)}), s8[524288]{0:T(1024)(128)(4,1)S(1)}, s32[]{:S(2)}) async-start(s8[4718592]{0:T(1024)(128)(4,1)} %bitcast.466), calls=%async_computation.7 | async-start | bytes 1048576
  447.9 5.6 copy-start.74
  447.9 5.5 copy-start.9
  448.0 5.5 copy-start.48
  448.0 5.5 copy-start.49
  448.0 5.5 copy-start.50
  448.0 5.5 copy-start.51
  475.9 11.7 %slice-start = ((s8[6291456]{0:T(1024)(128)(4,1)}), s8[4194304]{0:T(1024)(128)(4,1)S(1)}, s32[]{:S(2)}) async-start(s8[6291456]{0:T(1024)(128)(4,1)} %bitcast.457), calls=%async_computation.1 | async-start | bytes 8388608
  480.4 7.2 slice-start.1
  504.6 7.4 slice-start.21
  511.9 6.5 copy-start.130
  512.0 6.5 copy-start.159
  522.9 14.2 %slice-start.19 = ((s8[4718592]{0:T(1024)(128)(4,1)}), s8[524288]{0:T(1024)(128)(4,1)S(1)}, s32[]{:S(2)}) async-start(s8[4718592]{0:T(1024)(128)(4,1)} %bitcast.522), calls=%async_computation.20 | async-start | bytes 1048576
  529.5 7.5 slice-start.20
  531.2 17.0 %slice-start.17 = ((s8[4718592]{0:T(1024)(128)(4,1)}), s8[4194304]{0:T(1024)(128)(4,1)S(1)}, s32[]{:S(2)}) async-start(s8[4718592]{0:T(1024)(128)(4,1)} %bitcast.519), calls=%async_computation.18 | async-start | bytes 8388608
  537.1 11.1 %slice-start.18 = ((s8[4718592]{0:T(1024)(128)(4,1)}), s8[524288]{0:T(1024)(128)(4,1)S(1)}, s32[]{:S(2)}) async-start(s8[4718592]{0:T(1024)(128)(4,1)} %bitcast.519), calls=%async_computation.19 | async-start | bytes 1048576
  537.4 9.7 %copy-start.18 = (bf16[1,4,2,1152,768]{4,3,2,1,0:T(8,128)(2,1)}, bf16[1,4,2,1152,768]{4,3,2,1,0:T(8,128)(2,1)S(1)}, u32[]{:S(2)}) copy-start(bf16[1,4,2,1152,768]{4,3,2,1,0:T(8,128)(2,1)S(1)} %constant_dynamic-update-slice_fusion) | copy-start | bytes 42467332
  775.4 34.3 %copy-start.113 = (f32[64,768]{1,0:T(8,128)S(1)}, f32[64,768]{1,0:T(8,128)}, u32[]{:S(2)}) copy-start(f32[64,768]{1,0:T(8,128)} %copy-done.112) | copy-start | bytes 589828
  775.4 34.4 %copy-start.101 = (bf16[768,768]{1,0:T(8,128)(2,1)S(1)}, bf16[768,768]{1,0:T(8,128)(2,1)}, u32[]{:S(2)}) copy-start(bf16[768,768]{1,0:T(8,128)(2,1)} %copy-done.100) | copy-start | bytes 3538948
  775.4 34.4 %copy-start.111 = (f32[64,768]{1,0:T(8,128)S(1)}, f32[64,768]{1,0:T(8,128)}, u32[]{:S(2)}) copy-start(f32[64,768]{1,0:T(8,128)} %copy-done.110) | copy-start | bytes 589828
  775.7 34.7 %copy-start.167 = (s32[64]{0:T(128)S(1)}, s32[64]{0:T(128)}, u32[]{:S(2)}) copy-start(s32[64]{0:T(128)} %select_n.67) | copy-start | bytes 772
  844.7 7.3 copy-start.12
  852.1 11.9 %copy-start.133 = (f32[10752]{0:T(1024)S(1)}, f32[10752]{0:T(1024)}, u32[]{:S(2)}) copy-start(f32[10752]{0:T(1024)} %param.43) | copy-start | bytes 129028
  852.1 16.5 %copy-start.143 = (f32[2,2304]{1,0:T(2,128)S(1)}, f32[2,2304]{1,0:T(2,128)}, u32[]{:S(2)}) copy-start(f32[2,2304]{1,0:T(2,128)} %param.35) | copy-start | bytes 55300
  852.1 16.7 %copy-start.140 = (f32[2,3072]{1,0:T(2,128)S(1)}, f32[2,3072]{1,0:T(2,128)}, u32[]{:S(2)}) copy-start(f32[2,3072]{1,0:T(2,128)} %param.39) | copy-start | bytes 73732
  852.1 17.9 %copy-start.155 = (f32[2,96]{1,0:T(2,128)S(1)}, f32[2,96]{1,0:T(2,128)}, u32[]{:S(2)}) copy-start(f32[2,96]{1,0:T(2,128)} %copy-done.154) | copy-start | bytes 2308
  858.3 14.2 %copy-start.20 = (f32[2,96,2304]{2,1,0:T(8,128)S(1)}, f32[2,96,2304]{2,1,0:T(8,128)}, u32[]{:S(2)}) copy-start(f32[2,96,2304]{2,1,0:T(8,128)} %copy-done.19) | copy-start | bytes 5308420
  858.3 14.2 %copy-start.157 = (f32[2,96]{1,0:T(2,128)S(1)}, f32[2,96]{1,0:T(2,128)}, u32[]{:S(2)}) copy-start(f32[2,96]{1,0:T(2,128)} %copy-done.156) | copy-start | bytes 2308
  865.4 17.0 %copy-start.114 = (f32[10752]{0:T(1024)}, f32[10752]{0:T(1024)S(1)}, u32[]{:S(2)}) copy-start(f32[10752]{0:T(1024)S(1)} %get-tuple-element.83) | copy-start | bytes 129028
  867.8 8.4 copy-start.138
  868.6 7.6 copy-start.139
  868.8 7.4 copy-start.128
  868.9 9.8 %copy-start.125 = (f32[2,3072]{1,0:T(2,128)}, f32[2,3072]{1,0:T(2,128)S(1)}, u32[]{:S(2)}) copy-start(f32[2,3072]{1,0:T(2,128)S(1)} %get-tuple-element.91) | copy-start | bytes 73732
  (141 other events, 396.0 us)
Sparse Core Ops, SparseCore 0:
  772.4 71.3 all-reduce.4

commit v3 on v1

--- a/solution.py
+++ b/solution.py
@@ -4,6 +4,8 @@
 import jax
 import jax.numpy as jnp
 from jax import lax
+from jax.experimental import pallas as pl
+from jax.experimental.pallas import tpu as pltpu
 from jax.sharding import PartitionSpec as P
 
 D = 768
@@ -226,6 +228,1169 @@
     return (grad_in, (grad_qkv, grad_proj, grad_fc1, grad_fc2), grad_bias, grad_spans)
 
 
+MESH_IDS = pl.DeviceIdType.MESH
+Z_SIZE, Y_SIZE, X_SIZE, C_SIZE = 4, 2, 2, 2
+LANES = 128
+
+
+def place():
+    dp, rep = lax.axis_index("dp"), lax.axis_index("rep")
+    return (dp // Y_SIZE, dp % Y_SIZE, rep // C_SIZE, rep % C_SIZE)
+
+
+def device(z, y, x, c):
+    return (z * Y_SIZE + y, x * C_SIZE + c)
+
+
+def meet(peers):
+    barrier = pltpu.get_barrier_semaphore()
+    for peer in peers:
+        pl.semaphore_signal(barrier, inc=1, device_id=peer, device_id_type=MESH_IDS)
+    pl.semaphore_wait(barrier, len(peers))
+
+
+def push(source, target, send, receive, peer):
+    return pltpu.make_async_remote_copy(
+        src_ref=source,
+        dst_ref=target,
+        send_sem=send,
+        recv_sem=receive,
+        device_id=peer,
+        device_id_type=MESH_IDS,
+    )
+
+
+def ids_kernel(own, full, send, receive, local):
+    dp, rep = lax.axis_index("dp"), lax.axis_index("rep")
+    dps, reps = Z_SIZE * Y_SIZE, X_SIZE * C_SIZE
+    offsets = [(i, j) for i in range(dps) for j in range(reps) if i or j]
+    peers = [((dp + i) % dps, (rep + j) % reps) for i, j in offsets]
+    meet(peers)
+    mine = dp * reps + rep
+    copies = [
+        push(own, full.at[mine], send.at[n], receive.at[n], peer) for n, peer in enumerate(peers)
+    ]
+    for copy in copies:
+        copy.start()
+    keep = pltpu.make_async_copy(own, full.at[mine], local)
+    keep.start()
+    keep.wait()
+    for copy in copies:
+        copy.wait()
+
+
+def gather_ids(own):
+    count = Z_SIZE * Y_SIZE * X_SIZE * C_SIZE
+    return pl.pallas_call(
+        ids_kernel,
+        out_shape=jax.ShapeDtypeStruct((count,) + own.shape, own.dtype),
+        in_specs=[pl.BlockSpec(memory_space=pltpu.VMEM)],
+        out_specs=pl.BlockSpec(memory_space=pltpu.VMEM),
+        scratch_shapes=[
+            pltpu.SemaphoreType.DMA((count - 1,)),
+            pltpu.SemaphoreType.DMA((count - 1,)),
+            pltpu.SemaphoreType.DMA,
+        ],
+        compiler_params=pltpu.CompilerParams(collective_id=1, has_side_effects=True),
+        name="gather_ids",
+    )(own)
+
+
+def gather_kernel(groups, packed, parts, full, summed, part_in, z_s, z_r, y_s, y_r, x_s, x_r, c_s, c_r, p_s, p_r, local):
+    z, y, x, c = place()
+    dp = z * Y_SIZE + y
+    dps = Z_SIZE * Y_SIZE
+    part_peers = [((dp + k) % dps, x * C_SIZE + c) for k in range(1, dps)]
+    across_y, across_x, sibling = device(z, 1 - y, x, c), device(z, y, 1 - x, c), device(z, y, x, 1 - c)
+    meet(part_peers + [across_x, sibling])
+    part_copies = [
+        push(parts.at[peer[0]], part_in.at[dp], p_s.at[k], p_r.at[k], peer)
+        for k, peer in enumerate(part_peers)
+    ]
+    for copy in part_copies:
+        copy.start()
+    keeps = []
+    for layer in range(LAYERS):
+        keep = pltpu.make_async_copy(packed.at[layer], full.at[layer, dp], local.at[layer])
+        keep.start()
+        keeps.append(keep)
+    started = []
+
+    def rows(group, third, count):
+        layer, first, size = groups[group]
+        step = size // 6
+        return pl.ds(pl.multiple_of(first + c * 3 * step + third * step, 16), count * step)
+
+    def source(k, other):
+        return ((z - k) % Z_SIZE) * Y_SIZE + (1 - y if other else y)
+
+    def piece(group, owner, third, count):
+        return full.at[groups[group][0], owner, rows(group, third, count)]
+
+    def go(source_ref, target_ref, send, receive, peer):
+        copy = push(source_ref, target_ref, send, receive, peer)
+        copy.start()
+        started.append(copy)
+
+    def first_hop(group):
+        own = packed.at[groups[group][0], rows(group, x, 2)]
+        target = piece(group, dp, x, 2)
+        go(own, target, y_s.at[group, 0], y_r.at[group, 0], across_y)
+        for k in range(1, Z_SIZE):
+            peer = device((z + k) % Z_SIZE, y, x, c)
+            go(own, target, z_s.at[group, k - 1], z_r.at[group, k - 1], peer)
+
+    def arrive(ref, send, receive, peer):
+        push(ref, ref, send, receive, peer).wait_recv()
+
+    def spread(group, index, owner):
+        third = piece(group, owner, 2 * x, 1)
+        go(third, third, x_s.at[group, index], x_r.at[group, index], across_x)
+        both = piece(group, owner, x, 2)
+        go(both, both, c_s.at[group, index], c_r.at[group, index], sibling)
+
+    def on_z(group, k):
+        ref = piece(group, source(k, False), x, 2)
+        arrive(ref, z_s.at[group, k - 1], z_r.at[group, k - 1], across_y)
+        go(ref, ref, y_s.at[group, k], y_r.at[group, k], across_y)
+        spread(group, k - 1, source(k, False))
+
+    def on_y(group, k):
+        ref = piece(group, source(k, True), x, 2)
+        arrive(ref, y_s.at[group, k], y_r.at[group, k], across_y)
+        spread(group, Z_SIZE - 1 + k, source(k, True))
+
+    def on_x(group, index):
+        owner = source(index + 1, False) if index < Z_SIZE - 1 else source(index - Z_SIZE + 1, True)
+        ref = piece(group, owner, 2 - 2 * x, 1)
+        arrive(ref, x_s.at[group, index], x_r.at[group, index], across_x)
+        slot = index + 2 * Z_SIZE - 1
+        go(ref, ref, c_s.at[group, slot], c_r.at[group, slot], sibling)
+
+    def on_c(group):
+        layer, first, size = groups[group]
+        step = size // 6
+        other = 1 - c
+        for index in range(2 * Z_SIZE - 1):
+            owner = source(index + 1, False) if index < Z_SIZE - 1 else source(index - Z_SIZE + 1, True)
+            for slot, third, count in ((index, x, 2), (index + 2 * Z_SIZE - 1, 2 - 2 * x, 1)):
+                start = pl.multiple_of(first + other * 3 * step + third * step, 16)
+                ref = full.at[layer, owner, pl.ds(start, count * step)]
+                arrive(ref, c_s.at[group, slot], c_r.at[group, slot], sibling)
+
+    first_hop(0)
+    count = len(groups)
+    for group in range(count + 1):
+        if group + 1 < count:
+            first_hop(group + 1)
+        events = []
+        if group < count:
+            events = [(on_y, group, 0)]
+            for k in range(1, Z_SIZE):
+                events += [(on_z, group, k), (on_y, group, k)]
+        for index in range(2 * Z_SIZE - 1):
+            if events:
+                step, *where = events[index]
+                step(*where)
+            if group > 0:
+                on_x(group - 1, index)
+        if group == 0:
+            for copy in part_copies:
+                copy.wait()
+            total = jnp.where(dp == 0, parts[0], part_in[0])
+            for k in range(1, dps):
+                total = total + jnp.where(dp == k, parts[k], part_in[k])
+            summed[...] = total
+    for group in range(count):
+        on_c(group)
+    for copy in started:
+        copy.wait_send()
+    for keep in keeps:
+        keep.wait()
+
+
+def gather_weights(packed, parts, groups):
+    layers, height, width = packed.shape
+    dps = Z_SIZE * Y_SIZE
+    count = len(groups)
+    dma = pltpu.SemaphoreType.DMA
+    return pl.pallas_call(
+        partial(gather_kernel, groups),
+        out_shape=(
+            jax.ShapeDtypeStruct((layers, dps, height, width), packed.dtype),
+            jax.ShapeDtypeStruct(parts.shape[1:], parts.dtype),
+        ),
+        in_specs=[pl.BlockSpec(memory_space=pl.ANY), pl.BlockSpec(memory_space=pltpu.VMEM)],
+        out_specs=(pl.BlockSpec(memory_space=pl.ANY), pl.BlockSpec(memory_space=pltpu.VMEM)),
+        scratch_shapes=[
+            pltpu.VMEM(parts.shape, parts.dtype),
+            dma((count, Z_SIZE - 1)),
+            dma((count, Z_SIZE - 1)),
+            dma((count, Z_SIZE)),
+            dma((count, Z_SIZE)),
+            dma((count, 2 * Z_SIZE - 1)),
+            dma((count, 2 * Z_SIZE - 1)),
+            dma((count, 4 * Z_SIZE - 2)),
+            dma((count, 4 * Z_SIZE - 2)),
+            dma((dps - 1,)),
+            dma((dps - 1,)),
+            dma((layers,)),
+        ],
+        compiler_params=pltpu.CompilerParams(
+            collective_id=2, has_side_effects=True, vmem_limit_bytes=16 * 2**20
+        ),
+        name="gather_weights",
+    )(packed, parts)
+
+
+GELU_A, GELU_B = 0.79788456, 0.044715
+FF_BLOCKS = FF // D
+TILE = 256
+ROWS = 64
+
+
+def centre(values):
+    centered = values - jnp.mean(values, axis=-1, keepdims=True)
+    inverse = lax.rsqrt(jnp.mean(centered * centered, axis=-1, keepdims=True) + EPS_NORM)
+    return centered * inverse, inverse
+
+
+def dot_nn(left, right):
+    return lax.dot_general(left, right, (((1,), (0,)), ((), ())), preferred_element_type=jnp.float32)
+
+
+def dot_nt(left, right):
+    return lax.dot_general(left, right, (((1,), (1,)), ((), ())), preferred_element_type=jnp.float32)
+
+
+def dot_tn(left, right):
+    return lax.dot_general(left, right, (((0,), (0,)), ((), ())), preferred_element_type=jnp.float32)
+
+
+def each(count, body):
+    if count <= 3:
+        for i in range(count):
+            body(i)
+        return
+    lax.fori_loop(0, count, lambda i, carry: (body(i), carry)[1], 0)
+
+
+def row_blocks(tokens, body, step=ROWS):
+    each(tokens // step, lambda i: body(pl.ds(pl.multiple_of(i * step, step), step), i // (GRID * GRID // step)))
+
+
+def modulate(source, mods, shift, scale, target, tokens):
+    def body(rows, image):
+        normed, _ = centre(source[rows])
+        target[rows] = (normed * (1.0 + mods[image, scale]) + mods[image, shift]).astype(jnp.bfloat16)
+
+    row_blocks(tokens, body)
+
+
+def block_at(i, size):
+    return pl.ds(i * size if isinstance(i, int) else pl.multiple_of(i * size, size), size)
+
+
+def columns(i):
+    return block_at(i, TILE)
+
+
+def head_lanes(head):
+    lane = lax.broadcasted_iota(jnp.int32, (GRID * GRID, 2 * D // HEADS), 1)
+    return lane // (D // HEADS) == head
+
+
+def softmax(query, keys):
+    scores = dot_nt(query, keys) * (1.0 / math.sqrt(D // HEADS))
+    powers = jnp.exp(scores - jnp.max(scores, axis=-1, keepdims=True))
+    return powers * (1.0 / jnp.sum(powers, axis=-1, keepdims=True))
+
+
+def pick(lanes, values):
+    return jnp.where(lanes, values, jnp.zeros_like(values))
+
+
+def attention_forward(projected, attended, images):
+    pairs = HEADS // 2
+    size, width = GRID * GRID, 2 * D // HEADS
+
+    def body(i, image):
+        rows, lanes = block_at(image, size), block_at(i, width)
+        query, keys, values = (projected[p, rows, lanes] for p in range(3))
+        first = head_lanes(0)
+        outs = []
+        for own in (first, jnp.logical_not(first)):
+            weights = softmax(pick(own, query), keys).astype(jnp.bfloat16)
+            outs.append(dot_nn(weights, values))
+        attended[rows, lanes] = jnp.where(first, outs[0], outs[1]).astype(jnp.bfloat16)
+
+    each(pairs, lambda i: [body(i, image) for image in range(images)])
+
+
+def attention_backward(projected, grad_attended, grad_projected, image, first_pair, pairs):
+    size, width = GRID * GRID, 2 * D // HEADS
+    scaling = 1.0 / math.sqrt(D // HEADS)
+
+    def body(i):
+        rows, lanes = block_at(image, size), block_at(first_pair + i, width)
+        query, keys, values = (projected[p, rows, lanes] for p in range(3))
+        grad_out = grad_attended[rows, lanes]
+        first = head_lanes(0)
+        outs = []
+        for own in (first, jnp.logical_not(first)):
+            weights = softmax(pick(own, query), keys)
+            grad_values = dot_tn(weights.astype(jnp.bfloat16), grad_out)
+            grad_weights = dot_nt(pick(own, grad_out), values)
+            inner = jnp.sum(weights * grad_weights, axis=-1, keepdims=True)
+            grad_scores = (weights * (grad_weights - inner)).astype(jnp.bfloat16)
+            outs.append(
+                (dot_nn(grad_scores, keys) * scaling, dot_tn(grad_scores, query) * scaling, grad_values)
+            )
+        for p in range(3):
+            grad_projected[p, rows, lanes] = jnp.where(first, outs[0][p], outs[1][p]).astype(jnp.bfloat16)
+
+    each(pairs, body)
+
+
+def whole(block):
+    return block.reshape(D, block.shape[-1])
+
+
+def forward_kernel(
+    start, mods, biases, full, out, x_h, proj_h, att_h, branch_a_h, middle_h, branch_b_h,
+    w_in, w_out, x_v, proj_v, att_v, branch_a, middle, branch_b, mixed, active, w_sem, save_sem,
+):
+    tokens = start.shape[0]
+    images = mods.shape[0]
+    shard = w_in.shape[3]
+    deep = w_out.shape[3]
+    count = 4 + FF_BLOCKS
+
+    def load(layer, index):
+        if index < count:
+            return pltpu.make_async_copy(
+                full.at[layer, :, pl.ds(index * shard, shard)], w_in.at[layer, index], w_sem.at[layer, index]
+            )
+        block = index - count
+        per = D // deep
+        return pltpu.make_async_copy(
+            full.at[layer, pl.ds(block * per, per), pl.ds(count * shard, deep)],
+            w_out.at[layer, block],
+            w_sem.at[layer, index],
+        )
+
+    order = [0, 1, 2, 3] + [i for b in range(FF_BLOCKS) for i in (4 + b, count + b)]
+    for layer in range(LAYERS):
+        for index in order:
+            load(layer, index).start()
+    x_v[0] = start[...]
+
+    def one_layer(layer):
+        saves = []
+
+        def save(source, target, index):
+            copy = pltpu.make_async_copy(source.at[layer], target.at[layer], save_sem.at[layer, index])
+            copy.start()
+            saves.append(copy)
+
+        base = 6 * layer
+        x, projected, attended = x_v.at[layer], proj_v.at[layer], att_v.at[layer]
+        mid = middle.at[layer]
+        save(x_v, x_h, 0)
+        modulate(x, mods, base, base + 1, mixed, tokens)
+        for p in range(3):
+            load(layer, p).wait()
+
+            def project(i, p=p):
+                value = dot_nn(mixed[...], whole(w_in[layer, p, :, :, columns(i)]))
+                if p != 1:
+                    value = value + biases[layer, p // 2, :, columns(i)]
+                projected[p, :, columns(i)] = value.astype(jnp.bfloat16)
+
+            each(D // TILE, project)
+        save(proj_v, proj_h, 1)
+        attention_forward(projected, attended, images)
+        save(att_v, att_h, 2)
+        load(layer, 3).wait()
+
+        def first_branch(i):
+            value = dot_nn(attended[...], whole(w_in[layer, 3, :, :, columns(i)]))
+            value = value + biases[layer, 2, :, columns(i)]
+            branch_a[layer, :, columns(i)] = value
+            for image in range(images):
+                rows = pl.ds(image * GRID * GRID, GRID * GRID)
+                part = value[image * GRID * GRID : (image + 1) * GRID * GRID]
+                mid[rows, columns(i)] = x[rows, columns(i)] + mods[image, base + 2, :, columns(i)] * part
+
+        each(D // TILE, first_branch)
+        save(branch_a, branch_a_h, 3)
+        save(middle, middle_h, 4)
+        modulate(mid, mods, base + 3, base + 4, mixed, tokens)
+        for block in range(FF_BLOCKS):
+            load(layer, 4 + block).wait()
+
+            def expand(i, block=block):
+                hidden = dot_nn(mixed[...], whole(w_in[layer, 4 + block, :, :, columns(i)]))
+                hidden = hidden + biases[layer, 3 + block, :, columns(i)]
+                inner = jnp.tanh(GELU_A * (hidden + GELU_B * hidden * hidden * hidden))
+                active[:, columns(i)] = (0.5 * hidden * (1.0 + inner)).astype(jnp.bfloat16)
+
+            each(D // TILE, expand)
+            load(layer, count + block).wait()
+
+            def contract(i, block=block):
+                value = dot_nn(active[...], whole(w_out[layer, block, :, :, columns(i)]))
+                if block == 0:
+                    branch_b[layer, :, columns(i)] = value + biases[layer, 3 + FF_BLOCKS, :, columns(i)]
+                else:
+                    branch_b[layer, :, columns(i)] += value
+
+            each(D // TILE, contract)
+        save(branch_b, branch_b_h, 5)
+
+        def finish(rows, image):
+            value = mid[rows] + mods[image, base + 5] * branch_b[layer, rows]
+            out[rows] = value
+
+            @pl.when(layer + 1 < LAYERS)
+            def _():
+                x_v[layer + 1, rows] = value
+
+        row_blocks(tokens, finish)
+        for copy in saves:
+            copy.wait()
+
+    each(LAYERS, one_layer)
+
+
+def run_forward(start, mods, biases, full):
+    tokens = start.shape[0]
+    layers, owners, height, width = full.shape
+    shard, deep = D // owners, FF // owners
+    wide, low = jnp.float32, jnp.bfloat16
+    keep = [
+        ((tokens, D), wide), ((3, tokens, D), low), ((tokens, D), low),
+        ((tokens, D), wide), ((tokens, D), wide), ((tokens, D), wide),
+    ]
+    vmem, anywhere = pl.BlockSpec(memory_space=pltpu.VMEM), pl.BlockSpec(memory_space=pl.ANY)
+    kept = [jax.ShapeDtypeStruct((layers,) + shape, kind) for shape, kind in keep]
+    return pl.pallas_call(
+        forward_kernel,
+        out_shape=[jax.ShapeDtypeStruct((tokens, D), wide)] + kept,
+        in_specs=[vmem, vmem, vmem, anywhere],
+        out_specs=[vmem] + [anywhere] * len(keep),
+        scratch_shapes=[
+            pltpu.VMEM((layers, 4 + FF_BLOCKS, owners, shard, D), low),
+            pltpu.VMEM((layers, FF_BLOCKS, D // deep, deep, D), low),
+        ]
+        + [pltpu.VMEM(entry.shape, entry.dtype) for entry in kept]
+        + [
+            pltpu.VMEM((tokens, D), low),
+            pltpu.VMEM((tokens, D), low),
+            pltpu.SemaphoreType.DMA((layers, 4 + 2 * FF_BLOCKS)),
+            pltpu.SemaphoreType.DMA((layers, len(keep))),
+        ],
+        compiler_params=pltpu.CompilerParams(vmem_limit_bytes=62 * 2**20),
+        name="blocks_forward",
+    )(start, mods, biases, full)
+
+
+class Pace:
+    RATE = 48e3
+    LATENCY = 2.2
+
+    def __init__(self):
+        self.now = 0.0
+        self.free = {}
+        self.entries = []
+
+    def send(self, link, count):
+        rate = 10 * self.RATE if link == "c" else self.RATE
+        self.free[link] = max(self.now, self.free.get(link, 0.0)) + count / rate
+        return self.free[link] + self.LATENCY
+
+    def add(self, ready, run):
+        self.entries.append([ready, len(self.entries), run])
+
+    def serve(self, entry):
+        cost, ready = entry[2]()
+        self.now += cost
+        if ready is None:
+            self.entries.remove(entry)
+        else:
+            entry[0] = ready
+
+    def spend(self, cost):
+        self.now += cost
+        while self.entries:
+            entry = min(self.entries, key=lambda e: e[:2])
+            if entry[0] > self.now:
+                return
+            self.serve(entry)
+
+    def drain(self):
+        while self.entries:
+            entry = min(self.entries, key=lambda e: e[:2])
+            self.now = max(self.now, entry[0])
+            self.serve(entry)
+
+
+class Reduction:
+    COSTS = (0.6, 0.4, 0.8, 0.5, 0.4, 0.1)
+
+    def __init__(self, pace, groups, shard, spot, buffers, semaphores, credits, finals):
+        self.pace, self.groups, self.shard, self.spot = pace, groups, shard, spot
+        self.held, self.from_c, self.from_x, self.from_y, self.from_z, self.from_fin = buffers
+        self.sems, self.credits, self.finals = semaphores, credits, finals
+        z, y, x, c = spot
+        self.z_peers = [device((z + k) % Z_SIZE, y, x, c) for k in range(1, Z_SIZE)]
+        self.z_before = [device((z - k) % Z_SIZE, y, x, c) for k in range(1, Z_SIZE)]
+        self.across_y, self.across_x = device(z, 1 - y, x, c), device(z, y, 1 - x, c)
+        self.sibling = device(z, y, x, 1 - c)
+        self.started, self.kept, self.filled, self.busy = {}, {}, {}, {}
+        self.at_half = [first for first, _, _ in groups]
+        self.halves = [rows for _, rows, _ in groups]
+        self.parts = [part for _, _, part in groups]
+        most = [rows - part for _, rows, part in groups]
+        self.at_part = [sum(self.parts[:g]) for g in range(len(groups))]
+        self.at_most = [sum(most[:g]) for g in range(len(groups))]
+
+    def peers(self):
+        return self.z_peers + [self.across_y, self.across_x, self.sibling]
+
+    def go(self, key, source, target, sems, peer):
+        copy = push(source, target, sems[0], sems[1], peer)
+        copy.start()
+        self.started.setdefault(key, []).append(copy)
+
+    def arrive(self, ref, sems):
+        push(ref, ref, sems[0], sems[1], self.across_y).wait_recv()
+
+    def sem(self, name, layer, *index):
+        send, receive = self.sems[name]
+        return send.at[(layer,) + index], receive.at[(layer,) + index]
+
+    def give(self, layer, name, peer, *index):
+        if layer == LAYERS - 1:
+            pl.semaphore_signal(
+                self.credits[name].at[index], inc=1, device_id=peer, device_id_type=MESH_IDS
+            )
+
+    def take(self, layer, name, *index):
+        if layer != LAYERS - 1:
+            pl.semaphore_wait(self.credits[name].at[index], 1)
+
+    def put(self, layer, group, stage, first, squares, owner_z, slot):
+        c = self.spot[3]
+        half = self.shard // 2
+        if (layer, group) not in self.filled:
+            while (layer + 1, group) in self.busy:
+                self.pace.spend(0.5)
+            for copy in self.started.pop((layer + 1, group), []):
+                copy.wait_send()
+            self.take(layer, "c", group)
+            self.filled[layer, group] = []
+        rows = pl.ds(first, squares * half)
+        theirs = stage.at[:, :, :, pl.ds(pl.multiple_of((1 - c) * half, 16), half)]
+        ours = stage.at[:, :, :, pl.ds(pl.multiple_of(c * half, 16), half)]
+        zs = stage.shape[0]
+
+        def view(ref):
+            pieces = ref.reshape(Z_SIZE, Y_SIZE, ref.shape[2] // half, half, D)
+            return pieces.at[pl.ds(owner_z, zs), :, pl.ds(first // half, squares)]
+
+        sems = self.sem("c", layer, group, slot)
+        send = push(theirs, view(self.from_c), sems[0], sems[1], self.sibling)
+        keep = pltpu.make_async_copy(ours, view(self.held), self.sems["keep"].at[layer, group, slot])
+        send.start()
+        keep.start()
+        self.filled[layer, group].append((slot, owner_z, zs, rows))
+        self.kept[layer, group, slot] = keep
+        self.ready = self.pace.send("c", zs * Y_SIZE * squares * half * D * 2)
+
+        def free():
+            send.wait_send()
+            self.keep_wait(layer, group, slot)
+
+        return free
+
+    def begin(self, layer, group):
+        stages = [self.on_c, self.on_x, self.on_y, self.on_z, self.on_fin, self.on_last]
+        costs = list(self.COSTS)
+        self.busy[layer, group] = True
+
+        def run():
+            ready = stages.pop(0)(layer, group)
+            if not stages:
+                del self.busy[layer, group]
+            return costs.pop(0), ready
+
+        self.pace.add(self.ready, run)
+
+    def keep_wait(self, *key):
+        keep = self.kept.pop(key, None)
+        if keep is not None:
+            keep.wait()
+
+    def add(self, target, extra):
+        def body(owner):
+            total = target[owner].astype(jnp.float32) + extra[owner].astype(jnp.float32)
+            target[owner] = total.astype(jnp.bfloat16)
+
+        each(Z_SIZE, body)
+
+    def on_c(self, layer, group):
+        z, y, x, c = self.spot
+        half, part = self.halves[group], self.parts[group]
+        first = self.at_half[group]
+        for slot, owner_z, zs, rows in self.filled[layer, group]:
+            self.keep_wait(layer, group, slot)
+            self.arrive(self.from_c.at[pl.ds(owner_z, zs), :, rows], self.sem("c", layer, group, slot))
+        theirs = pl.ds(pl.multiple_of(first + (1 - x) * (half - part), 16), part)
+        ours = pl.ds(pl.multiple_of(first + x * part, 16), half - part)
+        for side in range(Y_SIZE):
+            self.add(self.held.at[:, side, theirs], self.from_c.at[:, side, theirs])
+        target = self.from_x.at[:, :, pl.ds(self.at_part[group], part)]
+        self.take(layer, "x", group)
+        self.go((layer, group), self.held.at[:, :, theirs], target, self.sem("x", layer, group), self.across_x)
+        for side in range(Y_SIZE):
+            self.add(self.held.at[:, side, ours], self.from_c.at[:, side, ours])
+        self.give(layer, "c", self.sibling, group)
+        return self.pace.send("x", 8 * part * D * 2)
+
+    def on_x(self, layer, group):
+        z, y, x, c = self.spot
+        half, part = self.halves[group], self.parts[group]
+        first = self.at_half[group]
+        got = self.from_x.at[:, :, pl.ds(self.at_part[group], part)]
+        self.arrive(got, self.sem("x", layer, group))
+        ours = pl.ds(pl.multiple_of(first + x * (half - part), 16), part)
+        for side in (1 - y, y):
+            self.add(self.held.at[:, side, ours], self.from_x.at[:, side, pl.ds(self.at_part[group], part)])
+        self.give(layer, "x", self.across_x, group)
+        most = pl.ds(pl.multiple_of(first + x * part, 16), half - part)
+        self.take(layer, "y", group)
+        self.go(
+            (layer, group), self.held.at[:, 1 - y, most], self.from_y.at[:, pl.ds(self.at_most[group], half - part)],
+            self.sem("y", layer, group), self.across_y,
+        )
+        return self.pace.send("y", 4 * (half - part) * D * 2)
+
+    def on_y(self, layer, group):
+        z, y, x, c = self.spot
+        half, part = self.halves[group], self.parts[group]
+        got = self.from_y.at[:, pl.ds(self.at_most[group], half - part)]
+        self.arrive(got, self.sem("y", layer, group))
+        most = pl.ds(pl.multiple_of(self.at_half[group] + x * part, 16), half - part)
+        self.add(self.held.at[:, y, most], got)
+        self.give(layer, "y", self.across_y, group)
+        for k in range(1, Z_SIZE):
+            self.take(layer, "z", group, k - 1)
+            self.go(
+                (layer, group), self.held.at[(z + k) % Z_SIZE, y, most],
+                self.from_z.at[k - 1, pl.ds(self.at_most[group], half - part)],
+                self.sem("z", layer, group, k - 1), self.z_peers[k - 1],
+            )
+        return self.pace.send("z", 4 * (half - part) * D * 2)
+
+    def on_z(self, layer, group):
+        z, y, x, c = self.spot
+        half, part = self.halves[group], self.parts[group]
+        most = pl.ds(pl.multiple_of(self.at_half[group] + x * part, 16), half - part)
+        got = pl.ds(self.at_most[group], half - part)
+        for k in range(1, Z_SIZE):
+            self.arrive(self.from_z.at[k - 1, got], self.sem("z", layer, group, k - 1))
+        total = self.held[z, y, most].astype(jnp.float32)
+        for k in range(1, Z_SIZE):
+            total = total + self.from_z[k - 1, got].astype(jnp.float32)
+        self.held[z, y, most] = total.astype(jnp.bfloat16)
+        for k in range(1, Z_SIZE):
+            self.give(layer, "z", self.z_before[k - 1], group, k - 1)
+        self.take(layer, "e", group)
+        self.go((layer, group), self.held.at[z, y, most], self.from_fin.at[got], self.sem("e", layer, group), self.across_x)
+        return self.pace.send("x", (half - part) * D * 2)
+
+    def on_fin(self, layer, group):
+        z, y, x, c = self.spot
+        half, part = self.halves[group], self.parts[group]
+        middle = half - 2 * part
+        base, start = self.at_most[group], self.at_half[group]
+        self.arrive(self.from_fin.at[pl.ds(base, half - part)], self.sem("e", layer, group))
+        wide = jnp.float32
+
+        def span(begin, size):
+            return pl.ds(pl.multiple_of(begin, 16), size)
+
+        ours, theirs = span(start + x * (half - part), part), span(start + (1 - x) * (half - part), part)
+        both = span(start + part, middle)
+        self.finals[layer, c, ours] = self.held[z, y, ours].astype(wide)
+        self.finals[layer, c, theirs] = self.from_fin[span(base + (1 - x) * middle, part)].astype(wide)
+        self.finals[layer, c, both] = self.held[z, y, both].astype(wide) + self.from_fin[
+            span(base + x * part, middle)
+        ].astype(wide)
+        self.give(layer, "e", self.across_x, group)
+        ref = self.finals.at[layer, c, pl.ds(start, half)]
+        self.go((layer, group), ref, ref, self.sem("f", layer, group), self.sibling)
+        return self.pace.send("c", half * D * 4)
+
+    def on_last(self, layer, group):
+        c = self.spot[3]
+        ref = self.finals.at[layer, 1 - c, pl.ds(self.at_half[group], self.halves[group])]
+        self.arrive(ref, self.sem("f", layer, group))
+        return None
+
+    def finish(self):
+        for copies in self.started.values():
+            for copy in copies:
+                copy.wait_send()
+
+
+class Sums:
+    def __init__(self, reduction, own, total, small_c, small_x, small_y, small_z, mods, mods_all, sems, mod_sems, local):
+        self.r = reduction
+        self.own, self.total = own, total
+        self.small_c, self.small_x, self.small_y, self.small_z = small_c, small_x, small_y, small_z
+        self.mods, self.mods_all, self.v, self.m, self.local = mods, mods_all, sems, mod_sems, local
+        self.stages = [self.first, self.to_x, self.to_y, self.to_z, self.to_c, self.last]
+
+    def sem(self, pair, index):
+        return pair[0].at[index], pair[1].at[index]
+
+    def go(self, ref, target, pair, index, peer):
+        self.r.go("sums", ref, target, self.sem(pair, index), peer)
+
+    def arrive(self, ref, pair, index):
+        self.r.arrive(ref, self.sem(pair, index))
+
+    def run(self):
+        self.stages.pop(0)()
+        return 1.0, self.r.pace.now + 7.0 if self.stages else None
+
+    def halves(self):
+        span = self.small_c.shape[0]
+        c = self.r.spot[3]
+        return [pl.ds(pl.multiple_of(i * span, 8), span) for i in (c, 1 - c)]
+
+    def first(self):
+        z, y, x, c = self.r.spot
+        mine, other = self.halves()
+        self.go(self.own.at[other], self.small_c, self.v, 0, self.r.sibling)
+        own = self.mods_all.at[z, y, x * C_SIZE + c]
+        keep = pltpu.make_async_copy(self.mods, own, self.local)
+        keep.start()
+        for k in range(1, Z_SIZE):
+            self.go(self.mods, own, self.m, k - 1, self.r.z_peers[k - 1])
+        keep.wait()
+
+    def to_x(self):
+        z, y, x, c = self.r.spot
+        mine, other = self.halves()
+        self.arrive(self.small_c, self.v, 0)
+        self.small_c[...] = self.small_c[...] + self.own[mine]
+        self.go(self.small_c, self.small_x, self.v, 1, self.r.across_x)
+        slot = x * C_SIZE + c
+        for k in range(1, Z_SIZE):
+            self.arrive(self.mods_all.at[(z - k) % Z_SIZE, y, slot], self.m, k - 1)
+        ref = self.mods_all.at[:, y, slot]
+        self.go(ref, ref, self.m, 3, self.r.across_y)
+
+    def to_y(self):
+        z, y, x, c = self.r.spot
+        self.arrive(self.small_x, self.v, 1)
+        self.small_x[...] = self.small_x[...] + self.small_c[...]
+        self.go(self.small_x, self.small_y, self.v, 2, self.r.across_y)
+        slot = x * C_SIZE + c
+        self.arrive(self.mods_all.at[:, 1 - y, slot], self.m, 3)
+        ref = self.mods_all.at[:, :, slot]
+        self.go(ref, ref, self.m, 4, self.r.across_x)
+
+    def to_z(self):
+        z, y, x, c = self.r.spot
+        self.arrive(self.small_y, self.v, 2)
+        self.small_z[z] = self.small_y[...] + self.small_x[...]
+        own = self.small_z.at[z]
+        for k in range(1, Z_SIZE):
+            self.go(own, own, self.v, 2 + k, self.r.z_peers[k - 1])
+        self.arrive(self.mods_all.at[:, :, (1 - x) * C_SIZE + c], self.m, 4)
+        for k in range(X_SIZE):
+            ref = self.mods_all.at[:, :, k * C_SIZE + c]
+            self.go(ref, ref, self.m, 5 + k, self.r.sibling)
+
+    def to_c(self):
+        z, y, x, c = self.r.spot
+        mine, other = self.halves()
+        for k in range(1, Z_SIZE):
+            self.arrive(self.small_z.at[(z - k) % Z_SIZE], self.v, 2 + k)
+        self.total[mine] = (self.small_z[0] + self.small_z[1]) + (self.small_z[2] + self.small_z[3])
+        self.go(self.total.at[mine], self.total.at[mine], self.v, 6, self.r.sibling)
+        for k in range(X_SIZE):
+            self.arrive(self.mods_all.at[:, :, k * C_SIZE + 1 - c], self.m, 5 + k)
+
+    def last(self):
+        mine, other = self.halves()
+        self.arrive(self.total.at[other], self.v, 6)
+
+
+def backward_kernel(
+    groups, grad_out, mods, biases, tokens_t, head_sums, head_mods, full,
+    x_h, proj_h, att_h, branch_a_h, middle_h, branch_b_h,
+    finals, mods_all, sums_out,
+    w_v, grad_x, x_v, proj_v, att_v, branch, middle, mixed, grad_b, active, grad_hidden, grad_mixed,
+    grad_projected, stage, mods_acc, mods_tile, mods_low, sums,
+    held, from_c, from_x, from_y, from_z, from_fin, small_c, small_x, small_y, small_z,
+    w_sem, load_sem, keep_sem, c_s, c_r, x_s, x_r, y_s, y_r, z_s, z_r, e_s, e_r, f_s, f_r,
+    v_s, v_r, m_s, m_r, local, cred_c, cred_x, cred_y, cred_z, cred_e,
+):
+    tokens = grad_out.shape[0]
+    images = mods.shape[0]
+    owners = full.shape[1]
+    shard, deep = D // owners, FF // owners
+    count = 4 + FF_BLOCKS
+    per = D // deep
+    slots = w_v.shape[0]
+    spot = place()
+    pace = Pace()
+    reduction = Reduction(
+        pace, groups, shard, spot, (held, from_c, from_x, from_y, from_z, from_fin),
+        {"c": (c_s, c_r), "x": (x_s, x_r), "y": (y_s, y_r), "z": (z_s, z_r), "e": (e_s, e_r), "f": (f_s, f_r), "keep": keep_sem},
+        {"c": cred_c, "x": cred_x, "y": cred_y, "z": cred_z, "e": cred_e}, finals,
+    )
+    order = [i for b in range(FF_BLOCKS) for i in (4 + b, count + b)] + [3, 0, 1, 2]
+    order = [(layer, index) for layer in reversed(range(LAYERS)) for index in order]
+
+    def load(at):
+        layer, index = order[at]
+        slot = at % slots
+        target = w_v.at[slot]
+        if index < count:
+            return pltpu.make_async_copy(
+                full.at[layer, :, pl.ds(index * shard, shard)], target.reshape(owners, shard, D), w_sem.at[slot]
+            )
+        return pltpu.make_async_copy(
+            full.at[layer, pl.ds((index - count) * per, per), pl.ds(count * shard, deep)],
+            target.reshape(per, deep, D),
+            w_sem.at[slot],
+        )
+
+    def fetch(at):
+        if at < len(order):
+            load(at).start()
+
+    def weight(at):
+        load(at).wait()
+        return w_v.at[at % slots]
+
+    def total(values):
+        return jnp.sum(values, axis=0, keepdims=True)
+
+    for at in range(slots):
+        fetch(at)
+    reduction_peers = reduction.peers()
+    meet(reduction_peers)
+    sums[...] = jnp.zeros_like(sums)
+    sums[pl.ds(PDIM, 2 * PDIM)] = head_sums[...]
+    mods_acc[...] = jnp.zeros_like(mods_acc)
+    for image in range(images):
+        for k in range(2):
+            mods_acc[image, 6 * LAYERS + k] = head_mods[image, k]
+    grad_x[...] = grad_out[...]
+    busy = [[], []]
+    turn = [0]
+
+    def weight_grad(layer, left, right, index):
+        slot = turn[0] % 2
+        turn[0] += 1
+        for wait in busy[slot]:
+            wait()
+
+        def body(i):
+            cut = block_at(i, D // 2)
+            value = dot_tn(left[:, cut], right[...]).astype(jnp.bfloat16)
+            stage[slot, cut] = value
+
+        each(2, body)
+        half = shard // 2
+        if index < count:
+            group = next(g for g, entry in enumerate(groups) if entry[0] <= index * half < entry[0] + entry[1])
+            view = stage.at[slot].reshape(Z_SIZE, Y_SIZE, 1, shard, D)
+            busy[slot] = [
+                reduction.put(layer, group, view, index * half, 1, 0, (index * half - groups[group][0]) // half)
+            ]
+            if index * half == groups[group][0] + groups[group][1] - half:
+                reduction.begin(layer, group)
+        else:
+            block = index - count
+            busy[slot] = []
+            for group, (first, rows, _) in enumerate(groups):
+                if first >= count * half:
+                    squares = rows // half
+                    view = stage.at[slot].reshape(1, Y_SIZE, deep // shard, shard, D)
+                    view = view.at[:, :, pl.ds((first - count * half) // half, squares)]
+                    busy[slot].append(reduction.put(layer, group, view, first, squares, block, block))
+                    if block == FF_BLOCKS - 1:
+                        reduction.begin(layer, group)
+        pace.spend(1.3)
+
+    for layer in reversed(range(LAYERS)):
+        base = 6 * layer
+        at = (LAYERS - 1 - layer) * (count + FF_BLOCKS)
+        bias_row = 3 * PDIM + layer * (4 + FF_BLOCKS)
+
+        def bias_add(k, values, cut=slice(None), bias_row=bias_row):
+            sums[pl.ds(bias_row + k, 1), cut] += total(values)
+
+        saved = [
+            (branch_b_h, branch), (middle_h, middle), (att_h, att_v), (proj_h, proj_v), (x_h, x_v), (branch_a_h, branch),
+        ]
+        copies = [
+            pltpu.make_async_copy(source.at[layer], target, load_sem.at[i])
+            for i, (source, target) in enumerate(saved)
+        ]
+        for copy in copies[:-1]:
+            copy.start()
+        copies[0].wait()
+        copies[1].wait()
+
+        def enter(rows, image, base=base, bias_add=bias_add):
+            grad = grad_x[rows]
+            low = (mods[image, base + 5] * grad).astype(jnp.bfloat16)
+            grad_b[rows] = low
+            bias_add(3 + FF_BLOCKS, low.astype(jnp.float32))
+            mods_acc[image, base + 5] += total(grad * branch[rows])
+            normed, _ = centre(middle[rows])
+            mixed[rows] = (normed * (1.0 + mods[image, base + 4]) + mods[image, base + 3]).astype(jnp.bfloat16)
+
+        row_blocks(tokens, enter)
+        pace.spend(1.8)
+        copies[-1].start()
+        for block in range(FF_BLOCKS):
+            w_one, w_two = weight(at), weight(at + 1)
+
+            def expand(i, block=block, w_one=w_one, w_two=w_two, layer=layer, bias_add=bias_add):
+                hidden = dot_nn(mixed[...], w_one[:, columns(i)]) + biases[layer, 3 + block, :, columns(i)]
+                square = hidden * hidden
+                inner = jnp.tanh(GELU_A * (hidden + GELU_B * hidden * square))
+                active[:, columns(i)] = (0.5 * hidden * (1.0 + inner)).astype(jnp.bfloat16)
+                slope = 0.5 * (1.0 + inner) + 0.5 * hidden * (1.0 - inner * inner) * (
+                    GELU_A * (1.0 + 3.0 * GELU_B * square)
+                )
+                low = (slope * dot_nt(grad_b[...], w_two[columns(i)])).astype(jnp.bfloat16)
+                grad_hidden[:, columns(i)] = low
+                bias_add(3 + block, low.astype(jnp.float32), columns(i))
+
+            each(D // TILE, expand)
+            pace.spend(3.6)
+            weight_grad(layer, active, grad_b, count + block)
+
+            def back(i, block=block, w_one=w_one):
+                value = dot_nt(grad_hidden[...], w_one[columns(i)])
+                if block == 0:
+                    grad_mixed[:, columns(i)] = value
+                else:
+                    grad_mixed[:, columns(i)] += value
+
+            each(D // TILE, back)
+            pace.spend(1.0)
+            fetch(at + slots)
+            fetch(at + slots + 1)
+            weight_grad(layer, mixed, grad_hidden, 4 + block)
+            at += 2
+        for copy in copies[2:]:
+            copy.wait()
+
+        def leave(rows, image, base=base, bias_add=bias_add):
+            grad = grad_mixed[rows]
+            normed, inverse = centre(middle[rows])
+            mods_acc[image, base + 3] += total(grad)
+            mods_acc[image, base + 4] += total(grad * normed)
+            grad = grad * (1.0 + mods[image, base + 4])
+            grad = grad_x[rows] + inverse * (
+                grad - jnp.mean(grad, axis=-1, keepdims=True) - normed * jnp.mean(grad * normed, axis=-1, keepdims=True)
+            )
+            middle[rows] = grad
+            low = (mods[image, base + 2] * grad).astype(jnp.bfloat16)
+            grad_b[rows] = low
+            bias_add(2, low.astype(jnp.float32))
+            mods_acc[image, base + 2] += total(grad * branch[rows])
+            normed, _ = centre(x_v[rows])
+            mixed[rows] = (normed * (1.0 + mods[image, base + 1]) + mods[image, base]).astype(jnp.bfloat16)
+
+        row_blocks(tokens, leave)
+        pace.spend(2.6)
+        w_proj = weight(at)
+
+        def through(i, w_proj=w_proj):
+            active[:, columns(i)] = dot_nt(grad_b[...], w_proj[columns(i)]).astype(jnp.bfloat16)
+
+        each(D // TILE, through)
+        pace.spend(0.9)
+        fetch(at + slots)
+        weight_grad(layer, att_v, grad_b, 3)
+        for image in range(images):
+            for pair in range(0, HEADS // 2, 2):
+                attention_backward(proj_v, active, grad_projected, image, pair, 2)
+                pace.spend(2.1)
+        for p in range(3):
+            w_part = weight(at + 1 + p)
+
+            def into(i, p=p, w_part=w_part):
+                value = dot_nt(grad_projected[p], w_part[columns(i)])
+                if p == 0:
+                    grad_mixed[:, columns(i)] = value
+                else:
+                    grad_mixed[:, columns(i)] += value
+
+            weight_grad(layer, mixed, grad_projected.at[p], p)
+            each(D // TILE, into)
+            pace.spend(1.0)
+            fetch(at + 1 + p + slots)
+
+        def last(rows, image, base=base, bias_add=bias_add):
+            grad = grad_mixed[rows]
+            normed, inverse = centre(x_v[rows])
+            mods_acc[image, base] += total(grad)
+            mods_acc[image, base + 1] += total(grad * normed)
+            grad = grad * (1.0 + mods[image, base + 1])
+            grad_x[rows] = middle[rows] + inverse * (
+                grad - jnp.mean(grad, axis=-1, keepdims=True) - normed * jnp.mean(grad * normed, axis=-1, keepdims=True)
+            )
+            bias_add(0, grad_projected[0, rows].astype(jnp.float32))
+            bias_add(1, grad_projected[2, rows].astype(jnp.float32))
+
+        row_blocks(tokens, last)
+        pace.spend(2.2)
+
+    def patch(rows, image):
+        low = grad_x[rows].astype(jnp.bfloat16)
+        grad_b[rows] = low
+        sums[pl.ds(2 * PDIM + 8, 1)] += total(low.astype(jnp.float32))
+
+    row_blocks(tokens, patch)
+    sums[pl.ds(0, PDIM)] = dot_nn(tokens_t[...], grad_b[...])
+    mods_tile[...] = jnp.zeros_like(mods_tile)
+    entries = mods.shape[1]
+    for image in range(images):
+        for k in range(entries):
+            mods_tile[pl.ds(image * entries + k, 1)] = mods_acc[image, k]
+    mods_low[...] = mods_tile[...].astype(jnp.bfloat16)
+    small = Sums(
+        reduction, sums, sums_out, small_c, small_x, small_y, small_z, mods_low, mods_all, (v_s, v_r), (m_s, m_r), local
+    )
+    pace.add(pace.now, small.run)
+    pace.drain()
+    reduction.finish()
+    for waits in busy:
+        for wait in waits:
+            wait()
+
+
+def run_backward(grad_out, mods, biases, tokens_t, head_sums, head_mods, full, kept):
+    tokens = grad_out.shape[0]
+    images, entries = mods.shape[:2]
+    layers, owners, height, width = full.shape
+    shard = D // owners
+    count = 4 + FF_BLOCKS
+    piece = shard // 2
+    sizes = [(2, 1), (1, 1), (1, 1), (2, 2), (2, 1), (2, 2), (2, 1)]
+    groups = []
+    for squares, thirds in sizes:
+        first = sum(group[1] for group in groups)
+        groups.append((first, squares * piece, thirds * piece // 3))
+    half = height // 2
+    part = sum(group[2] for group in groups)
+    most = half - part
+    wide, low = jnp.float32, jnp.bfloat16
+    vmem, anywhere = pl.BlockSpec(memory_space=pltpu.VMEM), pl.BlockSpec(memory_space=pl.ANY)
+    rows = (tokens, D)
+    dma, regular = pltpu.SemaphoreType.DMA, pltpu.SemaphoreType.REGULAR
+    number = len(groups)
+    sum_rows = 3 * PDIM + LAYERS * count
+    mod_rows = -(-images * entries // 16) * 16
+    pair = [dma((layers, number))] * 2
+    return pl.pallas_call(
+        partial(backward_kernel, groups),
+        out_shape=[
+            jax.ShapeDtypeStruct((layers, 2, half, width), wide),
+            jax.ShapeDtypeStruct((Z_SIZE, Y_SIZE, X_SIZE * C_SIZE, mod_rows, D), low),
+            jax.ShapeDtypeStruct((sum_rows, D), wide),
+        ],
+        in_specs=[vmem] * 6 + [anywhere] * 7,
+        out_specs=[vmem] * 3,
+        scratch_shapes=[
+            pltpu.VMEM((4, D, D), low),
+            pltpu.VMEM(rows, wide),
+            pltpu.VMEM(rows, wide),
+            pltpu.VMEM((3,) + rows, low),
+            pltpu.VMEM(rows, low),
+            pltpu.VMEM(rows, wide),
+            pltpu.VMEM(rows, wide),
+            pltpu.VMEM(rows, low),
+            pltpu.VMEM(rows, low),
+            pltpu.VMEM(rows, low),
+            pltpu.VMEM(rows, low),
+            pltpu.VMEM(rows, wide),
+            pltpu.VMEM((3,) + rows, low),
+            pltpu.VMEM((2, D, D), low),
+            pltpu.VMEM((images, entries, 1, D), wide),
+            pltpu.VMEM((mod_rows, D), wide),
+            pltpu.VMEM((mod_rows, D), low),
+            pltpu.VMEM((sum_rows, D), wide),
+            pltpu.VMEM((Z_SIZE, Y_SIZE, half, D), low),
+            pltpu.VMEM((Z_SIZE, Y_SIZE, half, D), low),
+            pltpu.VMEM((Z_SIZE, Y_SIZE, part, D), low),
+            pltpu.VMEM((Z_SIZE, most, D), low),
+            pltpu.VMEM((Z_SIZE - 1, most, D), low),
+            pltpu.VMEM((most, D), low),
+            pltpu.VMEM((sum_rows // 2, D), wide),
+            pltpu.VMEM((sum_rows // 2, D), wide),
+            pltpu.VMEM((sum_rows // 2, D), wide),
+            pltpu.VMEM((Z_SIZE, sum_rows // 2, D), wide),
+            dma((4,)),
+            dma((6,)),
+            dma((layers, number, FF_BLOCKS)),
+            dma((layers, number, FF_BLOCKS)),
+            dma((layers, number, FF_BLOCKS)),
+            *pair,
+            *pair,
+            dma((layers, number, Z_SIZE - 1)),
+            dma((layers, number, Z_SIZE - 1)),
+            *pair,
+            *pair,
+            dma((7,)),
+            dma((7,)),
+            dma((7,)),
+            dma((7,)),
+            dma,
+            regular((number,)),
+            regular((number,)),
+            regular((number,)),
+            regular((number, Z_SIZE - 1)),
+            regular((number,)),
+        ],
+        compiler_params=pltpu.CompilerParams(
+            collective_id=3, has_side_effects=True, vmem_limit_bytes=63 * 2**20
+        ),
+        name="blocks_backward",
+    )(grad_out, mods, biases, tokens_t, head_sums, head_mods, full, *kept)
+
+
+def pack_shard(w_qkv, w_proj, w_fc1, w_fc2):
+    pieces = [w_qkv[:, D * i : D * (i + 1)] for i in range(3)] + [w_proj]
+    pieces += [w_fc1[:, D * i : D * (i + 1)] for i in range(FF // D)] + [w_fc2]
+    return jnp.concatenate(pieces, axis=0).astype(jnp.bfloat16)
+
+
+def unpack_shard(packed, rows):
+    count = FF // D
+    blocks = [packed[:, rows * i : rows * (i + 1)] for i in range(4 + count)]
+    return (
+        jnp.concatenate(blocks[:3], axis=-1),
+        blocks[3],
+        jnp.concatenate(blocks[4:], axis=-1),
+        packed[:, rows * (4 + count) :],
+    )
+
+
 def local(
     latents,
     noise_field,
@@ -266,7 +1431,12 @@
     mod_shard = w_mod.astype(jnp.bfloat16)
 
     own_ids = jnp.stack([timesteps, labels, drop_mask]).reshape(3, number)
-    all_ids = lax.all_gather(own_ids, ("dp", "rep"), axis=0, tiled=False)
+    direct = (dp_size, rep_size) == (Z_SIZE * Y_SIZE, X_SIZE * C_SIZE) and rows_mod % 96 == 0
+    if direct:
+        tile = jnp.pad(own_ids, ((0, 8 - 3), (0, LANES - number))).astype(jnp.float32)
+        all_ids = gather_ids(tile)[:, :3, :number].astype(jnp.int32)
+    else:
+        all_ids = lax.all_gather(own_ids, ("dp", "rep"), axis=0, tiled=False)
     all_ids = all_ids.transpose(1, 0, 2).reshape(3, everyone * number)
     features = time_features(all_ids[0]).astype(jnp.bfloat16)
     hidden_t = product(features, time1_low) + pieces["time1_b"]
@@ -286,10 +1456,19 @@
         axis=1,
         keepdims=False,
     ).reshape(dp_size * number, rows_mod)
-    modulation = (
-        lax.psum_scatter(product(group_rows, mod_shard), "dp", scatter_dimension=0, tiled=True)
-        + pieces["mod_b"]
-    )
+    mod_part = product(group_rows, mod_shard)
+    if direct:
+        packed = jnp.stack(
+            [pack_shard(w_qkv[i], w_proj[i], w_fc1[i], w_fc2[i]) for i in range(LAYERS)]
+        )
+        heights = [(0, 384), (384, 384), (768, 384)]
+        groups = [(i, first, size) for i in range(LAYERS) for first, size in heights]
+        mod_part = mod_part.reshape(dp_size, -1, LANES)
+        packed_full, mod_sum = gather_weights(packed, mod_part, groups)
+        mod_sum = mod_sum.reshape(number, MOD)
+    else:
+        mod_sum = lax.psum_scatter(mod_part, "dp", scatter_dimension=0, tiled=True)
+    modulation = mod_sum + pieces["mod_b"]
 
     picker = (timesteps.reshape(-1)[:, None] == jnp.arange(STEPS_T)[None, :]).astype(jnp.float32)
     factors = jnp.dot(picker, roster.T, precision=HIGHEST)
@@ -300,10 +1479,17 @@
     residual = (product(tokens.reshape(-1, PDIM), patch_low) + pieces["patch_b"]).reshape(
         number, GRID * GRID, D
     ) + places
+    if direct:
+        mods = modulation.reshape(number, -1, 1, D)
+        biases = pieces["block_b"].reshape(LAYERS, -1, 1, D)
+        residual, *kept_blocks = run_forward(residual.reshape(-1, D), mods, biases, packed_full)
+        residual = residual.reshape(number, GRID * GRID, D)
     kept_all = []
     gathered_all = []
     spans_all = []
     for layer_index in range(LAYERS):
+        if direct:
+            break
         weights = tuple(
             lax.all_gather(w[layer_index].astype(jnp.bfloat16), "dp", axis=0, tiled=True)
             for w in (w_qkv, w_proj, w_fc1, w_fc2)
@@ -329,24 +1515,61 @@
     grad_final = product(grad_output, head_low.T).reshape(number, GRID * GRID, D)
     final_grads = [jnp.sum(grad_final, axis=1), jnp.sum(grad_final * normed_f, axis=1)]
     grad_res = norm_back(grad_final * (1.0 + final_scale), normed_f, inverse_f)
-    layer_spans = [None] * LAYERS
-    bias_grads = [None] * LAYERS
-    block_grads = [None] * LAYERS
-    for layer_index in reversed(range(LAYERS)):
-        grad_res, grads, grad_bias, grad_spans = layer_backward(
-            grad_res, spans_all[layer_index], gathered_all[layer_index], kept_all[layer_index]
+    if direct:
+        head_row = jnp.pad(jnp.append(grad_head_b, loss_own), (0, D - PDIM - 1))[None]
+        head_sums = jnp.concatenate([grad_head.T, head_row, jnp.zeros((PDIM - 1, D), jnp.float32)])
+        head_mods = jnp.stack(final_grads, axis=1)[:, :, None]
+        finals, mod_all, sums = run_backward(
+            grad_res.reshape(-1, D), mods, biases, tokens.reshape(-1, PDIM).T, head_sums, head_mods, packed_full, kept_blocks
         )
-        layer_spans[layer_index] = grad_spans
-        bias_grads[layer_index] = grad_bias
-        block_grads[layer_index] = tuple(
-            lax.psum_scatter(g, "dp", scatter_dimension=0, tiled=True) for g in grads
+        finals = finals.reshape(LAYERS, C_SIZE, -1, rows_mod // C_SIZE, D).transpose(0, 2, 1, 3, 4)
+        grad_qkv, grad_proj, grad_fc1, grad_fc2 = unpack_shard(finals.reshape(LAYERS, -1, D), rows_mod)
+        grad_mod = mod_all.reshape(everyone, -1, D)[:, : number * (MOD // D)].reshape(-1, MOD)
+        sum_patch = jnp.concatenate([sums[:PDIM], sums[2 * PDIM + 8 :][:1]]).reshape(-1)
+        sum_head = jnp.append(sums[PDIM : 2 * PDIM].T.reshape(-1), sums[2 * PDIM, :PDIM])
+        sum_bias = sums[3 * PDIM :].reshape(-1)
+        loss_total = sums[2 * PDIM, PDIM]
+    else:
+        layer_spans = [None] * LAYERS
+        bias_grads = [None] * LAYERS
+        block_grads = [None] * LAYERS
+        for layer_index in reversed(range(LAYERS)):
+            grad_res, grads, grad_bias, grad_spans = layer_backward(
+                grad_res, spans_all[layer_index], gathered_all[layer_index], kept_all[layer_index]
+            )
+            layer_spans[layer_index] = grad_spans
+            bias_grads[layer_index] = grad_bias
+            block_grads[layer_index] = tuple(
+                lax.psum_scatter(g, "dp", scatter_dimension=0, tiled=True) for g in grads
+            )
+
+        grad_start = grad_res.reshape(-1, D).astype(jnp.bfloat16)
+        grad_patch = product(tokens.reshape(-1, PDIM).T, grad_start)
+        grad_patch_b = jnp.sum(grad_start.astype(jnp.float32), axis=0)
+        own_sums = jnp.concatenate(
+            [
+                grad_patch.reshape(-1),
+                grad_patch_b,
+                grad_head.reshape(-1),
+                jnp.stack(bias_grads).reshape(-1),
+                grad_head_b,
+                loss_own[None],
+            ]
         )
-    grad_qkv, grad_proj, grad_fc1, grad_fc2 = lax.psum(
-        tuple(jnp.stack([block_grads[i][k] for i in range(LAYERS)]) for k in range(4)), "rep"
-    )
-
-    own_mod = jnp.concatenate(layer_spans + final_grads, axis=-1).astype(jnp.bfloat16)
-    grad_mod = lax.all_gather(own_mod, ("dp", "rep"), axis=0, tiled=True)
+        own_mod = jnp.concatenate(layer_spans + final_grads, axis=-1).astype(jnp.bfloat16)
+        grad_qkv, grad_proj, grad_fc1, grad_fc2 = lax.psum(
+            tuple(jnp.stack([block_grads[i][k] for i in range(LAYERS)]) for k in range(4)), "rep"
+        )
+        grad_mod = lax.all_gather(own_mod, ("dp", "rep"), axis=0, tiled=True)
+        summed = lax.psum(own_sums, ("dp", "rep"))
+        cut_patch = (PDIM + 1) * D
+        cut_head = cut_patch + D * PDIM
+        cut_bias = cut_head + LAYERS * (4 * D + FF)
+        loss_total = summed[cut_bias + PDIM]
+        sum_patch = summed[:cut_patch]
+        sum_head = jnp.append(summed[cut_patch:cut_head], summed[cut_bias : cut_bias + PDIM])
+        sum_bias = summed[cut_head:cut_bias]
+
     grad_wmod = product(silu_rows.T, grad_mod)
     grad_mod_b = jnp.sum(grad_mod.astype(jnp.float32), axis=0)
     cond_rows = lax.all_gather(product(grad_mod, mod_shard.T), "dp", axis=1, tiled=True)
@@ -359,38 +1582,17 @@
     grad_hidden_t = silu_time_pull(product(grad_cond, time2_low.T))[0].astype(jnp.bfloat16)
     grad_time1 = product(features.T, grad_hidden_t)
     grad_time1_b = jnp.sum(grad_hidden_t.astype(jnp.float32), axis=0)
-    grad_start = grad_res.reshape(-1, D).astype(jnp.bfloat16)
-    grad_patch = product(tokens.reshape(-1, PDIM).T, grad_start)
-    grad_patch_b = jnp.sum(grad_start.astype(jnp.float32), axis=0)
-    summed = lax.psum(
-        jnp.concatenate(
-            [
-                grad_patch.reshape(-1),
-                grad_patch_b,
-                grad_head.reshape(-1),
-                jnp.stack(bias_grads).reshape(-1),
-                grad_head_b,
-                loss_own[None],
-            ]
-        ),
-        ("dp", "rep"),
-    )
-    cut_patch = (PDIM + 1) * D
-    cut_head = cut_patch + D * PDIM
-    cut_bias = cut_head + LAYERS * (4 * D + FF)
-    loss_total = summed[cut_bias + PDIM]
     small_grad = jnp.concatenate(
         [
-            summed[:cut_patch],
+            sum_patch,
             grad_time1.reshape(-1),
             grad_time1_b,
             grad_time2.reshape(-1),
             grad_time2_b,
             grad_class.reshape(-1),
             grad_mod_b,
-            summed[cut_patch:cut_head],
-            summed[cut_bias : cut_bias + PDIM],
-            summed[cut_head:cut_bias],
+            sum_head,
+            sum_bias,
         ]
     )
     beta = 1.0 - STEP ** (-0.8)

time: 2330 us -> 688 us (0.30)
  waiting for transfers between devices: 1770 us -> 0.02 us
  Pallas kernels: 0 us -> 440 us
  matrix products: 184 us -> 18.2 us
  local copies, waits for them, and re-layouts: 155 us -> 93.1 us
  other arithmetic: 116 us -> 73.3 us
  blocking collectives: 74.2 us -> 34.2 us
    reduce_scatter x8 -> x0, waiting for transfers between devices: 1060 us -> none  [local(): lax.psum_scatter(g, 'dp', scatter_dimension=0, tiled=True)]
    all_gather x9 -> x0, waiting for transfers between devices: 498 us -> none  [the longest x8 441 us: local(): lax.all_gather(w[layer_index].astype(jnp.bfloat16), 'dp', axis=0, tiled=T...]
    pallas_call x0 -> x4, Pallas kernels: none -> 440 us  [the longest x1 218 us: run_backward(): pl.pallas_call(partial(backward_kernel, groups), out_shape=[jax.ShapeDtyp...]
    dot_general x37 -> x12, matrix products: 157 us -> 17.5 us  [product(): return jnp.dot(left, right, preferred_element_type=jnp.float32)]
    psum x2 -> x0, waiting for transfers between devices: 98.1 us -> none  [the longest x1 50.1 us: local(): lax.psum(jnp.concatenate([grad_patch.reshape(-1), grad_patch_b, grad_head...]
    psum x1, waiting for transfers between devices: 63.1 us -> 0.01 us  [local(): lax.psum(jnp.concatenate([entry[k].reshape(-1) for k in range(1, 5) for e...]
    unnamed x22 -> x1, waiting for transfers between devices: 44.9 us -> 0.02 us
    all_gather x1 -> x0, blocking collectives: 43.4 us -> none  [local(): all_ids = lax.all_gather(own_ids, ('dp', 'rep'), axis=0, tiled=False)]
  transfers between devices with their start and end apart: 21 -> 1, of which waited for: 21 -> 0; matrix products, arithmetic and copies ran while one was open for 11% -> 9% of each run, Pallas kernels for 0% -> 0%
where the time goes in v3:
time: 688 us; the launch traced here: 678 us
  Pallas kernels  440 us (64%)
  local copies, waits for them, and re-layouts  93.1 us (14%)
  other arithmetic  73.3 us (11%)
  blocking collectives  34.2 us (5%)
  between operations  19.3 us (3%)
  matrix products  18.2 us (3%)
    pallas_call x1, Pallas kernels, run_backward(): pl.pallas_call(partial(backward_kernel, groups), out_shape=[jax.ShapeDtyp...  218 us
    pallas_call x1, Pallas kernels, gather_weights(): pl.pallas_call(partial(gather_kernel, groups), out_shape=(jax.ShapeDtypeS...  161 us
    pallas_call x1, Pallas kernels, run_forward(): pl.pallas_call(forward_kernel, out_shape=[jax.ShapeDtypeStruct((tokens, D...  49.5 us
    all_gather x1, blocking collectives, local(): lax.all_gather(product(grad_mod, mod_shard.T), 'dp', axis=1, tiled=True)  34.2 us
    concatenate x1, local copies, waits for them, and re-layouts, local(): jnp.concatenate([sum_patch, grad_time1.reshape(-1), grad_time1_b, grad_ti...  31.2 us
    unnamed x185, local copies, waits for them, and re-layouts  20.6 us
    dot_general x12, matrix products, product(): return jnp.dot(left, right, preferred_element_type=jnp.float32)  17.5 us
    convert_element_type x5, other arithmetic, local(): new_weight.astype(jnp.bfloat16)  15.6 us
  transfers between devices with their start and end apart: 1, of which 0 were waited for; matrix products, arithmetic and copies ran while one was open for 9% of the time, Pallas kernels for 0%

profile of v3, /device:TPU:0, one launch (start us, length us, event | category | flops | bytes accessed | tf_op | source)
XLA Modules:
  0.0 678.3 jit_solution(17309090353028359423)
XLA Ops:
  7.3 4.5 multiply_reduce_fusion.2
  11.8 1.0 fusion.83
  13.0 1.3 slice.368
  15.1 12.1 %gather_ids.1 = f32[32,8,128]{2,1,0:T(8,128)} custom-call(f32[8,128]{1,0:T(8,128)} %pad_convert_fusion.own), custom_call_target="tpu_custom_call" | custom-call | tf_op jit(solution)/shard_map/gather_ids/pallas_call | solution.py:284
  28.3 0.9 slice.304
  31.2 1.4 fusion.84
  32.5 1.5 slice.306
  34.1 1.2 slice.310
  37.4 1.1 copy-done.33
  38.5 1.2 copy-done.32
  39.7 1.9 multiply_reduce_fusion.3
  42.1 1.9 convert_element_type.159
  44.5 1.7 convolution_add_fusion.2
  46.7 2.6 fusion.3
  49.5 1.6 reshape.681
  52.1 2.5 reshape.680
  54.6 2.0 fusion.7
  56.6 1.8 copy.70
  58.4 1.1 convert_element_type.149
  60.2 1.1 slice_dynamic-update-slice_fusion.1
  61.3 2.3 pad_maximum_fusion.packed
  63.7 160.8 %gather_weights.1 = (bf16[2,8,1152,768]{3,2,1,0:T(8,128)(2,1)S(1)}, f32[168,128]{1,0:T(8,128)S(1)}) custom-call(bf16[2,1152,768]{2,1,0:T(8,128)(2,1)S(1)} %pad_maximum_fusion.packed, f32[8,168,128]{2,1,0:T(8,128)S(1)} %reshape.686.parts), custom_call_target="tpu_custom_call" | custom-call | tf_op jit(solution)/shard_map/gather_weights/pallas_call | solution.py:417
  224.5 9.3 %copy-done.2 = bf16[2,8,1152,768]{3,2,1,0:T(8,128)(2,1)} copy-done((bf16[2,8,1152,768]{3,2,1,0:T(8,128)(2,1)}, bf16[2,8,1152,768]{3,2,1,0:T(8,128)(2,1)S(1)}, u32[]{:S(2)}) %copy-start.2) | copy-done | bytes 28311576
  234.6 1.9 multiply_sine_fusion.1
  236.8 1.5 bitcast_add_fusion.1.start
  238.3 49.5 %blocks_forward.1 = (f32[512,768]{1,0:T(8,128)}, f32[2,512,768]{2,1,0:T(8,128)}, bf16[2,3,512,768]{3,2,1,0:T(8,128)(2,1)}, bf16[2,512,768]{2,1,0:T(8,128)(2,1)},...) custom-call(f32[512,768]{1,0:T(8,128)} %bitcast_add_fusion.1.start, ...), custom_call_target="tpu_custom_call" | custom-call | tf_op jit(solution)/shard_map/blocks_forward/pallas_call | solution.py:677
  287.9 1.7 reduce_sum.393
  290.3 1.1 copy.73
  293.1 1.2 multiply_reduce_fusion.9
  296.5 1.6 subtract_multiply_fusion
  298.1 217.8 %blocks_backward.1 = (f32[2,2,576,768]{3,2,1,0:T(8,128)}, bf16[4,2,4,32,768]{4,3,2,1,0:T(8,128)(2,1)}, f32[64,768]{1,0:T(8,128)}) custom-call(f32[512,768]{1,0:T(8,128)} %bitcast.173, f32[2,14,1,768]{3,2,1,0:T(1,128)} %broadcast_add_fusion.1.mods, f32[2,8,1,768]{3,2,1,0:T(1,128)} %bitcast.176, bf16[16,512]{1,0:T(8,128)(2,1)} %bitcast.177, ...), custom_call_target="tpu_custom_call" | custom-call | tf_op jit(solution)/shard_map/blocks_backward/pallas_call | solution.py:1310
  516.0 3.5 copy.76
  519.5 1.6 add_reduce_fusion.2
  521.1 1.7 fusion.82
  522.8 1.5 copy-done.3
  524.3 1.7 multiply_reduce_fusion
  526.6 1.1 copy-done.16
  528.0 3.3 reshape.699
  531.3 2.8 add_reduce_fusion
  534.7 1.6 add_reduce_fusion.4
  536.5 1.2 copy-done.8
  539.1 1.4 add_reduce_fusion.6
  540.6 1.1 copy-done.10
  542.7 3.0 divide_reduce_fusion
  545.8 2.1 concatenate.104
  548.5 3.0 convolution_bitcast_fusion
  551.6 34.2 %all-gather = f32[8,96,64]{1,2,0:T(8,128)S(1)} all-gather(f32[1,96,64]{1,2,0:T(8,128)S(1)} %convolution_bitcast_fusion), channel_id=1, replica_groups=mesh['dp'=8,'rep'=4] {'dp'}, dimensions={0}, use_global_device_ids=true | all-gather | bytes 221184 | tf_op jit(solution)/shard_map/all_gather | solution.py:1575
  586.8 1.1 convert_reduce_fusion.2
  587.9 1.9 fusion.67
  591.0 1.3 slice_bitcast_fusion.15
  594.2 1.6 reshape.710
  597.4 31.2 %concatenate.106 = f32[861712]{0:T(1024)S(1)} concatenate(f32[13056]{0:T(1024)} %reshape.708, f32[196608]{0:T(1024)} %reshape.709, f32[768]{0:T(1024)} %get-tuple-element.76, f32[589824]{0:T(1024)} %reshape.710, f32[768]{0:T(1024)} %get-tuple-element.74, f32[25344]{0:T(1024)S(1)} %reshape.711, f32[10752]{0:T(1024)} %convert_reduce_fusion, f32[12288]{0:T(1024)} %reshape.712, ...), dimensions={0} | concatenate | bytes 6893696 | tf_op jit(solution)/shard_map/concatenate | solution.py:1585
  628.5 6.6 multiply_reduce_fusion.1
  636.6 6.1 fusion.68
  642.7 1.3 slice.311
  643.9 1.3 fusion.85
  645.9 1.5 fusion.33
  652.5 7.3 %fusion.71 = (bf16[96,10752]{1,0:T(8,128)(2,1)}, f32[96,10752]{1,0:T(8,128)}) fusion(f32[96,10752]{1,0:T(8,128)} %param.33, f32[]{:T(128)} %bitcast.48, f32[96,10752]{1,0:T(8,128)} %get-tuple-element.186, f32[]{:T(128)} %bitcast.46, f32[10752]{0:T(1024)S(1)} %get-tuple-element.81, f32[96]{0:T(128)S(1)} %copy-done.67, f32[]{:T(128)} %bitcast.45), kind=kLoop, calls=%fused_computation.222 | loop fusion | flops 7225344 | bytes 14494092 | tf_op jit(solution)/shard_map/convert_element_type | solution.py:1649
  659.9 1.1 fusion.55
  661.0 2.5 fusion.73
  663.5 1.1 copy-done.14
  664.7 2.5 fusion.74
  667.2 1.2 fusion.75
  669.0 2.0 fusion.76
  (283 shorter events, 29.5 us)
Async XLA Ops:
  7.2 43.8 %copy-start = (f32[2,1000]{1,0:T(2,128)S(1)}, f32[2,1000]{1,0:T(2,128)}, u32[]{:S(2)}) copy-start(f32[2,1000]{1,0:T(2,128)} %param.28) | copy-start | bytes 24004
  7.2 636.7 %all-reduce.4.cloned.1.call-start = ((), (), s32[]{:S(2)}) async-start(), calls=%async_computation | async-start | bytes 401408 | tf_op jit(solution)/shard_map/psum | solution.py:1620
  11.8 2.5 copy-start.80
  11.8 2.5 copy-start.81
  11.8 2.5 copy-start.82
  13.0 22.2 %copy-start.15 = (f32[2,96,2304]{2,1,0:T(8,128)S(1)}, f32[2,96,2304]{2,1,0:T(8,128)}, u32[]{:S(2)}) copy-start(f32[2,96,2304]{2,1,0:T(8,128)} %param.29) | copy-start | bytes 5308420
  28.1 7.3 %copy-start.30 = (f32[2,96,768]{2,1,0:T(8,128)S(1)}, f32[2,96,768]{2,1,0:T(8,128)}, u32[]{:S(2)}) copy-start(f32[2,96,768]{2,1,0:T(8,128)} %param.30) | copy-start | bytes 1769476
  37.1 2.6 copy-start.21
  39.7 2.4 copy-start.26
  44.1 2.5 copy-start.72
  44.3 4.9 copy-start.43
  44.5 4.7 copy-start.35
  46.5 2.7 copy-start.37
  46.6 2.6 copy-start.48
  46.7 2.7 copy-start.52
  49.3 2.7 copy-start.53
  51.0 5.5 copy-start.18
  54.6 5.6 copy-start.27
  59.4 177.3 %copy-start.42 = (bf16[512,16]{0,1:T(8,128)(2,1)}, bf16[512,16]{0,1:T(8,128)(2,1)S(1)}, u32[]{:S(2)}) copy-start(bf16[512,16]{0,1:T(8,128)(2,1)S(1)} %convert_element_type.149) | copy-start | bytes 49156
  63.7 170.9 %copy-start.68 = (f32[256]{0:T(256)S(1)}, f32[256]{0:T(256)}, u32[]{:S(2)}) copy-start(f32[256]{0:T(256)} %get-tuple-element.189) | copy-start | bytes 3076
  63.7 170.9 %copy-start.69 = (f32[256]{0:T(256)S(1)}, f32[256]{0:T(256)}, u32[]{:S(2)}) copy-start(f32[256]{0:T(256)} %get-tuple-element.190) | copy-start | bytes 3076
  63.7 170.9 %copy-start.75 = (f32[192]{0:T(256)S(1)}, f32[192]{0:T(256)}, u32[]{:S(2)}) copy-start(f32[192]{0:T(256)} %multiply_exponential_fusion) | copy-start | bytes 2308
  224.5 9.4 %copy-start.2 = (bf16[2,8,1152,768]{3,2,1,0:T(8,128)(2,1)}, bf16[2,8,1152,768]{3,2,1,0:T(8,128)(2,1)S(1)}, u32[]{:S(2)}) copy-start(bf16[2,8,1152,768]{3,2,1,0:T(8,128)(2,1)S(1)} %get-tuple-element.43.full) | copy-start | bytes 84934656
  287.9 2.4 copy-start.19
  521.1 3.2 copy-start.3
  524.3 14.1 %copy-start.24 = (f32[2,96,768]{2,1,0:T(8,128)}, f32[2,96,768]{2,1,0:T(8,128)S(1)}, u32[]{:S(2)}) copy-start(f32[2,96,768]{2,1,0:T(8,128)S(1)} %get-tuple-element.123) | copy-start | bytes 1769476
  528.0 3.3 copy-start.49
  531.3 2.8 copy-start.70
  531.3 3.0 copy-start.6
  534.2 126.7 %copy-start.54 = (f32[2,384]{1,0:T(2,128)}, f32[2,384]{1,0:T(2,128)S(1)}, u32[]{:S(2)}) copy-start(f32[2,384]{1,0:T(2,128)S(1)} %get-tuple-element.101) | copy-start | bytes 9220
  536.4 2.6 copy-start.28
  536.4 2.6 copy-start.29
  540.6 5.2 copy-start.63
  542.7 3.1 copy-start.66
  542.7 3.1 copy-start.71
  542.7 3.1 copy-start.74
  542.7 5.2 copy-start.45
  548.5 37.5 %copy-start.38 = (f32[64,768]{1,0:T(8,128)S(1)}, f32[64,768]{1,0:T(8,128)}, u32[]{:S(2)}) copy-start(f32[64,768]{1,0:T(8,128)} %copy-done.37) | copy-start | bytes 589828
  551.6 35.2 %copy-start.34 = (bf16[768,768]{1,0:T(8,128)(2,1)S(1)}, bf16[768,768]{1,0:T(8,128)(2,1)}, u32[]{:S(2)}) copy-start(bf16[768,768]{1,0:T(8,128)(2,1)} %convert_element_type.159) | copy-start | bytes 3538948
  551.6 35.2 %copy-start.36 = (f32[64,768]{1,0:T(8,128)S(1)}, f32[64,768]{1,0:T(8,128)}, u32[]{:S(2)}) copy-start(f32[64,768]{1,0:T(8,128)} %copy-done.35) | copy-start | bytes 589828
  587.9 5.1 copy-start.44
  591.0 3.2 copy-start.20
  594.2 2.5 copy-start.40
  628.5 8.0 %copy-start.5 = (f32[861712]{0:T(1024)}, f32[861712]{0:T(1024)S(1)}, u32[]{:S(2)}) copy-start(f32[861712]{0:T(1024)S(1)} %concatenate.106) | copy-start | bytes 10340548
  636.5 9.4 %copy-start.51 = (f32[10752]{0:T(1024)S(1)}, f32[10752]{0:T(1024)}, u32[]{:S(2)}) copy-start(f32[10752]{0:T(1024)} %param.43) | copy-start | bytes 129028
  636.5 14.7 %copy-start.65 = (f32[2,768]{1,0:T(2,128)S(1)}, f32[2,768]{1,0:T(2,128)}, u32[]{:S(2)}) copy-start(f32[2,768]{1,0:T(2,128)} %param.41) | copy-start | bytes 18436
  636.5 14.8 %copy-start.58 = (f32[2,2304]{1,0:T(2,128)S(1)}, f32[2,2304]{1,0:T(2,128)}, u32[]{:S(2)}) copy-start(f32[2,2304]{1,0:T(2,128)} %param.35) | copy-start | bytes 55300
  636.5 15.8 %copy-start.57 = (f32[2,3072]{1,0:T(2,128)S(1)}, f32[2,3072]{1,0:T(2,128)}, u32[]{:S(2)}) copy-start(f32[2,3072]{1,0:T(2,128)} %param.39) | copy-start | bytes 73732
  636.6 16.0 %copy-start.67 = (f32[96]{0:T(128)S(1)}, f32[96]{0:T(128)}, u32[]{:S(2)}) copy-start(f32[96]{0:T(128)} %copy-done.66) | copy-start | bytes 1156
  647.4 12.5 %copy-start.41 = (f32[10752]{0:T(1024)}, f32[10752]{0:T(1024)S(1)}, u32[]{:S(2)}) copy-start(f32[10752]{0:T(1024)S(1)} %get-tuple-element.81) | copy-start | bytes 129028
  651.4 9.6 %copy-start.55 = (f32[2,768]{1,0:T(2,128)}, f32[2,768]{1,0:T(2,128)S(1)}, u32[]{:S(2)}) copy-start(f32[2,768]{1,0:T(2,128)S(1)} %get-tuple-element.85) | copy-start | bytes 18436
  651.5 16.9 %copy-start.50 = (f32[2,2304]{1,0:T(2,128)}, f32[2,2304]{1,0:T(2,128)S(1)}, u32[]{:S(2)}) copy-start(f32[2,2304]{1,0:T(2,128)S(1)} %get-tuple-element.97) | copy-start | bytes 55300
  652.3 14.9 %copy-start.56 = (f32[2,768]{1,0:T(2,128)}, f32[2,768]{1,0:T(2,128)S(1)}, u32[]{:S(2)}) copy-start(f32[2,768]{1,0:T(2,128)S(1)} %get-tuple-element.93) | copy-start | bytes 18436
  652.5 11.0 %copy-start.47 = (f32[2,3072]{1,0:T(2,128)}, f32[2,3072]{1,0:T(2,128)S(1)}, u32[]{:S(2)}) copy-start(f32[2,3072]{1,0:T(2,128)S(1)} %get-tuple-element.89) | copy-start | bytes 73732
  652.5 8.5 %copy-start.7 = (f32[2,384,768]{2,1,0:T(8,128)S(1)}, f32[2,384,768]{2,1,0:T(8,128)}, u32[]{:S(2)}) copy-start(f32[2,384,768]{2,1,0:T(8,128)} %get-tuple-element.109) | copy-start | bytes 7077892
  652.5 8.5 %copy-start.22 = (f32[2,384,768]{2,1,0:T(8,128)S(1)}, f32[2,384,768]{2,1,0:T(8,128)}, u32[]{:S(2)}) copy-start(f32[2,384,768]{2,1,0:T(8,128)} %param.32) | copy-start | bytes 7077892
  661.0 2.5 copy-start.9
  661.0 3.6 copy-start.14
  661.0 3.6 copy-start.60
  664.7 2.5 copy-start.25
  664.7 2.5 copy-start.31
  664.7 2.6 copy-start.62
  664.7 3.8 copy-start.17
  668.5 2.6 copy-start.1
  (21 other events, 33.2 us)
Sparse Core Ops, SparseCore 0:
  548.0 72.9 all-reduce.3

commit v4 on v3

--- a/solution.py
+++ b/solution.py
@@ -260,189 +260,6 @@
     )
 
 
-def ids_kernel(own, full, send, receive, local):
-    dp, rep = lax.axis_index("dp"), lax.axis_index("rep")
-    dps, reps = Z_SIZE * Y_SIZE, X_SIZE * C_SIZE
-    offsets = [(i, j) for i in range(dps) for j in range(reps) if i or j]
-    peers = [((dp + i) % dps, (rep + j) % reps) for i, j in offsets]
-    meet(peers)
-    mine = dp * reps + rep
-    copies = [
-        push(own, full.at[mine], send.at[n], receive.at[n], peer) for n, peer in enumerate(peers)
-    ]
-    for copy in copies:
-        copy.start()
-    keep = pltpu.make_async_copy(own, full.at[mine], local)
-    keep.start()
-    keep.wait()
-    for copy in copies:
-        copy.wait()
-
-
-def gather_ids(own):
-    count = Z_SIZE * Y_SIZE * X_SIZE * C_SIZE
-    return pl.pallas_call(
-        ids_kernel,
-        out_shape=jax.ShapeDtypeStruct((count,) + own.shape, own.dtype),
-        in_specs=[pl.BlockSpec(memory_space=pltpu.VMEM)],
-        out_specs=pl.BlockSpec(memory_space=pltpu.VMEM),
-        scratch_shapes=[
-            pltpu.SemaphoreType.DMA((count - 1,)),
-            pltpu.SemaphoreType.DMA((count - 1,)),
-            pltpu.SemaphoreType.DMA,
-        ],
-        compiler_params=pltpu.CompilerParams(collective_id=1, has_side_effects=True),
-        name="gather_ids",
-    )(own)
-
-
-def gather_kernel(groups, packed, parts, full, summed, part_in, z_s, z_r, y_s, y_r, x_s, x_r, c_s, c_r, p_s, p_r, local):
-    z, y, x, c = place()
-    dp = z * Y_SIZE + y
-    dps = Z_SIZE * Y_SIZE
-    part_peers = [((dp + k) % dps, x * C_SIZE + c) for k in range(1, dps)]
-    across_y, across_x, sibling = device(z, 1 - y, x, c), device(z, y, 1 - x, c), device(z, y, x, 1 - c)
-    meet(part_peers + [across_x, sibling])
-    part_copies = [
-        push(parts.at[peer[0]], part_in.at[dp], p_s.at[k], p_r.at[k], peer)
-        for k, peer in enumerate(part_peers)
-    ]
-    for copy in part_copies:
-        copy.start()
-    keeps = []
-    for layer in range(LAYERS):
-        keep = pltpu.make_async_copy(packed.at[layer], full.at[layer, dp], local.at[layer])
-        keep.start()
-        keeps.append(keep)
-    started = []
-
-    def rows(group, third, count):
-        layer, first, size = groups[group]
-        step = size // 6
-        return pl.ds(pl.multiple_of(first + c * 3 * step + third * step, 16), count * step)
-
-    def source(k, other):
-        return ((z - k) % Z_SIZE) * Y_SIZE + (1 - y if other else y)
-
-    def piece(group, owner, third, count):
-        return full.at[groups[group][0], owner, rows(group, third, count)]
-
-    def go(source_ref, target_ref, send, receive, peer):
-        copy = push(source_ref, target_ref, send, receive, peer)
-        copy.start()
-        started.append(copy)
-
-    def first_hop(group):
-        own = packed.at[groups[group][0], rows(group, x, 2)]
-        target = piece(group, dp, x, 2)
-        go(own, target, y_s.at[group, 0], y_r.at[group, 0], across_y)
-        for k in range(1, Z_SIZE):
-            peer = device((z + k) % Z_SIZE, y, x, c)
-            go(own, target, z_s.at[group, k - 1], z_r.at[group, k - 1], peer)
-
-    def arrive(ref, send, receive, peer):
-        push(ref, ref, send, receive, peer).wait_recv()
-
-    def spread(group, index, owner):
-        third = piece(group, owner, 2 * x, 1)
-        go(third, third, x_s.at[group, index], x_r.at[group, index], across_x)
-        both = piece(group, owner, x, 2)
-        go(both, both, c_s.at[group, index], c_r.at[group, index], sibling)
-
-    def on_z(group, k):
-        ref = piece(group, source(k, False), x, 2)
-        arrive(ref, z_s.at[group, k - 1], z_r.at[group, k - 1], across_y)
-        go(ref, ref, y_s.at[group, k], y_r.at[group, k], across_y)
-        spread(group, k - 1, source(k, False))
-
-    def on_y(group, k):
-        ref = piece(group, source(k, True), x, 2)
-        arrive(ref, y_s.at[group, k], y_r.at[group, k], across_y)
-        spread(group, Z_SIZE - 1 + k, source(k, True))
-
-    def on_x(group, index):
-        owner = source(index + 1, False) if index < Z_SIZE - 1 else source(index - Z_SIZE + 1, True)
-        ref = piece(group, owner, 2 - 2 * x, 1)
-        arrive(ref, x_s.at[group, index], x_r.at[group, index], across_x)
-        slot = index + 2 * Z_SIZE - 1
-        go(ref, ref, c_s.at[group, slot], c_r.at[group, slot], sibling)
-
-    def on_c(group):
-        layer, first, size = groups[group]
-        step = size // 6
-        other = 1 - c
-        for index in range(2 * Z_SIZE - 1):
-            owner = source(index + 1, False) if index < Z_SIZE - 1 else source(index - Z_SIZE + 1, True)
-            for slot, third, count in ((index, x, 2), (index + 2 * Z_SIZE - 1, 2 - 2 * x, 1)):
-                start = pl.multiple_of(first + other * 3 * step + third * step, 16)
-                ref = full.at[layer, owner, pl.ds(start, count * step)]
-                arrive(ref, c_s.at[group, slot], c_r.at[group, slot], sibling)
-
-    first_hop(0)
-    count = len(groups)
-    for group in range(count + 1):
-        if group + 1 < count:
-            first_hop(group + 1)
-        events = []
-        if group < count:
-            events = [(on_y, group, 0)]
-            for k in range(1, Z_SIZE):
-                events += [(on_z, group, k), (on_y, group, k)]
-        for index in range(2 * Z_SIZE - 1):
-            if events:
-                step, *where = events[index]
-                step(*where)
-            if group > 0:
-                on_x(group - 1, index)
-        if group == 0:
-            for copy in part_copies:
-                copy.wait()
-            total = jnp.where(dp == 0, parts[0], part_in[0])
-            for k in range(1, dps):
-                total = total + jnp.where(dp == k, parts[k], part_in[k])
-            summed[...] = total
-    for group in range(count):
-        on_c(group)
-    for copy in started:
-        copy.wait_send()
-    for keep in keeps:
-        keep.wait()
-
-
-def gather_weights(packed, parts, groups):
-    layers, height, width = packed.shape
-    dps = Z_SIZE * Y_SIZE
-    count = len(groups)
-    dma = pltpu.SemaphoreType.DMA
-    return pl.pallas_call(
-        partial(gather_kernel, groups),
-        out_shape=(
-            jax.ShapeDtypeStruct((layers, dps, height, width), packed.dtype),
-            jax.ShapeDtypeStruct(parts.shape[1:], parts.dtype),
-        ),
-        in_specs=[pl.BlockSpec(memory_space=pl.ANY), pl.BlockSpec(memory_space=pltpu.VMEM)],
-        out_specs=(pl.BlockSpec(memory_space=pl.ANY), pl.BlockSpec(memory_space=pltpu.VMEM)),
-        scratch_shapes=[
-            pltpu.VMEM(parts.shape, parts.dtype),
-            dma((count, Z_SIZE - 1)),
-            dma((count, Z_SIZE - 1)),
-            dma((count, Z_SIZE)),
-            dma((count, Z_SIZE)),
-            dma((count, 2 * Z_SIZE - 1)),
-            dma((count, 2 * Z_SIZE - 1)),
-            dma((count, 4 * Z_SIZE - 2)),
-            dma((count, 4 * Z_SIZE - 2)),
-            dma((dps - 1,)),
-            dma((dps - 1,)),
-            dma((layers,)),
-        ],
-        compiler_params=pltpu.CompilerParams(
-            collective_id=2, has_side_effects=True, vmem_limit_bytes=16 * 2**20
-        ),
-        name="gather_weights",
-    )(packed, parts)
-
-
 GELU_A, GELU_B = 0.79788456, 0.044715
 FF_BLOCKS = FF // D
 TILE = 256
@@ -510,12 +327,11 @@
     return jnp.where(lanes, values, jnp.zeros_like(values))
 
 
-def attention_forward(projected, attended, images):
-    pairs = HEADS // 2
+def attention_forward(projected, attended, images, first_pair, pairs):
     size, width = GRID * GRID, 2 * D // HEADS
 
     def body(i, image):
-        rows, lanes = block_at(image, size), block_at(i, width)
+        rows, lanes = block_at(image, size), block_at(first_pair + i, width)
         query, keys, values = (projected[p, rows, lanes] for p in range(3))
         first = head_lanes(0)
         outs = []
@@ -556,15 +372,188 @@
     return block.reshape(D, block.shape[-1])
 
 
+class Pace:
+    RATE = 48e3
+    LATENCY = 2.2
+
+    def __init__(self):
+        self.now = 0.0
+        self.free = {}
+        self.entries = []
+
+    def send(self, link, count):
+        rate = 10 * self.RATE if link == "c" else self.RATE
+        self.free[link] = max(self.now, self.free.get(link, 0.0)) + count / rate
+        return self.free[link] + self.LATENCY
+
+    def add(self, ready, run):
+        self.entries.append([ready, len(self.entries), run])
+
+    def serve(self, entry):
+        cost, ready = entry[2]()
+        self.now += cost
+        if ready is None:
+            self.entries.remove(entry)
+        else:
+            entry[0] = ready
+
+    def spend(self, cost):
+        self.now += cost
+        while self.entries:
+            entry = min(self.entries, key=lambda e: e[:2])
+            if entry[0] > self.now:
+                return
+            self.serve(entry)
+
+    def next(self):
+        entry = min(self.entries, key=lambda e: e[:2])
+        self.now = max(self.now, entry[0])
+        self.serve(entry)
+
+    def until(self, done):
+        while not done():
+            self.next()
+
+    def drain(self):
+        while self.entries:
+            self.next()
+
+
+class Gather:
+    def __init__(self, pace, groups, spot, packed, full, semaphores, prepare, loads):
+        self.pace, self.groups, self.spot = pace, groups, spot
+        self.packed = packed
+        layers, owners, height, width = full.shape
+        self.full = full.reshape(layers, Z_SIZE, Y_SIZE, height, width)
+        self.sems, self.prepare, self.loads = semaphores, prepare, loads
+        z, y, x, c = spot
+        self.z_peers = [device((z + k) % Z_SIZE, y, x, c) for k in range(1, Z_SIZE)]
+        self.across_y, self.across_x = device(z, 1 - y, x, c), device(z, y, 1 - x, c)
+        self.sibling = device(z, y, x, 1 - c)
+        self.done, self.copies, self.keeps = set(), [], {}
+        self.waiting = list(range(len(groups)))
+
+    def rows(self, group, third, count, core):
+        _, first, size = self.groups[group]
+        step = size // 6
+        return pl.ds(pl.multiple_of(first + core * 3 * step + third * step, 16), count * step)
+
+    def size(self, group, count):
+        return self.groups[group][2] // 6 * count * D * 2
+
+    def sem(self, name, group, *index):
+        send, receive = self.sems[name]
+        return send.at[(group,) + index], receive.at[(group,) + index]
+
+    def go(self, source, target, sems, peer):
+        copy = push(source, target, sems[0], sems[1], peer)
+        copy.start()
+        self.copies.append(copy)
+
+    def arrive(self, ref, sems):
+        push(ref, ref, sems[0], sems[1], self.across_y).wait_recv()
+
+    def start(self):
+        z, y, x, c = self.spot
+        group = self.waiting.pop(0)
+        layer = self.groups[group][0]
+        self.prepare(group)
+        own = self.packed.at[layer, self.rows(group, x, 2, c)]
+        target = self.full.at[layer, z, y, self.rows(group, x, 2, c)]
+        for k in range(1, Z_SIZE):
+            self.go(own, target, self.sem("z", group, k - 1), self.z_peers[k - 1])
+        keep = pltpu.make_async_copy(own, target, self.sems["keep"].at[group])
+        keep.start()
+        self.keeps[group] = keep
+        stages = [self.on_z, self.on_y, self.on_x, self.on_c]
+        self.pace.add(
+            self.pace.send("z", 4 * self.size(group, 2)), lambda: (0.6, stages.pop(0)(group, layer))
+        )
+        return 1.4, self.pace.free["z"] - 9.0 if self.waiting else None
+
+    def on_z(self, group, layer):
+        z, y, x, c = self.spot
+        self.keeps[group].wait()
+        both, third = self.rows(group, x, 2, c), self.rows(group, 2 * x, 1, c)
+        for k in range(1, Z_SIZE):
+            self.arrive(self.full.at[layer, (z - k) % Z_SIZE, y, both], self.sem("z", group, k - 1))
+        ref = self.full.at[layer, :, y, both]
+        self.go(ref, ref, self.sem("y", group), self.across_y)
+        part = self.full.at[layer, :, y, third]
+        self.go(part, part, self.sem("x", group, 0), self.across_x)
+        self.go(ref, ref, self.sem("c", group, 0), self.sibling)
+        self.x_ready = self.pace.send("x", 4 * self.size(group, 1))
+        return self.pace.send("y", 4 * self.size(group, 2))
+
+    def on_y(self, group, layer):
+        z, y, x, c = self.spot
+        ref = self.full.at[layer, :, 1 - y, self.rows(group, x, 2, c)]
+        self.arrive(ref, self.sem("y", group))
+        part = self.full.at[layer, :, 1 - y, self.rows(group, 2 * x, 1, c)]
+        self.go(part, part, self.sem("x", group, 1), self.across_x)
+        self.go(ref, ref, self.sem("c", group, 1), self.sibling)
+        return self.pace.send("x", 4 * self.size(group, 1))
+
+    def on_x(self, group, layer):
+        z, y, x, c = self.spot
+        third = self.rows(group, 2 - 2 * x, 1, c)
+        for k, side in enumerate((y, 1 - y)):
+            self.arrive(self.full.at[layer, :, side, third], self.sem("x", group, k))
+        ref = self.full.at[layer, :, :, third]
+        self.go(ref, ref, self.sem("c", group, 2), self.sibling)
+        return self.pace.send("c", 8 * self.size(group, 1))
+
+    def on_c(self, group, layer):
+        z, y, x, c = self.spot
+        for k, side in enumerate((y, 1 - y)):
+            self.arrive(self.full.at[layer, :, side, self.rows(group, x, 2, 1 - c)], self.sem("c", group, k))
+        third = self.rows(group, 2 - 2 * x, 1, 1 - c)
+        self.arrive(self.full.at[layer, :, :, third], self.sem("c", group, 2))
+        self.done.add(group)
+        self.loads(group)
+        return None
+
+    def finish(self):
+        for copy in self.copies:
+            copy.wait_send()
+
+
+def silu(values):
+    return values / (1.0 + jnp.exp(-values))
+
+
+def conditions(ids, time1_w, time1_b, time2_w, time2_b, class_tab, hidden_t, condition):
+    rows, half = ids.shape[0], FREQ // 2
+    k = lax.broadcasted_iota(jnp.int32, (1, half), 1).astype(jnp.float32)
+    angles = ids[:, 0:1] * jnp.exp(-math.log(10000.0) * k / half)
+    features = jnp.concatenate([jnp.cos(angles), jnp.sin(angles)], axis=1).astype(jnp.bfloat16)
+    hidden = dot_nn(features, time1_w[...]) + time1_b
+    hidden_t[...] = hidden
+    chosen = jnp.where(ids[:, 2:3] == 1.0, float(CLASSES), ids[:, 1:2])
+    lane = lax.broadcasted_iota(jnp.int32, (rows, class_tab.shape[0]), 1).astype(jnp.float32)
+    picked = jnp.dot(
+        (lane == chosen).astype(jnp.float32), class_tab, precision=HIGHEST, preferred_element_type=jnp.float32
+    )
+    condition[...] = dot_nn(silu(hidden).astype(jnp.bfloat16), time2_w[...]) + time2_b + picked
+
+
 def forward_kernel(
-    start, mods, biases, full, out, x_h, proj_h, att_h, branch_a_h, middle_h, branch_b_h,
-    w_in, w_out, x_v, proj_v, att_v, branch_a, middle, branch_b, mixed, active, w_sem, save_sem,
+    groups, places_of, picked, places, ids, w_qkv, w_proj, w_fc1, w_fc2, w_mod, small, biases,
+    out, full, mods, ids_all, hidden_t, condition, x_h, proj_h, att_h, branch_a_h, middle_h, branch_b_h,
+    w_in, w_out, x_v, proj_v, att_v, branch_a, middle, branch_b, mixed, active,
+    mod_part, mod_y, mod_z, packed, raw, time1_w, time2_w, raw_sem, out_sem,
+    w_sem, save_sem, i_s, i_r, z_s, z_r, y_s, y_r, x_s, x_r, c_s, c_r, keep_sem, my_s, my_r, mz_s, mz_r,
 ):
-    tokens = start.shape[0]
-    images = mods.shape[0]
-    shard = w_in.shape[3]
-    deep = w_out.shape[3]
+    tokens = picked.shape[0]
+    images, entries = mods.shape[:2]
+    shard, deep = w_in.shape[3], w_out.shape[3]
+    ways = D // LANES
     count = 4 + FF_BLOCKS
+    spot = place()
+    z, y, x, c = spot
+    dps, reps = Z_SIZE * Y_SIZE, X_SIZE * C_SIZE
+    dp, rep = z * Y_SIZE + y, x * C_SIZE + c
+    pace = Pace()
 
     def load(layer, index):
         if index < count:
@@ -579,160 +568,304 @@
             w_sem.at[layer, index],
         )
 
-    order = [0, 1, 2, 3] + [i for b in range(FF_BLOCKS) for i in (4 + b, count + b)]
+    def loads(group):
+        layer, first, size = groups[group]
+        for index in range(count):
+            if first <= index * shard < first + size:
+                load(layer, index).start()
+        ends = {g for g, (at, begin, _) in enumerate(groups) if at == layer and begin >= count * shard}
+        if group in ends and ends <= gather.done:
+            for block in range(FF_BLOCKS):
+                load(layer, count + block).start()
+
+    def square(layer, index):
+        if index < 3:
+            return w_qkv.at[layer, :, pl.ds(index * D, D)]
+        if index == 3:
+            return w_proj.at[layer]
+        if index < count:
+            return w_fc1.at[layer, :, pl.ds((index - 4) * D, D)]
+        return w_fc2.at[layer, pl.ds((index - count) * shard, shard)]
+
+    def fetch(group):
+        if group < len(groups):
+            layer, first, size = groups[group]
+            slot = group % raw.shape[0]
+            for k in range(size // shard):
+                pltpu.make_async_copy(square(layer, first // shard + k), raw.at[slot, k], raw_sem.at[slot, k]).start()
+
+    def prepare(group):
+        layer, first, size = groups[group]
+        slot = group % raw.shape[0]
+        for k in range(size // shard):
+            pltpu.make_async_copy(square(layer, first // shard + k), raw.at[slot, k], raw_sem.at[slot, k]).wait()
+            packed[layer, pl.ds(first + k * shard, shard)] = raw[slot, k].astype(jnp.bfloat16)
+        fetch(group + raw.shape[0])
+
+    gather = Gather(
+        pace, groups, spot, packed, full,
+        {"z": (z_s, z_r), "y": (y_s, y_r), "x": (x_s, x_r), "c": (c_s, c_r), "keep": keep_sem}, prepare, loads,
+    )
+    for group in range(raw.shape[0]):
+        fetch(group)
+
+    def rows_of(name, k, first=0, size=None):
+        at, height = places_of[name]
+        return small[pl.ds((at + first) * ways + k, size or height, stride=ways)]
+
+    def piece(name):
+        return jnp.concatenate([rows_of(name, k) for k in range(ways)], axis=1)
+    offsets = [(i, j) for i in range(dps) for j in range(reps) if i or j]
+    everyone = [((dp + i) % dps, (rep + j) % reps) for i, j in offsets]
+    meet(everyone)
+    mine = dp * reps + rep
+    id_copies = [push(ids, ids_all.at[mine], i_s.at[n], i_r.at[n], peer) for n, peer in enumerate(everyone)]
+    for copy in id_copies:
+        copy.start()
+    ids_all[mine] = ids[...]
+    ready = []
+
+    def mods_start():
+        for copy in id_copies:
+            copy.wait_recv()
+        for k in range(ways):
+            lanes = pl.ds(k * LANES, LANES)
+            time1_w[:, lanes] = rows_of("time1_w", k).astype(jnp.bfloat16)
+            time2_w[:, lanes] = rows_of("time2_w", k).astype(jnp.bfloat16)
+        conditions(
+            ids_all[...].reshape(dps * reps * 8, LANES), time1_w, piece("time1_b"), time2_w, piece("time2_b"),
+            piece("class_tab"), hidden_t, condition,
+        )
+        chosen = [condition[pl.ds(pl.multiple_of((d * reps + rep) * 8, 8), 8)] for d in range(dps)]
+        group_c = silu(jnp.concatenate(chosen, axis=0)).astype(jnp.bfloat16)
+        rows_mod = w_mod.shape[0]
+        entry = lax.broadcasted_iota(jnp.int32, (D, rows_mod), 0)
+        lane = lax.broadcasted_iota(jnp.int32, (D, rows_mod), 1)
+        select = (entry == lane + dp * rows_mod).astype(jnp.bfloat16)
+        own = dot_nn(group_c, select).astype(jnp.bfloat16)
+        for k in range(entries):
+            value = dot_nn(own, w_mod[:, k * D : (k + 1) * D].astype(jnp.bfloat16))
+            for d in range(dps):
+                for image in range(images):
+                    row = 8 * d + image
+                    mod_part[d // Y_SIZE, d % Y_SIZE, pl.ds(image * entries + k, 1)] = value[row : row + 1]
+        gather.go(mod_part.at[:, 1 - y], mod_y, (my_s, my_r), gather.across_y)
+        return 9.0, pace.send("y", 4 * mod_part.shape[2] * D * 4)
+
+    def mods_across():
+        gather.arrive(mod_y, (my_s, my_r))
+        for k in range(Z_SIZE):
+            mod_y[k] = mod_y[k] + mod_part[k, y]
+        for k in range(1, Z_SIZE):
+            peer = (z + k) % Z_SIZE
+            gather.go(mod_y.at[peer], mod_z.at[z], (mz_s.at[k - 1], mz_r.at[k - 1]), gather.z_peers[k - 1])
+        return 1.5, pace.send("z", 4 * mod_part.shape[2] * D * 4)
+
+    def mods_end():
+        mod_z[z] = mod_y[z]
+        for k in range(1, Z_SIZE):
+            gather.arrive(mod_z.at[(z - k) % Z_SIZE], (mz_s.at[k - 1], mz_r.at[k - 1]))
+        value = (mod_z[0] + mod_z[1]) + (mod_z[2] + mod_z[3])
+        shift = piece("mod_b")
+        for image in range(images):
+            for k in range(entries):
+                row = image * entries + k
+                mods[image, k] = value[row : row + 1] + shift[k : k + 1]
+        ready.append(True)
+        return 1.0, None
+
+    steps = [mods_start, mods_across, mods_end]
+    pace.now = 8.0
+    for _ in range(2):
+        gather.start()
+    pace.add(pace.now + 3.0, lambda: steps.pop(0)())
+    pace.add(pace.free["z"] - 9.0, gather.start)
+
+    def need(layer, which):
+        index = min(which, count)
+        last = (index if index < count else count + deep // shard - 1) * shard
+        first = min(last, index * shard)
+        wanted = {
+            g for g, (at, begin, size) in enumerate(groups) if at == layer and first < begin + size and begin <= last
+        }
+        pace.until(lambda: wanted <= gather.done)
+        load(layer, which).wait()
+
+    patch_w = piece("patch_w").astype(jnp.bfloat16)
+    strip = PDIM // PATCH
+    weights = jnp.concatenate([patch_w[u * strip : (u + 1) * strip] for u in range(PATCH) for _ in range(GRID)], axis=0)
+    shift = piece("patch_b")
+    for image in range(images):
+        rows = pl.ds(image * GRID * GRID, GRID * GRID)
+        x_v[rows] = dot_nn(picked[rows], weights) + shift + places[...]
+    pace.spend(1.5)
+    saves = {}
+
+    def save(layer, source, target, index):
+        copy = pltpu.make_async_copy(source, target.at[layer], save_sem.at[layer, index])
+        copy.start()
+        saves[index] = copy
+
+    def reuse(index):
+        copy = saves.pop(index, None)
+        if copy is not None:
+            copy.wait()
+
     for layer in range(LAYERS):
-        for index in order:
-            load(layer, index).start()
-    x_v[0] = start[...]
-
-    def one_layer(layer):
-        saves = []
-
-        def save(source, target, index):
-            copy = pltpu.make_async_copy(source.at[layer], target.at[layer], save_sem.at[layer, index])
-            copy.start()
-            saves.append(copy)
-
         base = 6 * layer
-        x, projected, attended = x_v.at[layer], proj_v.at[layer], att_v.at[layer]
-        mid = middle.at[layer]
-        save(x_v, x_h, 0)
-        modulate(x, mods, base, base + 1, mixed, tokens)
+        save(layer, x_v, x_h, 0)
+        pace.until(lambda: ready)
+        modulate(x_v, mods, base, base + 1, mixed, tokens)
+        pace.spend(1.0)
+        reuse(1)
         for p in range(3):
-            load(layer, p).wait()
-
-            def project(i, p=p):
+            need(layer, p)
+
+            def project(i, p=p, layer=layer):
                 value = dot_nn(mixed[...], whole(w_in[layer, p, :, :, columns(i)]))
                 if p != 1:
                     value = value + biases[layer, p // 2, :, columns(i)]
-                projected[p, :, columns(i)] = value.astype(jnp.bfloat16)
+                proj_v[p, :, columns(i)] = value.astype(jnp.bfloat16)
 
             each(D // TILE, project)
-        save(proj_v, proj_h, 1)
-        attention_forward(projected, attended, images)
-        save(att_v, att_h, 2)
-        load(layer, 3).wait()
-
-        def first_branch(i):
-            value = dot_nn(attended[...], whole(w_in[layer, 3, :, :, columns(i)]))
+            pace.spend(1.1)
+        save(layer, proj_v, proj_h, 1)
+        reuse(2)
+        for pair in range(0, HEADS // 2, 2):
+            attention_forward(proj_v, att_v, images, pair, 2)
+            pace.spend(2.3)
+        save(layer, att_v, att_h, 2)
+        reuse(3)
+        reuse(4)
+        need(layer, 3)
+
+        def first_branch(i, layer=layer, base=base):
+            value = dot_nn(att_v[...], whole(w_in[layer, 3, :, :, columns(i)]))
             value = value + biases[layer, 2, :, columns(i)]
-            branch_a[layer, :, columns(i)] = value
+            branch_a[:, columns(i)] = value
             for image in range(images):
                 rows = pl.ds(image * GRID * GRID, GRID * GRID)
                 part = value[image * GRID * GRID : (image + 1) * GRID * GRID]
-                mid[rows, columns(i)] = x[rows, columns(i)] + mods[image, base + 2, :, columns(i)] * part
+                middle[rows, columns(i)] = x_v[rows, columns(i)] + mods[image, base + 2, :, columns(i)] * part
 
         each(D // TILE, first_branch)
-        save(branch_a, branch_a_h, 3)
-        save(middle, middle_h, 4)
-        modulate(mid, mods, base + 3, base + 4, mixed, tokens)
+        save(layer, branch_a, branch_a_h, 3)
+        save(layer, middle, middle_h, 4)
+        modulate(middle, mods, base + 3, base + 4, mixed, tokens)
+        pace.spend(2.3)
         for block in range(FF_BLOCKS):
-            load(layer, 4 + block).wait()
-
-            def expand(i, block=block):
+            need(layer, 4 + block)
+
+            def expand(i, block=block, layer=layer):
                 hidden = dot_nn(mixed[...], whole(w_in[layer, 4 + block, :, :, columns(i)]))
                 hidden = hidden + biases[layer, 3 + block, :, columns(i)]
                 inner = jnp.tanh(GELU_A * (hidden + GELU_B * hidden * hidden * hidden))
-                active[:, columns(i)] = (0.5 * hidden * (1.0 + inner)).astype(jnp.bfloat16)
+                active[block, :, columns(i)] = (0.5 * hidden * (1.0 + inner)).astype(jnp.bfloat16)
 
             each(D // TILE, expand)
-            load(layer, count + block).wait()
-
-            def contract(i, block=block):
-                value = dot_nn(active[...], whole(w_out[layer, block, :, :, columns(i)]))
+            pace.spend(2.2)
+        reuse(5)
+        for block in range(FF_BLOCKS):
+            need(layer, count + block)
+
+            def contract(i, block=block, layer=layer):
+                value = dot_nn(active[block], whole(w_out[layer, block, :, :, columns(i)]))
                 if block == 0:
-                    branch_b[layer, :, columns(i)] = value + biases[layer, 3 + FF_BLOCKS, :, columns(i)]
+                    branch_b[:, columns(i)] = value + biases[layer, 3 + FF_BLOCKS, :, columns(i)]
                 else:
-                    branch_b[layer, :, columns(i)] += value
+                    branch_b[:, columns(i)] += value
 
             each(D // TILE, contract)
-        save(branch_b, branch_b_h, 5)
-
-        def finish(rows, image):
-            value = mid[rows] + mods[image, base + 5] * branch_b[layer, rows]
-            out[rows] = value
-
-            @pl.when(layer + 1 < LAYERS)
-            def _():
-                x_v[layer + 1, rows] = value
+            pace.spend(1.1)
+        save(layer, branch_b, branch_b_h, 5)
+        reuse(0)
+
+        def finish(rows, image, base=base):
+            x_v[rows] = middle[rows] + mods[image, base + 5] * branch_b[rows]
 
         row_blocks(tokens, finish)
-        for copy in saves:
-            copy.wait()
-
-    each(LAYERS, one_layer)
-
-
-def run_forward(start, mods, biases, full):
-    tokens = start.shape[0]
-    layers, owners, height, width = full.shape
+        pace.spend(1.0)
+    last = pltpu.make_async_copy(x_v, out, out_sem)
+    last.start()
+    pace.drain()
+    for copy in saves.values():
+        copy.wait()
+    last.wait()
+    gather.finish()
+    for copy in id_copies:
+        copy.wait_send()
+
+
+def run_forward(picked, places, ids, w_qkv, w_proj, w_fc1, w_fc2, w_mod, small, places_of, biases, images):
+    tokens = picked.shape[0]
+    layers = w_qkv.shape[0]
+    owners, everyone = Z_SIZE * Y_SIZE, Z_SIZE * Y_SIZE * X_SIZE * C_SIZE
     shard, deep = D // owners, FF // owners
+    height, width = (4 + FF_BLOCKS) * shard + deep, D
     wide, low = jnp.float32, jnp.bfloat16
+    entries = MOD // D
+    mod_rows = -(-images * entries // 8) * 8
     keep = [
         ((tokens, D), wide), ((3, tokens, D), low), ((tokens, D), low),
         ((tokens, D), wide), ((tokens, D), wide), ((tokens, D), wide),
     ]
+    groups = [(layer, first, 2 * shard) for layer in range(layers) for first in range(0, height, 2 * shard)]
+    number = len(groups)
+    dma = pltpu.SemaphoreType.DMA
     vmem, anywhere = pl.BlockSpec(memory_space=pltpu.VMEM), pl.BlockSpec(memory_space=pl.ANY)
-    kept = [jax.ShapeDtypeStruct((layers,) + shape, kind) for shape, kind in keep]
+    outs = [
+        jax.ShapeDtypeStruct((tokens, D), wide),
+        jax.ShapeDtypeStruct((layers, owners, height, width), low),
+        jax.ShapeDtypeStruct((images, entries, 1, D), wide),
+        jax.ShapeDtypeStruct((everyone,) + ids.shape, wide),
+        jax.ShapeDtypeStruct((everyone * ids.shape[0], D), wide),
+        jax.ShapeDtypeStruct((everyone * ids.shape[0], D), wide),
+    ]
     return pl.pallas_call(
-        forward_kernel,
-        out_shape=[jax.ShapeDtypeStruct((tokens, D), wide)] + kept,
-        in_specs=[vmem, vmem, vmem, anywhere],
-        out_specs=[vmem] + [anywhere] * len(keep),
+        partial(forward_kernel, groups, places_of),
+        out_shape=outs + [jax.ShapeDtypeStruct((layers,) + shape, kind) for shape, kind in keep],
+        in_specs=[vmem] * 3 + [anywhere] * 4 + [vmem] * 3,
+        out_specs=[anywhere, anywhere, vmem, vmem, vmem, vmem] + [anywhere] * len(keep),
         scratch_shapes=[
             pltpu.VMEM((layers, 4 + FF_BLOCKS, owners, shard, D), low),
             pltpu.VMEM((layers, FF_BLOCKS, D // deep, deep, D), low),
         ]
-        + [pltpu.VMEM(entry.shape, entry.dtype) for entry in kept]
+        + [pltpu.VMEM(shape, kind) for shape, kind in keep]
         + [
             pltpu.VMEM((tokens, D), low),
-            pltpu.VMEM((tokens, D), low),
-            pltpu.SemaphoreType.DMA((layers, 4 + 2 * FF_BLOCKS)),
-            pltpu.SemaphoreType.DMA((layers, len(keep))),
+            pltpu.VMEM((FF_BLOCKS, tokens, D), low),
+            pltpu.VMEM((Z_SIZE, Y_SIZE, mod_rows, D), wide),
+            pltpu.VMEM((Z_SIZE, mod_rows, D), wide),
+            pltpu.VMEM((Z_SIZE, mod_rows, D), wide),
+            pltpu.VMEM((layers, height, width), low),
+            pltpu.VMEM((3, 2, shard, D), wide),
+            pltpu.VMEM((FREQ, D), low),
+            pltpu.VMEM((D, D), low),
+            dma((3, 2)),
+            dma,
+            dma((layers, 4 + 2 * FF_BLOCKS)),
+            dma((layers, len(keep))),
+            dma((everyone - 1,)),
+            dma((everyone - 1,)),
+            dma((number, Z_SIZE - 1)),
+            dma((number, Z_SIZE - 1)),
+            dma((number,)),
+            dma((number,)),
+            dma((number, 2)),
+            dma((number, 2)),
+            dma((number, 3)),
+            dma((number, 3)),
+            dma((number,)),
+            dma,
+            dma,
+            dma((Z_SIZE - 1,)),
+            dma((Z_SIZE - 1,)),
         ],
-        compiler_params=pltpu.CompilerParams(vmem_limit_bytes=62 * 2**20),
+        compiler_params=pltpu.CompilerParams(
+            collective_id=2, has_side_effects=True, vmem_limit_bytes=63 * 2**20
+        ),
         name="blocks_forward",
-    )(start, mods, biases, full)
-
-
-class Pace:
-    RATE = 48e3
-    LATENCY = 2.2
-
-    def __init__(self):
-        self.now = 0.0
-        self.free = {}
-        self.entries = []
-
-    def send(self, link, count):
-        rate = 10 * self.RATE if link == "c" else self.RATE
-        self.free[link] = max(self.now, self.free.get(link, 0.0)) + count / rate
-        return self.free[link] + self.LATENCY
-
-    def add(self, ready, run):
-        self.entries.append([ready, len(self.entries), run])
-
-    def serve(self, entry):
-        cost, ready = entry[2]()
-        self.now += cost
-        if ready is None:
-            self.entries.remove(entry)
-        else:
-            entry[0] = ready
-
-    def spend(self, cost):
-        self.now += cost
-        while self.entries:
-            entry = min(self.entries, key=lambda e: e[:2])
-            if entry[0] > self.now:
-                return
-            self.serve(entry)
-
-    def drain(self):
-        while self.entries:
-            entry = min(self.entries, key=lambda e: e[:2])
-            self.now = max(self.now, entry[0])
-            self.serve(entry)
+    )(picked, places, ids, w_qkv, w_proj, w_fc1, w_fc2, w_mod, small, biases)
 
 
 class Reduction:
@@ -1032,16 +1165,16 @@
 
 
 def backward_kernel(
-    groups, grad_out, mods, biases, tokens_t, head_sums, head_mods, full,
+    groups, count_all, x_last, mods, biases, picked, wanted, head_w, head_b, full,
     x_h, proj_h, att_h, branch_a_h, middle_h, branch_b_h,
     finals, mods_all, sums_out,
     w_v, grad_x, x_v, proj_v, att_v, branch, middle, mixed, grad_b, active, grad_hidden, grad_mixed,
     grad_projected, stage, mods_acc, mods_tile, mods_low, sums,
     held, from_c, from_x, from_y, from_z, from_fin, small_c, small_x, small_y, small_z,
-    w_sem, load_sem, keep_sem, c_s, c_r, x_s, x_r, y_s, y_r, z_s, z_r, e_s, e_r, f_s, f_r,
+    w_sem, load_sem, last_sem, keep_sem, c_s, c_r, x_s, x_r, y_s, y_r, z_s, z_r, e_s, e_r, f_s, f_r,
     v_s, v_r, m_s, m_r, local, cred_c, cred_x, cred_y, cred_z, cred_e,
 ):
-    tokens = grad_out.shape[0]
+    tokens = x_last.shape[0]
     images = mods.shape[0]
     owners = full.shape[1]
     shard, deep = D // owners, FF // owners
@@ -1083,17 +1216,43 @@
     def total(values):
         return jnp.sum(values, axis=0, keepdims=True)
 
+    last_copy = pltpu.make_async_copy(x_last, grad_x, last_sem)
+    last_copy.start()
     for at in range(slots):
         fetch(at)
-    reduction_peers = reduction.peers()
-    meet(reduction_peers)
+    meet(reduction.peers())
     sums[...] = jnp.zeros_like(sums)
-    sums[pl.ds(PDIM, 2 * PDIM)] = head_sums[...]
     mods_acc[...] = jnp.zeros_like(mods_acc)
-    for image in range(images):
-        for k in range(2):
-            mods_acc[image, 6 * LAYERS + k] = head_mods[image, k]
-    grad_x[...] = grad_out[...]
+    last_copy.wait()
+    final = 6 * LAYERS
+    modulate(grad_x, mods, final, final + 1, mixed, tokens)
+    picks, wide = wanted.shape[1], head_w.shape[1]
+    strip = PDIM // PATCH
+    pixel = lax.broadcasted_iota(jnp.int32, (picks, wide), 0)
+    entry = lax.broadcasted_iota(jnp.int32, (picks, wide), 1)
+    select = (entry == pixel // (picks // PATCH) * strip + pixel % strip).astype(jnp.float32)
+    target = jnp.dot(wanted[...], select, precision=HIGHEST, preferred_element_type=jnp.float32)
+    error = dot_nn(mixed[...], head_w[...]) + head_b[...] - target
+    grad_low = (error * (2.0 / count_all)).astype(jnp.bfloat16)
+    sums[pl.ds(PDIM, PDIM)] = dot_tn(grad_low, mixed[...])[:PDIM]
+    lane = lax.broadcasted_iota(jnp.int32, (1, wide), 1)
+    sums[pl.ds(2 * PDIM, 1), pl.ds(0, wide)] = jnp.where(
+        lane == PDIM, jnp.sum(error * error), total(grad_low.astype(jnp.float32))
+    )
+    for i in range(D // TILE):
+        grad_mixed[:, columns(i)] = dot_nt(grad_low, head_w[columns(i)])
+
+    def head(rows, image):
+        grad = grad_mixed[rows]
+        normed, inverse = centre(grad_x[rows])
+        mods_acc[image, final] += total(grad)
+        mods_acc[image, final + 1] += total(grad * normed)
+        grad = grad * (1.0 + mods[image, final + 1])
+        grad_x[rows] = inverse * (
+            grad - jnp.mean(grad, axis=-1, keepdims=True) - normed * jnp.mean(grad * normed, axis=-1, keepdims=True)
+        )
+
+    row_blocks(tokens, head)
     busy = [[], []]
     turn = [0]
 
@@ -1266,7 +1425,13 @@
         sums[pl.ds(2 * PDIM + 8, 1)] += total(low.astype(jnp.float32))
 
     row_blocks(tokens, patch)
-    sums[pl.ds(0, PDIM)] = dot_nn(tokens_t[...], grad_b[...])
+    value = dot_tn(picked[...], grad_b[...])
+    for u in range(PATCH):
+        first = u * strip * GRID
+        part = value[first : first + strip]
+        for j in range(1, GRID):
+            part = part + value[first + j * strip : first + (j + 1) * strip]
+        sums[pl.ds(u * strip, strip)] = part
     mods_tile[...] = jnp.zeros_like(mods_tile)
     entries = mods.shape[1]
     for image in range(images):
@@ -1284,8 +1449,8 @@
             wait()
 
 
-def run_backward(grad_out, mods, biases, tokens_t, head_sums, head_mods, full, kept):
-    tokens = grad_out.shape[0]
+def run_backward(count_all, x_last, mods, biases, picked, wanted, head_w, head_b, full, kept):
+    tokens = x_last.shape[0]
     images, entries = mods.shape[:2]
     layers, owners, height, width = full.shape
     shard = D // owners
@@ -1308,13 +1473,13 @@
     mod_rows = -(-images * entries // 16) * 16
     pair = [dma((layers, number))] * 2
     return pl.pallas_call(
-        partial(backward_kernel, groups),
+        partial(backward_kernel, groups, count_all),
         out_shape=[
             jax.ShapeDtypeStruct((layers, 2, half, width), wide),
             jax.ShapeDtypeStruct((Z_SIZE, Y_SIZE, X_SIZE * C_SIZE, mod_rows, D), low),
             jax.ShapeDtypeStruct((sum_rows, D), wide),
         ],
-        in_specs=[vmem] * 6 + [anywhere] * 7,
+        in_specs=[anywhere] + [vmem] * 6 + [anywhere] * 7,
         out_specs=[vmem] * 3,
         scratch_shapes=[
             pltpu.VMEM((4, D, D), low),
@@ -1347,6 +1512,7 @@
             pltpu.VMEM((Z_SIZE, sum_rows // 2, D), wide),
             dma((4,)),
             dma((6,)),
+            dma,
             dma((layers, number, FF_BLOCKS)),
             dma((layers, number, FF_BLOCKS)),
             dma((layers, number, FF_BLOCKS)),
@@ -1371,13 +1537,106 @@
             collective_id=3, has_side_effects=True, vmem_limit_bytes=63 * 2**20
         ),
         name="blocks_backward",
-    )(grad_out, mods, biases, tokens_t, head_sums, head_mods, full, *kept)
-
-
-def pack_shard(w_qkv, w_proj, w_fc1, w_fc2):
-    pieces = [w_qkv[:, D * i : D * (i + 1)] for i in range(3)] + [w_proj]
-    pieces += [w_fc1[:, D * i : D * (i + 1)] for i in range(FF // D)] + [w_fc2]
-    return jnp.concatenate(pieces, axis=0).astype(jnp.bfloat16)
+    )(x_last, mods, biases, picked, wanted, head_w, head_b, full, *kept)
+
+
+def exchange_kernel(cond, stats, cond_all, total, pieces, c_s, c_r, p_s, p_r, g_s, g_r, r_s, r_r):
+    dp, rep = lax.axis_index("dp"), lax.axis_index("rep")
+    dps, reps = Z_SIZE * Y_SIZE, X_SIZE * C_SIZE
+    dp_peers = [((dp + k) % dps, rep) for k in range(1, dps)]
+    rep_peers = [(dp, (rep + k) % reps) for k in range(1, reps)]
+    meet(dp_peers + rep_peers)
+    quarter = stats.shape[0] // reps
+    size = quarter // dps
+    copies = []
+
+    def go(source, target, sems, index, peer):
+        copy = push(source, target, sems[0].at[index], sems[1].at[index], peer)
+        copy.start()
+        copies.append(copy)
+        return copy
+
+    def part(owner):
+        return pl.ds(pl.multiple_of(rep * quarter + owner * size, 8), size)
+
+    first = [go(stats.at[part(peer[0])], pieces.at[dp], (p_s, p_r), k, peer) for k, peer in enumerate(dp_peers)]
+    spread = [go(cond, cond_all.at[dp], (c_s, c_r), k, peer) for k, peer in enumerate(dp_peers)]
+    cond_all[dp] = cond[...]
+    pieces[dp] = stats[part(dp)]
+    for copy in first:
+        copy.wait_recv()
+    value = pieces[0]
+    for k in range(1, dps):
+        value = value + pieces[k]
+    total[part(dp)] = value
+    own = total.at[part(dp)]
+    second = [go(own, own, (g_s, g_r), k, peer) for k, peer in enumerate(dp_peers)]
+    for copy in second:
+        copy.wait_recv()
+    own = total.at[pl.ds(pl.multiple_of(rep * quarter, 8), quarter)]
+    third = [go(own, own, (r_s, r_r), k, peer) for k, peer in enumerate(rep_peers)]
+    for copy in third + spread:
+        copy.wait_recv()
+    for copy in copies:
+        copy.wait_send()
+
+
+def exchange(cond, stats):
+    dps, reps = Z_SIZE * Y_SIZE, X_SIZE * C_SIZE
+    vmem = pl.BlockSpec(memory_space=pltpu.VMEM)
+    dma = pltpu.SemaphoreType.DMA
+    return pl.pallas_call(
+        exchange_kernel,
+        out_shape=[
+            jax.ShapeDtypeStruct((dps,) + cond.shape, cond.dtype),
+            jax.ShapeDtypeStruct(stats.shape, stats.dtype),
+        ],
+        in_specs=[vmem, vmem],
+        out_specs=[vmem, vmem],
+        scratch_shapes=[pltpu.VMEM((dps, stats.shape[0] // (dps * reps), LANES), stats.dtype)]
+        + [dma((dps - 1,))] * 6
+        + [dma((reps - 1,))] * 2,
+        compiler_params=pltpu.CompilerParams(collective_id=4, has_side_effects=True),
+        name="exchange_sums",
+    )(cond, stats)
+
+
+def line_up_kernel(offsets, *refs):
+    pieces, (first, tail), out, spread = refs[: len(offsets)], refs[len(offsets) : -2], refs[-2], refs[-1]
+    ways = D // LANES
+    for piece, offset in zip(pieces, offsets):
+        rows = piece.shape[0]
+        for k in range(ways):
+            out[pl.ds(ways * offset + k, rows, stride=ways)] = piece[:, k * LANES : (k + 1) * LANES]
+    rows = tail.shape[0] * ways
+    for k in range(ways):
+        spread[pl.ds(k, tail.shape[0], stride=ways)] = tail[:, k * LANES : (k + 1) * LANES]
+    moved = pltpu.roll(spread[...], PDIM, 1)
+    lane = lax.broadcasted_iota(jnp.int32, (rows, LANES), 1)
+    spread[pl.ds(1, rows - 1)] = moved[: rows - 1]
+    spread[pl.ds(0, 1)] = first[...]
+    start = out.shape[0] - rows - 1
+    out[pl.ds(start, rows)] = jnp.where(lane >= PDIM, moved, spread[...])
+    out[pl.ds(start + rows, 1)] = moved[rows - 1 :]
+
+
+def line_up(pieces, first, tail):
+    offsets, at = [], 0
+    for piece in pieces:
+        offsets.append(at)
+        at += piece.shape[0]
+    ways = D // LANES
+    vmem = pl.BlockSpec(memory_space=pltpu.VMEM)
+    count = (at + tail.shape[0]) * ways + 1
+    return pl.pallas_call(
+        partial(line_up_kernel, offsets),
+        out_shape=jax.ShapeDtypeStruct((count, LANES), jnp.float32),
+        in_specs=[vmem] * (len(pieces) + 2),
+        out_specs=vmem,
+        scratch_shapes=[pltpu.VMEM((tail.shape[0] * ways, LANES), jnp.float32)],
+        compiler_params=pltpu.CompilerParams(vmem_limit_bytes=32 * 2**20),
+        name="line_up",
+    )(*pieces, first, tail)
 
 
 def unpack_shard(packed, rows):
@@ -1430,106 +1689,117 @@
     head_low = pieces["head_w"].astype(jnp.bfloat16)
     mod_shard = w_mod.astype(jnp.bfloat16)
 
-    own_ids = jnp.stack([timesteps, labels, drop_mask]).reshape(3, number)
     direct = (dp_size, rep_size) == (Z_SIZE * Y_SIZE, X_SIZE * C_SIZE) and rows_mod % 96 == 0
-    if direct:
-        tile = jnp.pad(own_ids, ((0, 8 - 3), (0, LANES - number))).astype(jnp.float32)
-        all_ids = gather_ids(tile)[:, :3, :number].astype(jnp.int32)
-    else:
-        all_ids = lax.all_gather(own_ids, ("dp", "rep"), axis=0, tiled=False)
-    all_ids = all_ids.transpose(1, 0, 2).reshape(3, everyone * number)
-    features = time_features(all_ids[0]).astype(jnp.bfloat16)
-    hidden_t = product(features, time1_low) + pieces["time1_b"]
-    silu_t = jax.nn.silu(hidden_t).astype(jnp.bfloat16)
-    chosen = jnp.where(all_ids[2] == 1, CLASSES, all_ids[1])
-    onehot = (chosen[:, None] == jnp.arange(CLASSES + 1)[None, :]).astype(jnp.float32)
-    condition = (
-        product(silu_t, time2_low)
-        + pieces["time2_b"]
-        + jnp.dot(onehot, pieces["class_tab"], precision=HIGHEST)
-    )
-    silu_c = jax.nn.silu(condition).astype(jnp.bfloat16)
-    silu_rows = lax.dynamic_slice_in_dim(silu_c, first_row, rows_mod, axis=1)
-    group_rows = lax.dynamic_index_in_dim(
-        silu_rows.reshape(dp_size, rep_size, number, rows_mod),
-        lax.axis_index("rep"),
-        axis=1,
-        keepdims=False,
-    ).reshape(dp_size * number, rows_mod)
-    mod_part = product(group_rows, mod_shard)
-    if direct:
-        packed = jnp.stack(
-            [pack_shard(w_qkv[i], w_proj[i], w_fc1[i], w_fc2[i]) for i in range(LAYERS)]
-        )
-        heights = [(0, 384), (384, 384), (768, 384)]
-        groups = [(i, first, size) for i in range(LAYERS) for first, size in heights]
-        mod_part = mod_part.reshape(dp_size, -1, LANES)
-        packed_full, mod_sum = gather_weights(packed, mod_part, groups)
-        mod_sum = mod_sum.reshape(number, MOD)
-    else:
-        mod_sum = lax.psum_scatter(mod_part, "dp", scatter_dimension=0, tiled=True)
-    modulation = mod_sum + pieces["mod_b"]
-
     picker = (timesteps.reshape(-1)[:, None] == jnp.arange(STEPS_T)[None, :]).astype(jnp.float32)
     factors = jnp.dot(picker, roster.T, precision=HIGHEST)
     noise_flat = noise_field.reshape(number, -1)
     noised = factors[:, 0:1] * latents.reshape(number, -1) + factors[:, 1:2] * noise_flat
-    tokens = patchify(noised).astype(jnp.bfloat16)
-    target = patchify(noise_flat).reshape(-1, PDIM)
-    residual = (product(tokens.reshape(-1, PDIM), patch_low) + pieces["patch_b"]).reshape(
-        number, GRID * GRID, D
-    ) + places
+    own_ids = jnp.stack([timesteps, labels, drop_mask]).reshape(3, number)
     if direct:
-        mods = modulation.reshape(number, -1, 1, D)
+        tile = jnp.pad(own_ids.T.astype(jnp.float32), ((0, 8 - number), (0, LANES - 3)))
+        column = jnp.arange(2 * LANES)[None, None, :] % LANES // (PATCH * CHAN)
+        own_place = column == jnp.arange(GRID)[None, :, None]
+
+        def pick(values):
+            values = values.reshape(number * GRID, 1, PATCH * LANES)
+            return jnp.where(own_place, values, jnp.zeros_like(values)).reshape(-1, PATCH * LANES)
+
+        picked, wanted = pick(noised.astype(jnp.bfloat16)), pick(noise_flat)
+        rows_at, places_of = 0, {}
+        for piece_name, piece_dims in layout()[:8]:
+            height = math.prod(piece_dims) // D
+            places_of[piece_name] = (rows_at, height)
+            rows_at += height
         biases = pieces["block_b"].reshape(LAYERS, -1, 1, D)
-        residual, *kept_blocks = run_forward(residual.reshape(-1, D), mods, biases, packed_full)
-        residual = residual.reshape(number, GRID * GRID, D)
-    kept_all = []
-    gathered_all = []
-    spans_all = []
-    for layer_index in range(LAYERS):
-        if direct:
-            break
-        weights = tuple(
-            lax.all_gather(w[layer_index].astype(jnp.bfloat16), "dp", axis=0, tiled=True)
-            for w in (w_qkv, w_proj, w_fc1, w_fc2)
+        x_last, packed_full, mods, all_ids, hidden_t, condition, *kept_blocks = run_forward(
+            picked,
+            places,
+            tile,
+            w_qkv,
+            w_proj,
+            w_fc1,
+            w_fc2,
+            w_mod,
+            small[: rows_at * D].reshape(-1, LANES),
+            places_of,
+            biases,
+            number,
         )
-        spans = [
-            modulation[:, None, D * (6 * layer_index + i) : D * (6 * layer_index + i + 1)]
-            for i in range(6)
-        ]
-        residual, kept = layer_forward(residual, spans, weights, pieces["block_b"][layer_index])
-        kept_all.append(kept)
-        gathered_all.append(weights)
-        spans_all.append(spans)
-    final_shift = modulation[:, None, 6 * D * LAYERS : 6 * D * LAYERS + D]
-    final_scale = modulation[:, None, 6 * D * LAYERS + D :]
-    normed_f, inverse_f = norm_rows(residual)
-    final_in = (normed_f * (1.0 + final_scale) + final_shift).astype(jnp.bfloat16).reshape(-1, D)
-    output = product(final_in, head_low) + pieces["head_b"]
-    error = output - target
-    loss_own = jnp.sum(error * error)
-    grad_output = (error * (2.0 / count_all)).astype(jnp.bfloat16)
-    grad_head = product(final_in.T, grad_output)
-    grad_head_b = jnp.sum(grad_output.astype(jnp.float32), axis=0)
-    grad_final = product(grad_output, head_low.T).reshape(number, GRID * GRID, D)
-    final_grads = [jnp.sum(grad_final, axis=1), jnp.sum(grad_final * normed_f, axis=1)]
-    grad_res = norm_back(grad_final * (1.0 + final_scale), normed_f, inverse_f)
+        all_ids = all_ids[:, :number, :3].reshape(-1, 3).T.astype(jnp.int32)
+        hidden_t = hidden_t.reshape(everyone, 8, D)[:, :number].reshape(-1, D)
+        condition = condition.reshape(everyone, 8, D)[:, :number].reshape(-1, D)
+    else:
+        all_ids = lax.all_gather(own_ids, ("dp", "rep"), axis=0, tiled=False)
+        all_ids = all_ids.transpose(1, 0, 2).reshape(3, everyone * number)
+    features = time_features(all_ids[0]).astype(jnp.bfloat16)
+    if not direct:
+        hidden_t = product(features, time1_low) + pieces["time1_b"]
+    silu_t = jax.nn.silu(hidden_t).astype(jnp.bfloat16)
+    chosen = jnp.where(all_ids[2] == 1, CLASSES, all_ids[1])
+    onehot = (chosen[:, None] == jnp.arange(CLASSES + 1)[None, :]).astype(jnp.float32)
+    if not direct:
+        condition = (
+            product(silu_t, time2_low)
+            + pieces["time2_b"]
+            + jnp.dot(onehot, pieces["class_tab"], precision=HIGHEST)
+        )
+    silu_c = jax.nn.silu(condition).astype(jnp.bfloat16)
+    silu_rows = lax.dynamic_slice_in_dim(silu_c, first_row, rows_mod, axis=1)
+    if not direct:
+        tokens = patchify(noised).astype(jnp.bfloat16)
+        target = patchify(noise_flat).reshape(-1, PDIM)
+        residual = (product(tokens.reshape(-1, PDIM), patch_low) + pieces["patch_b"]).reshape(
+            number, GRID * GRID, D
+        ) + places
+        group_rows = lax.dynamic_index_in_dim(
+            silu_rows.reshape(dp_size, rep_size, number, rows_mod),
+            lax.axis_index("rep"),
+            axis=1,
+            keepdims=False,
+        ).reshape(dp_size * number, rows_mod)
+        mod_part = product(group_rows, mod_shard)
+        mod_sum = lax.psum_scatter(mod_part, "dp", scatter_dimension=0, tiled=True)
+        modulation = mod_sum + pieces["mod_b"]
     if direct:
-        head_row = jnp.pad(jnp.append(grad_head_b, loss_own), (0, D - PDIM - 1))[None]
-        head_sums = jnp.concatenate([grad_head.T, head_row, jnp.zeros((PDIM - 1, D), jnp.float32)])
-        head_mods = jnp.stack(final_grads, axis=1)[:, :, None]
+        head_wide = jnp.pad(head_low, ((0, 0), (0, LANES - PDIM)))
+        head_shift = jnp.pad(pieces["head_b"], (0, LANES - PDIM))[None]
         finals, mod_all, sums = run_backward(
-            grad_res.reshape(-1, D), mods, biases, tokens.reshape(-1, PDIM).T, head_sums, head_mods, packed_full, kept_blocks
+            count_all, x_last, mods, biases, picked, wanted, head_wide, head_shift, packed_full, kept_blocks
         )
         finals = finals.reshape(LAYERS, C_SIZE, -1, rows_mod // C_SIZE, D).transpose(0, 2, 1, 3, 4)
         grad_qkv, grad_proj, grad_fc1, grad_fc2 = unpack_shard(finals.reshape(LAYERS, -1, D), rows_mod)
         grad_mod = mod_all.reshape(everyone, -1, D)[:, : number * (MOD // D)].reshape(-1, MOD)
-        sum_patch = jnp.concatenate([sums[:PDIM], sums[2 * PDIM + 8 :][:1]]).reshape(-1)
-        sum_head = jnp.append(sums[PDIM : 2 * PDIM].T.reshape(-1), sums[2 * PDIM, :PDIM])
-        sum_bias = sums[3 * PDIM :].reshape(-1)
         loss_total = sums[2 * PDIM, PDIM]
     else:
+        kept_all = []
+        gathered_all = []
+        spans_all = []
+        for layer_index in range(LAYERS):
+            weights = tuple(
+                lax.all_gather(w[layer_index].astype(jnp.bfloat16), "dp", axis=0, tiled=True)
+                for w in (w_qkv, w_proj, w_fc1, w_fc2)
+            )
+            spans = [
+                modulation[:, None, D * (6 * layer_index + i) : D * (6 * layer_index + i + 1)]
+                for i in range(6)
+            ]
+            residual, kept = layer_forward(residual, spans, weights, pieces["block_b"][layer_index])
+            kept_all.append(kept)
+            gathered_all.append(weights)
+            spans_all.append(spans)
+        final_shift = modulation[:, None, 6 * D * LAYERS : 6 * D * LAYERS + D]
+        final_scale = modulation[:, None, 6 * D * LAYERS + D :]
+        normed_f, inverse_f = norm_rows(residual)
+        final_in = (normed_f * (1.0 + final_scale) + final_shift).astype(jnp.bfloat16).reshape(-1, D)
+        output = product(final_in, head_low) + pieces["head_b"]
+        error = output - target
+        loss_own = jnp.sum(error * error)
+        grad_output = (error * (2.0 / count_all)).astype(jnp.bfloat16)
+        grad_head = product(final_in.T, grad_output)
+        grad_head_b = jnp.sum(grad_output.astype(jnp.float32), axis=0)
+        grad_final = product(grad_output, head_low.T).reshape(number, GRID * GRID, D)
+        final_grads = [jnp.sum(grad_final, axis=1), jnp.sum(grad_final * normed_f, axis=1)]
+        grad_res = norm_back(grad_final * (1.0 + final_scale), normed_f, inverse_f)
         layer_spans = [None] * LAYERS
         bias_grads = [None] * LAYERS
         block_grads = [None] * LAYERS
@@ -1572,31 +1842,7 @@
 
     grad_wmod = product(silu_rows.T, grad_mod)
     grad_mod_b = jnp.sum(grad_mod.astype(jnp.float32), axis=0)
-    cond_rows = lax.all_gather(product(grad_mod, mod_shard.T), "dp", axis=1, tiled=True)
-    _, silu_pull = jax.vjp(jax.nn.silu, condition)
-    grad_cond = silu_pull(cond_rows)[0].astype(jnp.bfloat16)
-    grad_class = jnp.dot(onehot.T, grad_cond.astype(jnp.float32), precision=HIGHEST)
-    grad_time2 = product(silu_t.T, grad_cond)
-    grad_time2_b = jnp.sum(grad_cond.astype(jnp.float32), axis=0)
-    _, silu_time_pull = jax.vjp(jax.nn.silu, hidden_t)
-    grad_hidden_t = silu_time_pull(product(grad_cond, time2_low.T))[0].astype(jnp.bfloat16)
-    grad_time1 = product(features.T, grad_hidden_t)
-    grad_time1_b = jnp.sum(grad_hidden_t.astype(jnp.float32), axis=0)
-    small_grad = jnp.concatenate(
-        [
-            sum_patch,
-            grad_time1.reshape(-1),
-            grad_time1_b,
-            grad_time2.reshape(-1),
-            grad_time2_b,
-            grad_class.reshape(-1),
-            grad_mod_b,
-            sum_head,
-            sum_bias,
-        ]
-    )
     beta = 1.0 - STEP ** (-0.8)
-    rows_dp = lax.axis_size("dp")
     kinds = [
         (w_qkv, grad_qkv, row_qkv, col_qkv),
         (w_proj, grad_proj, row_proj, col_proj),
@@ -1617,9 +1863,58 @@
                 jnp.sum(weight * weight, axis=(-2, -1)),
             )
         )
-    shared = lax.psum(
-        jnp.concatenate([entry[k].reshape(-1) for k in range(1, 5) for entry in firsts]), "dp"
-    )
+    stats = jnp.concatenate([entry[k].reshape(-1) for k in range(1, 5) for entry in firsts])
+    cond_own = product(grad_mod, mod_shard.T)
+    if direct:
+        cond_tile = jnp.pad(cond_own, ((0, 0), (0, -rows_mod % LANES)))
+        stats_tile = jnp.pad(stats, (0, -stats.size % (everyone * 8 * LANES))).reshape(-1, LANES)
+        cond_all, shared = exchange(cond_tile, stats_tile)
+        cond_rows = cond_all[:, :, :rows_mod].transpose(1, 0, 2).reshape(-1, D)
+        shared = shared.reshape(-1)
+    else:
+        cond_rows = lax.all_gather(cond_own, "dp", axis=1, tiled=True)
+        shared = lax.psum(stats, "dp")
+    _, silu_pull = jax.vjp(jax.nn.silu, condition)
+    grad_cond = silu_pull(cond_rows)[0].astype(jnp.bfloat16)
+    grad_class = jnp.dot(onehot.T, grad_cond.astype(jnp.float32), precision=HIGHEST)
+    grad_time2 = product(silu_t.T, grad_cond)
+    grad_time2_b = jnp.sum(grad_cond.astype(jnp.float32), axis=0)
+    _, silu_time_pull = jax.vjp(jax.nn.silu, hidden_t)
+    grad_hidden_t = silu_time_pull(product(grad_cond, time2_low.T))[0].astype(jnp.bfloat16)
+    grad_time1 = product(features.T, grad_hidden_t)
+    grad_time1_b = jnp.sum(grad_hidden_t.astype(jnp.float32), axis=0)
+    if direct:
+        lined = line_up(
+            [
+                sums[:PDIM],
+                sums[2 * PDIM + 8 :][:1],
+                grad_time1,
+                grad_time1_b[None],
+                grad_time2,
+                grad_time2_b[None],
+                grad_class,
+                grad_mod_b.reshape(-1, D),
+                sums[PDIM : 2 * PDIM].T.reshape(-1, D),
+            ],
+            sums[2 * PDIM : 2 * PDIM + 1, :LANES],
+            sums[3 * PDIM :],
+        )
+        small_grad = lined.reshape(-1)[: small.shape[0]]
+    else:
+        small_grad = jnp.concatenate(
+            [
+                sum_patch,
+                grad_time1.reshape(-1),
+                grad_time1_b,
+                grad_time2.reshape(-1),
+                grad_time2_b,
+                grad_class.reshape(-1),
+                grad_mod_b,
+                sum_head,
+                sum_bias,
+            ]
+        )
+    rows_dp = dp_size
     parts = []
     offset = 0
     for k in range(1, 5):

time: 688 us -> 550 us (0.80)
  local copies, waits for them, and re-layouts: 93.1 us -> 52 us
  Pallas kernels: 440 us -> 404 us
  blocking collectives: 34.2 us -> 0 us
  between operations: 19.3 us -> 5.29 us
  matrix products: 18.2 us -> 6.47 us
    pallas_call x4, Pallas kernels: 440 us -> 404 us  [the longest x1 226 us: run_backward(): pl.pallas_call(partial(backward_kernel, groups, count_all), out_shape=[ja...]
    all_gather x1 -> x0, blocking collectives: 34.2 us -> none  [local(): lax.all_gather(product(grad_mod, mod_shard.T), 'dp', axis=1, tiled=True)]
    concatenate x3 -> x0, local copies, waits for them, and re-layouts: 32.3 us -> none  [the longest x1 31.2 us: local(): jnp.concatenate([sum_patch, grad_time1.reshape(-1), grad_time1_b, grad_ti...]
    unnamed x185 -> x152, local copies, waits for them, and re-layouts: 20.6 us -> 7.77 us
    dot_general x12 -> x5, matrix products: 17.5 us -> 6.02 us  [product(): return jnp.dot(left, right, preferred_element_type=jnp.float32)]
  transfers between devices with their start and end apart: 1 -> 0, of which waited for: 0 -> 0; matrix products, arithmetic and copies ran while one was open for 9% -> 0% of each run, Pallas kernels for 0% -> 0%
where the time goes in v4:
time: 550 us; the launch traced here: 544 us
  Pallas kernels  404 us (73%)
  other arithmetic  76.3 us (14%)
  local copies, waits for them, and re-layouts  52 us (9%)
  matrix products  6.47 us (1%)
    pallas_call x1, Pallas kernels, run_backward(): pl.pallas_call(partial(backward_kernel, groups, count_all), out_shape=[ja...  226 us
    pallas_call x1, Pallas kernels, run_forward(): pl.pallas_call(partial(forward_kernel, groups, places_of), out_shape=outs...  157 us
    pallas_call x1, Pallas kernels, exchange(): pl.pallas_call(exchange_kernel, out_shape=[jax.ShapeDtypeStruct((dps,) +...  20.6 us
    convert_element_type x5, other arithmetic, local(): new_weight.astype(jnp.bfloat16)  13.9 us

profile of v4, /device:TPU:0, one launch (start us, length us, event | category | flops | bytes accessed | tf_op | source)
XLA Modules:
  0.0 543.8 jit_solution(16757149648353313081)
XLA Ops:
  0.7 4.0 multiply_reduce_fusion
  4.7 0.9 multiply_reduce_fusion.5
  6.4 0.9 multiply_reduce_fusion.4
  7.3 0.9 multiply_reduce_fusion.3
  13.4 0.9 reduce.16
  16.5 0.9 broadcast_select_fusion
  17.3 2.6 multiply_sine_fusion.1
  19.9 1.1 pad_maximum_fusion.2.places
  21.0 2.6 multiply_reduce_fusion.2
  25.1 2.6 slice.248
  27.6 3.9 convert_element_type.156
  31.5 0.8 convert_element_type.141
  32.3 1.6 pad.21.head_w
  34.0 1.9 slice_bitcast_fusion.small
  35.9 157.2 %blocks_forward.1 = (f32[512,768]{1,0:T(8,128)}, bf16[2,8,1152,768]{3,2,1,0:T(8,128)(2,1)}, f32[2,14,1,768]{3,2,1,0:T(1,128)}, f32[32,8,128]{2,1,0:T(8,128)}, f3...) custom-call(bf16[512,256]{1,0:T(8,128)(2,1)} %bitcast.70, ...), custom_call_target="tpu_custom_call" | custom-call | tf_op jit(solution)/shard_map/blocks_forward/pallas_call | solution.py:824
  193.1 225.8 %blocks_backward.1 = (f32[2,2,576,768]{3,2,1,0:T(8,128)}, bf16[4,2,4,32,768]{4,3,2,1,0:T(8,128)(2,1)}, f32[64,768]{1,0:T(8,128)}) custom-call(f32[512,768]{1,0:T(8,128)} %get-tuple-element.47.x_last, f32[2,14,1,768]{3,2,1,0:T(1,128)} %get-tuple-element.48.mods, f32[2,8,1,768]{3,2,1,0:T(1,128)} %bitcast.75, bf16[512,256]{1,0:T(8,128)(2,1)} %bitcast.71, ...), custom_call_target="tpu_custom_call" | custom-call | tf_op jit(solution)/shard_map/blocks_backward/pallas_call | solution.py:1475
  418.9 1.3 slice.181
  420.1 3.6 reshape.462
  423.8 6.7 %copy.79 = f32[2,12,2,48,768]{4,3,2,1,0:T(8,128)} copy(f32[2,12,2,48,768]{4,3,1,2,0:T(8,128)} %bitcast.69) | data formatting | bytes 14155776 | tf_op jit(solution)/shard_map/transpose | solution.py:1769
  430.6 0.9 fusion
  432.1 0.9 slice_convert_fusion
  433.7 0.8 fusion.15
  434.8 1.2 slice.237
  436.1 0.9 reshape.482
  437.0 1.2 slice.249
  438.3 0.8 reshape.484
  441.0 3.3 add_reduce_fusion.2
  444.3 3.7 fusion.63
  448.0 0.8 fusion.59
  448.7 1.7 add_reduce_fusion.4
  452.5 2.1 divide_reduce_fusion.2
  455.8 2.2 divide_reduce_fusion.1
  459.3 1.7 add_reduce_fusion.6
  462.3 1.0 divide_reduce_fusion.3
  463.3 1.3 reshape.471
  464.7 1.3 reshape.465
  466.0 1.8 add_reduce_fusion
  468.6 1.2 copy-done.4
  469.8 0.8 divide_reduce_fusion
  470.8 1.4 concatenate.19
  472.9 20.6 %exchange_sums.1 = (f32[8,64,128]{2,1,0:T(8,128)}, f32[512,128]{1,0:T(8,128)}) custom-call(f32[64,128]{1,0:T(8,128)} %pad.23.cond, f32[512,128]{1,0:T(8,128)} %pad_bitcast_fusion.stats), custom_call_target="tpu_custom_call" | custom-call | tf_op jit(solution)/shard_map/exchange_sums/pallas_call | solution.py:1588
  493.5 1.7 convert_reduce_fusion.1
  495.2 1.0 slice_bitcast_fusion.1
  496.9 1.3 fusion.64
  499.5 0.8 slice_multiply_fusion.2
  502.6 0.9 divide_reduce_fusion.6
  503.5 1.5 fusion.14
  505.6 0.8 slice_multiply_fusion
  506.4 0.9 divide_reduce_fusion.5
  507.3 1.6 fusion.37
  508.9 1.0 copy.83
  509.9 0.8 convert_element_type.155
  510.7 1.9 convert_reduce_fusion.2
  512.6 1.0 fusion.18.refs_2_
  513.7 1.3 fusion.56
  515.7 1.2 copy-done.14
  516.9 2.0 fusion.57
  518.9 0.9 copy-done.21
  519.9 4.7 multiply_reduce_fusion.1
  525.4 4.3 fusion.54
  529.8 2.5 fusion.55
  532.5 1.6 copy-done.16
  534.1 5.3 fusion.50
  539.8 3.8 fusion.53
  (217 shorter events, 24.2 us)
Async XLA Ops:
  0.7 8.9 %copy-start = (f32[2,1000]{1,0:T(2,128)S(1)}, f32[2,1000]{1,0:T(2,128)}, u32[]{:S(2)}) copy-start(f32[2,1000]{1,0:T(2,128)} %param.28) | copy-start | bytes 24004
  0.7 4.1 copy-start.13
  0.7 5.0 copy-start.17
  0.7 5.6 %copy-start.10 = (f32[2,96,3072]{2,1,0:T(8,128)S(1)}, f32[2,96,3072]{2,1,0:T(8,128)}, u32[]{:S(2)}) copy-start(f32[2,96,3072]{2,1,0:T(8,128)} %w_fc1.1) | copy-start | bytes 7077892
  6.4 3.0 copy-start.72
  6.4 3.1 copy-start.73
  6.4 3.2 copy-start.74
  6.4 6.9 %copy-start.36 = (f32[2,1,4096]{2,1,0:T(1,128)S(1)}, f32[2,1,4096]{2,1,0:T(1,128)}, u32[]{:S(2)}) copy-start(f32[2,1,4096]{2,1,0:T(1,128)} %param.23) | copy-start | bytes 98308
  423.8 6.8 %copy-start.26 = (f32[64,768]{1,0:T(8,128)S(1)}, f32[64,768]{1,0:T(8,128)}, u32[]{:S(2)}) copy-start(f32[64,768]{1,0:T(8,128)} %get-tuple-element.56) | copy-start | bytes 589828
  423.8 6.8 %copy-start.2 = (f32[96,10752]{1,0:T(8,128)S(1)}, f32[96,10752]{1,0:T(8,128)}, u32[]{:S(2)}) copy-start(f32[96,10752]{1,0:T(8,128)} %w_mod.1) | copy-start | bytes 12386308
  430.6 3.1 copy-start.69
  444.3 3.7 copy-start.51
  448.0 3.8 copy-start.19
  448.7 3.8 copy-start.37
  451.1 6.9 %copy-start.41 = (f32[2,96]{1,0:T(2,128)}, f32[2,96]{1,0:T(2,128)S(1)}, u32[]{:S(2)}) copy-start(f32[2,96]{1,0:T(2,128)S(1)} %get-tuple-element.110) | copy-start | bytes 2308
  451.7 3.5 copy-start.43
  458.0 3.0 copy-start.68
  461.0 54.7 %copy-start.15 = (f32[2,96,2304]{2,1,0:T(8,128)}, f32[2,96,2304]{2,1,0:T(8,128)S(1)}, u32[]{:S(2)}) copy-start(f32[2,96,2304]{2,1,0:T(8,128)S(1)} %get-tuple-element.122) | copy-start | bytes 5308420
  467.8 2.9 copy-start.27
  467.8 2.9 copy-start.28
  467.8 2.9 copy-start.30
  467.8 2.9 copy-start.31
  467.8 2.9 copy-start.33
  467.8 2.9 copy-start.34
  467.9 2.9 copy-start.35
  467.9 2.9 copy-start.52
  467.9 2.9 copy-start.53
  467.9 2.9 copy-start.54
  467.9 2.9 copy-start.61
  467.9 2.9 copy-start.62
  467.9 2.9 copy-start.63
  467.9 2.8 copy-start.64
  467.9 2.8 copy-start.65
  469.8 23.7 %copy-start.22 = (f32[64,8,96]{2,1,0:T(8,128)S(1)}, f32[64,8,96]{2,1,0:T(8,128)}, u32[]{:S(2)}) copy-start(f32[64,8,96]{2,1,0:T(8,128)} %reshape.482) | copy-start | bytes 589828
  470.6 25.9 %copy-start.70 = (s32[64]{0:T(128)S(1)}, s32[64]{0:T(128)}, u32[]{:S(2)}) copy-start(s32[64]{0:T(128)} %get-tuple-element.159) | copy-start | bytes 772
  470.6 29.7 %copy-start.47 = (f32[2,768]{1,0:T(2,128)S(1)}, f32[2,768]{1,0:T(2,128)}, u32[]{:S(2)}) copy-start(f32[2,768]{1,0:T(2,128)} %param.41) | copy-start | bytes 18436
  470.6 30.5 %copy-start.48 = (f32[2,768]{1,0:T(2,128)S(1)}, f32[2,768]{1,0:T(2,128)}, u32[]{:S(2)}) copy-start(f32[2,768]{1,0:T(2,128)} %param.37) | copy-start | bytes 18436
  496.7 16.9 %copy-start.18 = (f32[2,96,768]{2,1,0:T(8,128)S(1)}, f32[2,96,768]{2,1,0:T(8,128)}, u32[]{:S(2)}) copy-start(f32[2,96,768]{2,1,0:T(8,128)} %w_proj.1) | copy-start | bytes 1769476
  496.8 16.9 %copy-start.20 = (f32[2,96,768]{2,1,0:T(8,128)S(1)}, f32[2,96,768]{2,1,0:T(8,128)}, u32[]{:S(2)}) copy-start(f32[2,96,768]{2,1,0:T(8,128)} %copy-done.19) | copy-start | bytes 1769476
  496.8 16.9 %copy-start.44 = (f32[2,96]{1,0:T(2,128)S(1)}, f32[2,96]{1,0:T(2,128)}, u32[]{:S(2)}) copy-start(f32[2,96]{1,0:T(2,128)} %copy-done.43) | copy-start | bytes 2308
  503.5 12.3 %copy-start.32 = (f32[2,2304]{1,0:T(2,128)}, f32[2,2304]{1,0:T(2,128)S(1)}, u32[]{:S(2)}) copy-start(f32[2,2304]{1,0:T(2,128)S(1)} %get-tuple-element.104) | copy-start | bytes 55300
  504.9 34.5 %copy-start.25 = (f32[10752]{0:T(1024)}, f32[10752]{0:T(1024)S(1)}, u32[]{:S(2)}) copy-start(f32[10752]{0:T(1024)S(1)} %get-tuple-element.88) | copy-start | bytes 129028
  507.3 22.4 %copy-start.29 = (f32[2,3072]{1,0:T(2,128)}, f32[2,3072]{1,0:T(2,128)S(1)}, u32[]{:S(2)}) copy-start(f32[2,3072]{1,0:T(2,128)S(1)} %get-tuple-element.96) | copy-start | bytes 73732
  507.3 6.3 %copy-start.40 = (f32[2,768]{1,0:T(2,128)S(1)}, f32[2,768]{1,0:T(2,128)}, u32[]{:S(2)}) copy-start(f32[2,768]{1,0:T(2,128)} %get-tuple-element.100) | copy-start | bytes 18436
  510.7 4.2 copy-start.23
  510.7 4.2 copy-start.24
  516.9 2.9 copy-start.21
  519.8 5.4 copy-start.9
  519.8 5.4 %copy-start.38 = (f32[2,384]{1,0:T(2,128)S(1)}, f32[2,384]{1,0:T(2,128)}, u32[]{:S(2)}) copy-start(f32[2,384]{1,0:T(2,128)} %copy-done.37) | copy-start | bytes 9220
  519.8 5.5 %copy-start.39 = (f32[2,768]{1,0:T(2,128)S(1)}, f32[2,768]{1,0:T(2,128)}, u32[]{:S(2)}) copy-start(f32[2,768]{1,0:T(2,128)} %get-tuple-element.92) | copy-start | bytes 18436
  519.8 5.5 %copy-start.58 = (f32[2]{0:T(128)S(1)}, f32[2]{0:T(128)}, u32[]{:S(2)}) copy-start(f32[2]{0:T(128)} %get-tuple-element.136) | copy-start | bytes 28
  519.9 5.5 %copy-start.59 = (f32[2]{0:T(128)S(1)}, f32[2]{0:T(128)}, u32[]{:S(2)}) copy-start(f32[2]{0:T(128)} %get-tuple-element.137) | copy-start | bytes 28
  519.9 5.5 %copy-start.60 = (f32[2]{0:T(128)S(1)}, f32[2]{0:T(128)}, u32[]{:S(2)}) copy-start(f32[2]{0:T(128)} %get-tuple-element.141) | copy-start | bytes 28
  525.3 4.4 copy-start.11
  525.4 4.4 copy-start.12
  525.4 4.4 copy-start.42
  525.4 4.4 copy-start.55
  525.4 4.4 copy-start.56
  525.4 4.4 copy-start.57
  529.8 4.3 copy-start.16
  534.1 5.3 copy-start.3
  534.1 5.7 %copy-start.5 = (f32[96,10752]{1,0:T(8,128)S(1)}, f32[96,10752]{1,0:T(8,128)}, u32[]{:S(2)}) copy-start(f32[96,10752]{1,0:T(8,128)} %copy-done.4) | copy-start | bytes 12386308
  534.1 5.7 %copy-start.50 = (f32[96]{0:T(128)S(1)}, f32[96]{0:T(128)}, u32[]{:S(2)}) copy-start(f32[96]{0:T(128)} %copy-done.49) | copy-start | bytes 1156
  539.8 3.8 copy-start.1
  (11 other events, 20.8 us)

commit v5 on v4

--- a/solution.py
+++ b/solution.py
@@ -373,16 +373,16 @@
 
 
 class Pace:
-    RATE = 48e3
     LATENCY = 2.2
 
-    def __init__(self):
+    def __init__(self, rate=48e3, along_z=4):
+        self.rate, self.along_z = rate, along_z
         self.now = 0.0
         self.free = {}
         self.entries = []
 
     def send(self, link, count):
-        rate = 10 * self.RATE if link == "c" else self.RATE
+        rate = 10 * self.rate if link == "c" else self.rate
         self.free[link] = max(self.now, self.free.get(link, 0.0)) + count / rate
         return self.free[link] + self.LATENCY
 
@@ -1024,7 +1024,7 @@
                 self.from_z.at[k - 1, pl.ds(self.at_most[group], half - part)],
                 self.sem("z", layer, group, k - 1), self.z_peers[k - 1],
             )
-        return self.pace.send("z", 4 * (half - part) * D * 2)
+        return self.pace.send("z", self.pace.along_z * (half - part) * D * 2)
 
     def on_z(self, layer, group):
         z, y, x, c = self.spot
@@ -1182,7 +1182,7 @@
     per = D // deep
     slots = w_v.shape[0]
     spot = place()
-    pace = Pace()
+    pace = Pace(52e3, 3.3)
     reduction = Reduction(
         pace, groups, shard, spot, (held, from_c, from_x, from_y, from_z, from_fin),
         {"c": (c_s, c_r), "x": (x_s, x_r), "y": (y_s, y_r), "z": (z_s, z_r), "e": (e_s, e_r), "f": (f_s, f_r), "keep": keep_sem},
@@ -1540,13 +1540,108 @@
     )(x_last, mods, biases, picked, wanted, head_w, head_b, full, *kept)
 
 
-def exchange_kernel(cond, stats, cond_all, total, pieces, c_s, c_r, p_s, p_r, g_s, g_r, r_s, r_r):
+KINDS = [("qkv", 0, 3), ("proj", 3, 1), ("fc1", 4, FF // D), ("fc2", 4 + FF // D, 1)]
+
+
+def statistics_kernel(
+    finals, mods_all, silu_rows, w_qkv, w_proj, w_fc1, w_fc2, w_mod,
+    row_qkv, row_proj, row_fc1, row_fc2, row_mod,
+    cond_all, mod_b_grad, picked, stats, qkv_row, proj_row, fc1_row, fc2_row, mod_row,
+    mod_grad, lined, sums, pieces, cond, c_s, c_r, p_s, p_r, g_s, g_r, r_s, r_r,
+):
     dp, rep = lax.axis_index("dp"), lax.axis_index("rep")
     dps, reps = Z_SIZE * Y_SIZE, X_SIZE * C_SIZE
     dp_peers = [((dp + k) % dps, rep) for k in range(1, dps)]
     rep_peers = [(dp, (rep + k) % reps) for k in range(1, reps)]
-    meet(dp_peers + rep_peers)
-    quarter = stats.shape[0] // reps
+    barrier = pltpu.get_barrier_semaphore()
+    for peer in dp_peers + rep_peers:
+        pl.semaphore_signal(barrier, inc=1, device_id=peer, device_id_type=MESH_IDS)
+    beta = 1.0 - STEP ** (-0.8)
+    shard, half = w_mod.shape[0], w_mod.shape[0] // 2
+    entries, images = picked.shape[0], picked.shape[1]
+    ways = D // LANES
+    per = 5 + FF_BLOCKS
+    mats = [(w_qkv, row_qkv, qkv_row), (w_proj, row_proj, proj_row), (w_fc1, row_fc1, fc1_row), (w_fc2, row_fc2, fc2_row)]
+    columns_all = LAYERS * per + entries
+    scalars = LAYERS * len(KINDS) + 1
+    at_row, at_weight = 2 * columns_all, 2 * columns_all + scalars
+
+    def over_rows(values):
+        return jnp.sum(values, axis=0, keepdims=True)
+
+    def over_all(values):
+        return jnp.sum(jnp.sum(values, axis=1, keepdims=True), axis=0, keepdims=True)
+
+    stats[...] = jnp.zeros_like(stats)
+    lined[...] = jnp.zeros_like(lined)
+    cond[...] = jnp.zeros_like(cond)
+
+    number = mods_all.shape[0] // (dps * reps)
+    here = images // (dps * reps)
+    row = lax.broadcasted_iota(jnp.int32, (images, mods_all.shape[0]), 0)
+    at = lax.broadcasted_iota(jnp.int32, (images, mods_all.shape[0]), 1)
+    back = jnp.zeros((images, shard), jnp.float32)
+    for k in range(entries):
+        wanted = row // here * number + row % here * entries + k
+        picked[k] = dot_nn((at == wanted).astype(jnp.bfloat16), mods_all[...]).astype(jnp.bfloat16)
+        mod_b_grad[pl.ds(k, 1)] = over_rows(picked[k].astype(jnp.float32))
+        back = back + dot_nt(picked[k], w_mod[:, k * D : (k + 1) * D].astype(jnp.bfloat16))
+    cond[:, pl.ds(0, shard)] = back
+
+    def first_pass(blocks, rows, row_old, width, row_out, weights, stat):
+        total = jnp.zeros((rows, 1), jnp.float32)
+        for grad, _ in blocks:
+            value = grad()
+            total = total + jnp.sum(value * value + EPS_ONE, axis=1, keepdims=True)
+        factor = beta * row_old + (1.0 - beta) * (total / width)
+        row_out(factor)
+        inverse = 1.0 / factor
+        for grad, index in blocks:
+            value = grad()
+            value = value * value
+            stats[pl.ds(index, 1)] += over_rows(value + EPS_ONE)
+            stats[pl.ds(columns_all + index, 1)] += over_rows(value * inverse)
+        stats[pl.ds(at_row + stat, 1)] += over_rows(factor)
+        for weight in weights:
+            stats[pl.ds(at_weight + stat, 1), pl.ds(0, 1)] += over_all(weight() * weight())
+
+    def block(layer, index, core):
+        return lambda: finals[layer, core, pl.ds(index * half, half)]
+
+    for layer in range(LAYERS):
+        for kind, (name, first, count) in enumerate(KINDS):
+            weight, row_old, row_new = mats[kind]
+            stat = layer * len(KINDS) + kind
+            tall = weight.shape[1] // shard
+            for part in range(tall):
+                for core in range(C_SIZE):
+                    rows = pl.ds(part * shard + core * half, half)
+                    blocks, weights = [], []
+                    for j in range(count):
+                        grad = block(layer, first + part + j, core)
+                        cut = pl.ds(j * D, D)
+                        blocks.append((grad, layer * per + first + j))
+                        weights.append(lambda rows=rows, cut=cut, weight=weight, layer=layer: weight[layer, rows, cut])
+
+                    def keep(value, rows=rows, row_new=row_new, layer=layer):
+                        row_new[layer, rows] = value
+
+                    first_pass(blocks, half, row_old[layer, rows], count * D, keep, weights, stat)
+    blocks, weights = [], []
+    for k in range(entries):
+        cut = pl.ds(k * D, D)
+        mod_grad[:, cut] = dot_tn(silu_rows[...], picked[k])
+        blocks.append((lambda cut=cut: mod_grad[:, cut], LAYERS * per + k))
+        weights.append(lambda cut=cut: w_mod[:, cut])
+
+    def keep_mod(value):
+        mod_row[...] = value
+
+    first_pass(blocks, shard, row_mod[...], entries * D, keep_mod, weights, scalars - 1)
+
+    for k in range(ways):
+        lined[pl.ds(k, stats.shape[0], stride=ways)] = stats[:, k * LANES : (k + 1) * LANES]
+    quarter = lined.shape[0] // reps
     size = quarter // dps
     copies = []
 
@@ -1556,49 +1651,172 @@
         copies.append(copy)
         return copy
 
-    def part(owner):
+    def part_of(owner):
         return pl.ds(pl.multiple_of(rep * quarter + owner * size, 8), size)
 
-    first = [go(stats.at[part(peer[0])], pieces.at[dp], (p_s, p_r), k, peer) for k, peer in enumerate(dp_peers)]
+    pl.semaphore_wait(barrier, len(dp_peers + rep_peers))
+    first = [go(lined.at[part_of(peer[0])], pieces.at[dp], (p_s, p_r), k, peer) for k, peer in enumerate(dp_peers)]
     spread = [go(cond, cond_all.at[dp], (c_s, c_r), k, peer) for k, peer in enumerate(dp_peers)]
     cond_all[dp] = cond[...]
-    pieces[dp] = stats[part(dp)]
+    pieces[dp] = lined[part_of(dp)]
     for copy in first:
         copy.wait_recv()
     value = pieces[0]
     for k in range(1, dps):
         value = value + pieces[k]
-    total[part(dp)] = value
-    own = total.at[part(dp)]
+    sums[part_of(dp)] = value
+    own = sums.at[part_of(dp)]
     second = [go(own, own, (g_s, g_r), k, peer) for k, peer in enumerate(dp_peers)]
     for copy in second:
         copy.wait_recv()
-    own = total.at[pl.ds(pl.multiple_of(rep * quarter, 8), quarter)]
+    own = sums.at[pl.ds(pl.multiple_of(rep * quarter, 8), quarter)]
     third = [go(own, own, (r_s, r_r), k, peer) for k, peer in enumerate(rep_peers)]
     for copy in third + spread:
         copy.wait_recv()
+    for k in range(ways):
+        stats[:, pl.ds(k * LANES, LANES)] = sums[pl.ds(k, stats.shape[0], stride=ways)]
+
     for copy in copies:
         copy.wait_send()
 
 
-def exchange(cond, stats):
+def update_kernel(
+    finals, picked, stats, silu_rows, w_qkv, w_proj, w_fc1, w_fc2, w_mod,
+    row_qkv, row_proj, row_fc1, row_fc2, row_mod, col_qkv, col_proj, col_fc1, col_fc2, col_mod,
+    qkv_new, qkv_grad, qkv_col, qkv_low,
+    proj_new, proj_grad, proj_col, proj_low,
+    fc1_new, fc1_grad, fc1_col, fc1_low,
+    fc2_new, fc2_grad, fc2_col, fc2_low,
+    mod_new, mod_grad, mod_col, mod_low,
+):
+    dps = Z_SIZE * Y_SIZE
+    beta = 1.0 - STEP ** (-0.8)
+    shard, half = w_mod.shape[0], w_mod.shape[0] // 2
+    entries = picked.shape[0]
+    per = 5 + FF_BLOCKS
+    mats = [
+        (w_qkv, row_qkv, col_qkv, qkv_new, qkv_grad, qkv_col, qkv_low),
+        (w_proj, row_proj, col_proj, proj_new, proj_grad, proj_col, proj_low),
+        (w_fc1, row_fc1, col_fc1, fc1_new, fc1_grad, fc1_col, fc1_low),
+        (w_fc2, row_fc2, col_fc2, fc2_new, fc2_grad, fc2_col, fc2_low),
+    ]
+    columns_all = LAYERS * per + entries
+    scalars = LAYERS * len(KINDS) + 1
+    at_row, at_weight = 2 * columns_all, 2 * columns_all + scalars
+
+    def scale_of(indices, col_old, col_new, stat, rows_all):
+        width = len(indices) * D
+        row_mean = stats[pl.ds(at_row + stat, 1), pl.ds(0, 1)] / rows_all
+        weight_rms = jnp.sqrt(stats[pl.ds(at_weight + stat, 1), pl.ds(0, 1)] / (rows_all * width))
+        update_sq = jnp.zeros((1, 1), jnp.float32)
+        sides = []
+        for j, index in enumerate(indices):
+            cut = slice(j * D, (j + 1) * D)
+            value = beta * col_old[:, cut] + (1.0 - beta) * (stats[pl.ds(index, 1)] / rows_all)
+            col_new(j, value)
+            update_sq = update_sq + jnp.sum(stats[pl.ds(columns_all + index, 1)] / value, axis=1, keepdims=True)
+            sides.append(lax.rsqrt(value))
+        update_rms = jnp.sqrt(row_mean * update_sq / (rows_all * width))
+        rate = RATE * jnp.maximum(0.001, weight_rms) / jnp.maximum(1.0, update_rms / CLIP)
+        return row_mean, rate, sides
+
+    for layer in range(LAYERS):
+        for kind, (name, first_square, count) in enumerate(KINDS):
+            weight, row_new, col_old, new, grad_out, col_new, low = mats[kind]
+            indices = [layer * per + first_square + j for j in range(count)]
+
+            def put(j, value, col_new=col_new, layer=layer):
+                col_new[layer, :, pl.ds(j * D, D)] = value
+
+            row_mean, rate, sides = scale_of(
+                indices, col_old[layer], put, layer * len(KINDS) + kind, float(weight.shape[1] * dps)
+            )
+            for step in range(weight.shape[1] // half):
+                rows = pl.ds(step * half, half)
+                left = rate * lax.rsqrt(row_new[layer, rows] / row_mean)
+                for j in range(count):
+                    cut = pl.ds(j * D, D)
+                    index = first_square + step // C_SIZE + j
+                    grad = finals[layer, step % C_SIZE, pl.ds(index * half, half)]
+                    grad_out[layer, rows, cut] = grad
+                    value = weight[layer, rows, cut] - grad * left * sides[j]
+                    new[layer, rows, cut] = value
+                    low[layer, rows, cut] = value.astype(jnp.bfloat16)
+
+    def put_mod(j, value):
+        mod_col[:, pl.ds(j * D, D)] = value
+
+    indices = [LAYERS * per + k for k in range(entries)]
+    row_mean, rate, sides = scale_of(indices, col_mod[...], put_mod, scalars - 1, float(shard * dps))
+    left = rate * lax.rsqrt(row_mod[...] / row_mean)
+    for k in range(entries):
+        cut = pl.ds(k * D, D)
+        grad = dot_tn(silu_rows[...], picked[k])
+        mod_grad[:, cut] = grad
+        value = w_mod[:, cut] - grad * left * sides[k]
+        mod_new[:, cut] = value
+        mod_low[:, cut] = value.astype(jnp.bfloat16)
+
+
+def run_update(finals, mods_all, silu_rows, kinds, w_mod, row_mod, col_mod):
     dps, reps = Z_SIZE * Y_SIZE, X_SIZE * C_SIZE
+    wide, low = jnp.float32, jnp.bfloat16
+    images, shard = silu_rows.shape
+    entries = w_mod.shape[1] // D
     vmem = pl.BlockSpec(memory_space=pltpu.VMEM)
     dma = pltpu.SemaphoreType.DMA
-    return pl.pallas_call(
-        exchange_kernel,
+    weights, rows, cols, outs = [], [], [], []
+    for weight, row, col in kinds + [(w_mod, row_mod, col_mod)]:
+        weights.append(weight)
+        rows.append(row[..., None])
+        cols.append(col[..., None, :])
+        outs += [
+            jax.ShapeDtypeStruct(weight.shape, wide),
+            jax.ShapeDtypeStruct(weight.shape, wide),
+            jax.ShapeDtypeStruct(cols[-1].shape, wide),
+            jax.ShapeDtypeStruct(weight.shape, low),
+        ]
+    used = 2 * (LAYERS * (5 + FF_BLOCKS) + entries) + 2 * (LAYERS * len(KINDS) + 1)
+    height = -(-used // 8) * 8
+    lined = -(-height * D // LANES // (8 * dps * reps)) * 8 * dps * reps
+    cond_all, mod_b_grad, picked, stats, *rows_new = pl.pallas_call(
+        statistics_kernel,
         out_shape=[
-            jax.ShapeDtypeStruct((dps,) + cond.shape, cond.dtype),
-            jax.ShapeDtypeStruct(stats.shape, stats.dtype),
-        ],
-        in_specs=[vmem, vmem],
-        out_specs=[vmem, vmem],
-        scratch_shapes=[pltpu.VMEM((dps, stats.shape[0] // (dps * reps), LANES), stats.dtype)]
+            jax.ShapeDtypeStruct((dps, images, LANES), wide),
+            jax.ShapeDtypeStruct((entries, D), wide),
+            jax.ShapeDtypeStruct((entries, images, D), low),
+            jax.ShapeDtypeStruct((height, D), wide),
+        ]
+        + [jax.ShapeDtypeStruct(row.shape, wide) for row in rows],
+        in_specs=[vmem] * (3 + 2 * len(weights)),
+        out_specs=[vmem] * (4 + len(rows)),
+        scratch_shapes=[
+            pltpu.VMEM(w_mod.shape, wide),
+            pltpu.VMEM((lined, LANES), wide),
+            pltpu.VMEM((lined, LANES), wide),
+            pltpu.VMEM((dps, lined // (dps * reps), LANES), wide),
+            pltpu.VMEM((images, LANES), wide),
+        ]
         + [dma((dps - 1,))] * 6
         + [dma((reps - 1,))] * 2,
-        compiler_params=pltpu.CompilerParams(collective_id=4, has_side_effects=True),
-        name="exchange_sums",
-    )(cond, stats)
+        compiler_params=pltpu.CompilerParams(
+            collective_id=4, has_side_effects=True, vmem_limit_bytes=48 * 2**20
+        ),
+        name="statistics",
+    )(finals, mods_all, silu_rows, *weights, *rows)
+    results = pl.pallas_call(
+        update_kernel,
+        out_shape=outs,
+        in_specs=[vmem] * (4 + 3 * len(weights)),
+        out_specs=[vmem] * len(outs),
+        compiler_params=pltpu.CompilerParams(vmem_limit_bytes=58 * 2**20),
+        name="update_weights",
+    )(finals, picked, stats, silu_rows, *weights, *rows_new, *cols)
+    groups = [results[4 * i : 4 * i + 4] for i in range(len(weights))]
+    return cond_all, mod_b_grad, [
+        (new, grad, row[..., 0], col.reshape(col.shape[:-2] + col.shape[-1:]), rounded)
+        for (new, grad, col, rounded), row in zip(groups, rows_new)
+    ]
 
 
 def line_up_kernel(offsets, *refs):
@@ -1637,17 +1855,6 @@
         compiler_params=pltpu.CompilerParams(vmem_limit_bytes=32 * 2**20),
         name="line_up",
     )(*pieces, first, tail)
-
-
-def unpack_shard(packed, rows):
-    count = FF // D
-    blocks = [packed[:, rows * i : rows * (i + 1)] for i in range(4 + count)]
-    return (
-        jnp.concatenate(blocks[:3], axis=-1),
-        blocks[3],
-        jnp.concatenate(blocks[4:], axis=-1),
-        packed[:, rows * (4 + count) :],
-    )
 
 
 def local(
@@ -1766,9 +1973,6 @@
         finals, mod_all, sums = run_backward(
             count_all, x_last, mods, biases, picked, wanted, head_wide, head_shift, packed_full, kept_blocks
         )
-        finals = finals.reshape(LAYERS, C_SIZE, -1, rows_mod // C_SIZE, D).transpose(0, 2, 1, 3, 4)
-        grad_qkv, grad_proj, grad_fc1, grad_fc2 = unpack_shard(finals.reshape(LAYERS, -1, D), rows_mod)
-        grad_mod = mod_all.reshape(everyone, -1, D)[:, : number * (MOD // D)].reshape(-1, MOD)
         loss_total = sums[2 * PDIM, PDIM]
     else:
         kept_all = []
@@ -1840,40 +2044,73 @@
         sum_head = jnp.append(summed[cut_patch:cut_head], summed[cut_bias : cut_bias + PDIM])
         sum_bias = summed[cut_head:cut_bias]
 
-    grad_wmod = product(silu_rows.T, grad_mod)
-    grad_mod_b = jnp.sum(grad_mod.astype(jnp.float32), axis=0)
     beta = 1.0 - STEP ** (-0.8)
-    kinds = [
-        (w_qkv, grad_qkv, row_qkv, col_qkv),
-        (w_proj, grad_proj, row_proj, col_proj),
-        (w_fc1, grad_fc1, row_fc1, col_fc1),
-        (w_fc2, grad_fc2, row_fc2, col_fc2),
-        (w_mod[None], grad_wmod[None], row_mod[None], col_mod[None]),
-    ]
-    firsts = []
-    for weight, grad, row, col in kinds:
-        square = grad * grad
-        row_new = beta * row + (1.0 - beta) * jnp.mean(square + EPS_ONE, axis=-1)
-        firsts.append(
-            (
-                row_new,
-                jnp.sum(square + EPS_ONE, axis=-2),
-                jnp.sum(square / row_new[:, :, None], axis=-2),
-                jnp.sum(row_new, axis=-1),
-                jnp.sum(weight * weight, axis=(-2, -1)),
+    if direct:
+        kinds = [
+            (w_qkv, row_qkv, col_qkv),
+            (w_proj, row_proj, col_proj),
+            (w_fc1, row_fc1, col_fc1),
+            (w_fc2, row_fc2, col_fc2),
+        ]
+        cond_all, grad_mod_b, results = run_update(
+            finals, mod_all.reshape(-1, D), silu_rows, kinds, w_mod, row_mod, col_mod
+        )
+        cond_rows = cond_all[:, :, :rows_mod].transpose(1, 0, 2).reshape(-1, D)
+        results[4] = tuple(entry[None] for entry in results[4])
+    else:
+        grad_wmod = product(silu_rows.T, grad_mod)
+        grad_mod_b = jnp.sum(grad_mod.astype(jnp.float32), axis=0)
+        kinds = [
+            (w_qkv, grad_qkv, row_qkv, col_qkv),
+            (w_proj, grad_proj, row_proj, col_proj),
+            (w_fc1, grad_fc1, row_fc1, col_fc1),
+            (w_fc2, grad_fc2, row_fc2, col_fc2),
+            (w_mod[None], grad_wmod[None], row_mod[None], col_mod[None]),
+        ]
+        firsts = []
+        for weight, grad, row, col in kinds:
+            square = grad * grad
+            row_new = beta * row + (1.0 - beta) * jnp.mean(square + EPS_ONE, axis=-1)
+            firsts.append(
+                (
+                    row_new,
+                    jnp.sum(square + EPS_ONE, axis=-2),
+                    jnp.sum(square / row_new[:, :, None], axis=-2),
+                    jnp.sum(row_new, axis=-1),
+                    jnp.sum(weight * weight, axis=(-2, -1)),
+                )
             )
-        )
-    stats = jnp.concatenate([entry[k].reshape(-1) for k in range(1, 5) for entry in firsts])
-    cond_own = product(grad_mod, mod_shard.T)
-    if direct:
-        cond_tile = jnp.pad(cond_own, ((0, 0), (0, -rows_mod % LANES)))
-        stats_tile = jnp.pad(stats, (0, -stats.size % (everyone * 8 * LANES))).reshape(-1, LANES)
-        cond_all, shared = exchange(cond_tile, stats_tile)
-        cond_rows = cond_all[:, :, :rows_mod].transpose(1, 0, 2).reshape(-1, D)
-        shared = shared.reshape(-1)
-    else:
-        cond_rows = lax.all_gather(cond_own, "dp", axis=1, tiled=True)
+        stats = jnp.concatenate([entry[k].reshape(-1) for k in range(1, 5) for entry in firsts])
+        cond_rows = lax.all_gather(product(grad_mod, mod_shard.T), "dp", axis=1, tiled=True)
         shared = lax.psum(stats, "dp")
+        rows_dp = dp_size
+        parts = []
+        offset = 0
+        for k in range(1, 5):
+            for entry in firsts:
+                parts.append(shared[offset : offset + entry[k].size].reshape(entry[k].shape))
+                offset += entry[k].size
+        seconds = []
+        for index, kind in enumerate(kinds):
+            weight, grad, row, col = kind
+            rows_all = weight.shape[1] * rows_dp
+            col_count = weight.shape[2]
+            col_sum, over_rows, row_sum, weight_sq = (parts[index + len(kinds) * k] for k in range(4))
+            row_mean = row_sum / rows_all
+            weight_rms = jnp.sqrt(weight_sq / (rows_all * col_count))
+            col_new = beta * col + (1.0 - beta) * col_sum / rows_all
+            update_sq = row_mean * jnp.sum(over_rows / col_new, axis=-1)
+            estimate = firsts[index][0][:, :, None] * col_new[:, None, :] / row_mean[:, None, None]
+            update = grad * lax.rsqrt(estimate)
+            seconds.append((update, col_new, weight_rms, update_sq / (rows_all * col_count)))
+        results = []
+        for kind, first, second in zip(kinds, firsts, seconds):
+            weight, grad = (kind[0], kind[1])
+            update, col_new, weight_rms, update_ms = second
+            update_rms = jnp.sqrt(update_ms)
+            update = update / jnp.maximum(1.0, update_rms / CLIP)[:, None, None]
+            new_weight = weight - (RATE * jnp.maximum(0.001, weight_rms))[:, None, None] * update
+            results.append((new_weight, grad, first[0], col_new, new_weight.astype(jnp.bfloat16)))
     _, silu_pull = jax.vjp(jax.nn.silu, condition)
     grad_cond = silu_pull(cond_rows)[0].astype(jnp.bfloat16)
     grad_class = jnp.dot(onehot.T, grad_cond.astype(jnp.float32), precision=HIGHEST)
@@ -1893,7 +2130,7 @@
                 grad_time2,
                 grad_time2_b[None],
                 grad_class,
-                grad_mod_b.reshape(-1, D),
+                grad_mod_b,
                 sums[PDIM : 2 * PDIM].T.reshape(-1, D),
             ],
             sums[2 * PDIM : 2 * PDIM + 1, :LANES],
@@ -1914,34 +2151,6 @@
                 sum_bias,
             ]
         )
-    rows_dp = dp_size
-    parts = []
-    offset = 0
-    for k in range(1, 5):
-        for entry in firsts:
-            parts.append(shared[offset : offset + entry[k].size].reshape(entry[k].shape))
-            offset += entry[k].size
-    seconds = []
-    for index, kind in enumerate(kinds):
-        weight, grad, row, col = kind
-        rows_all = weight.shape[1] * rows_dp
-        col_count = weight.shape[2]
-        col_sum, over_rows, row_sum, weight_sq = (parts[index + len(kinds) * k] for k in range(4))
-        row_mean = row_sum / rows_all
-        weight_rms = jnp.sqrt(weight_sq / (rows_all * col_count))
-        col_new = beta * col + (1.0 - beta) * col_sum / rows_all
-        update_sq = row_mean * jnp.sum(over_rows / col_new, axis=-1)
-        estimate = firsts[index][0][:, :, None] * col_new[:, None, :] / row_mean[:, None, None]
-        update = grad * lax.rsqrt(estimate)
-        seconds.append((update, col_new, weight_rms, update_sq / (rows_all * col_count)))
-    results = []
-    for kind, first, second in zip(kinds, firsts, seconds):
-        weight, grad = (kind[0], kind[1])
-        update, col_new, weight_rms, update_ms = second
-        update_rms = jnp.sqrt(update_ms)
-        update = update / jnp.maximum(1.0, update_rms / CLIP)[:, None, None]
-        new_weight = weight - (RATE * jnp.maximum(0.001, weight_rms))[:, None, None] * update
-        results.append((new_weight, grad, first[0], col_new, new_weight.astype(jnp.bfloat16)))
     square = small_grad * small_grad + EPS_ONE
     small_second_new = beta * small_second + (1.0 - beta) * square
     update = small_grad * lax.rsqrt(small_second_new)

time: 550 us -> 515 us (0.936)
  other arithmetic: 76.3 us -> 28.1 us
  Pallas kernels: 404 us -> 432 us
  local copies, waits for them, and re-layouts: 52 us -> 40.4 us
    pallas_call x1 -> x2, Pallas kernels: 20.6 us -> 49.6 us  [the longest x1 32 us: run_update(): pl.pallas_call(statistics_kernel, out_shape=[jax.ShapeDtypeStruct((dps, i...]
    reduce_sum x24 -> x0, other arithmetic: 28.7 us -> none  [the longest x5 7.41 us: local(): jnp.sum(weight * weight, axis=(-2, -1))]
    convert_element_type x5 -> x1, other arithmetic: 13.9 us -> 0.09 us  [local(): silu_c = jax.nn.silu(condition).astype(jnp.bfloat16)]
    reshape x13 -> x0, local copies, waits for them, and re-layouts: 8.95 us -> none  [the longest x6 4.52 us: local(): entry[k].reshape(-1)]
    unnamed x152 -> x74, local copies, waits for them, and re-layouts: 7.77 us -> 15.1 us
    transpose x1 -> x0, local copies, waits for them, and re-layouts: 6.73 us -> none  [local(): finals.reshape(LAYERS, C_SIZE, -1, rows_mod // C_SIZE, D)]
where the time goes in v5:
time: 515 us; the launch traced here: 508 us
  Pallas kernels  432 us (84%)
  local copies, waits for them, and re-layouts  40.4 us (8%)
  other arithmetic  28.1 us (5%)
    pallas_call x1, Pallas kernels, run_backward(): pl.pallas_call(partial(backward_kernel, groups, count_all), out_shape=[ja...  225 us
    pallas_call x1, Pallas kernels, run_forward(): pl.pallas_call(partial(forward_kernel, groups, places_of), out_shape=outs...  157 us
    pallas_call x1, Pallas kernels, run_update(): pl.pallas_call(statistics_kernel, out_shape=[jax.ShapeDtypeStruct((dps, i...  32 us
    pallas_call x1, Pallas kernels, run_update(): pl.pallas_call(update_kernel, out_shape=outs, in_specs=[vmem] * (4 + 3 *...  17.5 us
    unnamed x74, local copies, waits for them, and re-layouts  15.1 us

profile of v5, /device:TPU:0, one launch (start us, length us, event | category | flops | bytes accessed | tf_op | source)
XLA Modules:
  0.0 508.2 jit_solution(13950619935883784226)
XLA Ops:
  0.7 1.9 multiply_sine_fusion.1
  2.6 1.1 pad_maximum_fusion.places
  3.7 0.9 reduce.4
  4.6 0.8 fusion.20
  6.0 0.9 reduce.2
  7.0 0.7 broadcast_select_fusion.1
  7.8 0.7 slice.78
  8.5 1.9 slice_bitcast_fusion.small
  10.8 0.6 pad.12.ids
  11.4 157.2 %blocks_forward.1 = (f32[512,768]{1,0:T(8,128)}, bf16[2,8,1152,768]{3,2,1,0:T(8,128)(2,1)}, f32[2,14,1,768]{3,2,1,0:T(1,128)}, f32[32,8,128]{2,1,0:T(8,128)}, f3...) custom-call(bf16[512,256]{1,0:T(8,128)(2,1)} %bitcast.58, ...), custom_call_target="tpu_custom_call" | custom-call | tf_op jit(solution)/shard_map/blocks_forward/pallas_call | solution.py:824
  168.6 4.5 multiply_reduce_fusion.1
  173.1 1.2 copy-done.19
  174.5 0.7 pad.13.head_w
  175.2 0.9 broadcast_select_fusion
  176.1 0.7 slice.80
  176.7 0.5 pad_bitcast_fusion.head_b
  177.3 225.3 %blocks_backward.1 = (f32[2,2,576,768]{3,2,1,0:T(8,128)}, bf16[4,2,4,32,768]{4,3,2,1,0:T(8,128)(2,1)}, f32[64,768]{1,0:T(8,128)}) custom-call(f32[512,768]{1,0:T(8,128)} %get-tuple-element.74.x_last, f32[2,14,1,768]{3,2,1,0:T(1,128)} %get-tuple-element.75.mods, f32[2,8,1,768]{3,2,1,0:T(1,128)} %bitcast.62, bf16[512,256]{1,0:T(8,128)(2,1)} %bitcast.59, ...), custom_call_target="tpu_custom_call" | custom-call | tf_op jit(solution)/shard_map/blocks_backward/pallas_call | solution.py:1475
  402.6 1.2 slice.97
  404.3 0.3 copy-done.21
  405.1 1.4 copy-done.3
  406.5 32.0 %statistics.1 = (f32[8,64,128]{2,1,0:T(8,128)S(1)}, f32[14,768]{1,0:T(8,128)S(1)}, bf16[14,64,768]{2,1,0:T(8,128)(2,1)S(1)}, f32[88,768]{1,0:T(8,128)S(1)}, f32[...) custom-call(f32[2,2,576,768]{3,2,1,0:T(8,128)} %get-tuple-element.84, ...), custom_call_target="tpu_custom_call" | custom-call | tf_op jit(solution)/shard_map/statistics/pallas_call | solution.py:1782
  438.6 0.7 copy-done.4
  439.3 1.1 copy-done.6
  440.4 0.6 copy-done.7
  441.0 0.6 copy-done.9
  441.7 0.6 copy-done.11
  442.3 0.7 copy-done.13
  443.0 0.6 copy-done.14
  444.0 0.9 slice_convert_fusion
  445.0 1.2 fusion.9.refs_6_
  446.2 0.2 reshape.313
  446.8 1.2 slice.99
  448.2 0.5 fusion.36.refs_4_
  448.7 0.3 reshape.315
  449.0 2.6 slice.98
  451.6 3.3 convert_element_type.124
  454.9 1.8 convert_reduce_fusion.1
  456.9 0.3 fusion.15.refs_2_
  457.3 0.9 fusion.35
  458.2 0.9 copy.102
  459.1 1.2 reshape.317.refs_8_
  460.3 0.7 slice.84.refs_1_
  461.0 0.7 slice.93.refs_9_
  461.7 0.2 line_up.1
  461.9 1.7 copy-done.20
  463.7 4.5 multiply_reduce_fusion
  469.7 6.2 %fusion.32 = (bf16[861712]{0:T(1024)(128)(2,1)}, f32[861712]{0:T(1024)}) fusion(f32[861712]{0:T(1024)S(1)} %copy-done.18, f32[]{:T(128)S(6)} %max_shard_map.7, f32[861712]{0:T(1024)} %get-tuple-element.124, f32[861712]{0:T(1024)} %get-tuple-element.123, f32[]{:T(128)S(6)} %mul_shard_map.3), kind=kLoop, calls=%fused_computation.82 | loop fusion | flops 4308560 | bytes 15510824 | tf_op jit(solution)/shard_map/convert_element_type | solution.py:2190
  475.8 0.6 broadcast_in_dim.119.col_mod
  476.5 0.6 broadcast_in_dim.117.col_fc1
  477.1 0.6 broadcast_in_dim.115.col_qkv
  477.7 0.6 broadcast_in_dim.116.col_proj
  478.3 0.6 broadcast_in_dim.118.col_fc2
  479.0 17.5 %update_weights.1 = (f32[2,96,2304]{2,1,0:T(8,128)}, f32[2,96,2304]{2,1,0:T(8,128)}, f32[2,1,2304]{2,1,0:T(1,128)}, bf16[2,96,2304]{2,1,0:T(8,128)(2,1)}, f32[2,...) custom-call(f32[2,2,576,768]{3,2,1,0:T(8,128)} %get-tuple-element.84, ...), custom_call_target="tpu_custom_call" | custom-call | tf_op jit(solution)/shard_map/update_weights/pallas_call | solution.py:1807
  496.5 1.5 reduce.10
  498.0 1.4 copy.115
  499.4 1.3 copy.116
  500.7 1.3 copy.117
  502.0 1.3 copy.118
  503.3 0.8 reduce.8
  504.1 0.7 reduce.5
  504.7 0.7 reduce.6
  505.4 0.7 reduce.7
  506.1 0.6 reduce.9
  506.7 1.3 slice.81
  (100 shorter events, 3.5 us)
Async XLA Ops:
  0.7 4.0 copy-start
  0.7 7.1 %copy-start.17 = (f32[861712]{0:T(1024)S(1)}, f32[861712]{0:T(1024)}, u32[]{:S(2)}) copy-start(f32[861712]{0:T(1024)} %param.44) | copy-start | bytes 10340548
  7.7 2.7 copy-start.32
  7.7 2.8 copy-start.33
  7.7 2.9 copy-start.34
  173.1 1.2 copy-start.19
  177.3 226.9 %copy-start.27 = (f32[2,384]{1,0:T(2,128)S(1)}, f32[2,384]{1,0:T(2,128)}, u32[]{:S(2)}) copy-start(f32[2,384]{1,0:T(2,128)} %param.40) | copy-start | bytes 9220
  177.3 227.3 %copy-start.28 = (f32[2,96]{1,0:T(2,128)S(1)}, f32[2,96]{1,0:T(2,128)}, u32[]{:S(2)}) copy-start(f32[2,96]{1,0:T(2,128)} %param.34) | copy-start | bytes 2308
  177.3 227.5 %copy-start.29 = (f32[2,96]{1,0:T(2,128)S(1)}, f32[2,96]{1,0:T(2,128)}, u32[]{:S(2)}) copy-start(f32[2,96]{1,0:T(2,128)} %param.36) | copy-start | bytes 2308
  177.3 227.6 %copy-start.30 = (f32[2,96]{1,0:T(2,128)S(1)}, f32[2,96]{1,0:T(2,128)}, u32[]{:S(2)}) copy-start(f32[2,96]{1,0:T(2,128)} %param.38) | copy-start | bytes 2308
  177.3 227.7 %copy-start.31 = (f32[96]{0:T(128)S(1)}, f32[96]{0:T(128)}, u32[]{:S(2)}) copy-start(f32[96]{0:T(128)} %param.42) | copy-start | bytes 1156
  177.3 227.8 %copy-start.2 = (f32[2,96,768]{2,1,0:T(8,128)S(1)}, f32[2,96,768]{2,1,0:T(8,128)}, u32[]{:S(2)}) copy-start(f32[2,96,768]{2,1,0:T(8,128)} %w_proj.5) | copy-start | bytes 1769476
  403.9 0.7 copy-start.21
  404.1 34.5 %copy-start.16 = (bf16[64,96]{1,0:T(8,128)(2,1)}, bf16[64,96]{1,0:T(8,128)(2,1)S(1)}, u32[]{:S(2)}) copy-start(bf16[64,96]{1,0:T(8,128)(2,1)S(1)} %fusion.14.silu_rows) | copy-start | bytes 36868
  405.1 1.4 copy-start.3
  438.6 0.7 copy-start.4
  439.3 1.1 copy-start.6
  440.4 0.6 copy-start.7
  441.0 0.6 copy-start.9
  441.7 0.6 copy-start.11
  442.3 0.7 copy-start.13
  443.0 0.6 copy-start.14
  461.7 2.0 copy-start.20
  463.7 5.9 %copy-start.18 = (f32[861712]{0:T(1024)S(1)}, f32[861712]{0:T(1024)}, u32[]{:S(2)}) copy-start(f32[861712]{0:T(1024)} %param.44) | copy-start | bytes 10340548
  469.6 6.2 %copy-start.22 = (f32[10752]{0:T(1024)S(1)}, f32[10752]{0:T(1024)}, u32[]{:S(2)}) copy-start(f32[10752]{0:T(1024)} %param.43) | copy-start | bytes 129028
  469.6 6.9 %copy-start.23 = (f32[2,3072]{1,0:T(2,128)S(1)}, f32[2,3072]{1,0:T(2,128)}, u32[]{:S(2)}) copy-start(f32[2,3072]{1,0:T(2,128)} %param.39) | copy-start | bytes 73732
  469.6 7.5 %copy-start.24 = (f32[2,2304]{1,0:T(2,128)S(1)}, f32[2,2304]{1,0:T(2,128)}, u32[]{:S(2)}) copy-start(f32[2,2304]{1,0:T(2,128)} %param.35) | copy-start | bytes 55300
  469.6 8.1 %copy-start.25 = (f32[2,768]{1,0:T(2,128)S(1)}, f32[2,768]{1,0:T(2,128)}, u32[]{:S(2)}) copy-start(f32[2,768]{1,0:T(2,128)} %param.37) | copy-start | bytes 18436
  469.6 8.7 %copy-start.26 = (f32[2,768]{1,0:T(2,128)S(1)}, f32[2,768]{1,0:T(2,128)}, u32[]{:S(2)}) copy-start(f32[2,768]{1,0:T(2,128)} %param.41) | copy-start | bytes 18436
  478.9 24.4 %copy-start.5 = (f32[2,384,1]{2,1,0:T(8,128)S(1)}, f32[2,384,1]{2,1,0:T(8,128)}, u32[]{:S(2)}) copy-start(f32[2,384,1]{2,1,0:T(8,128)} %copy-done.4) | copy-start | bytes 9220
  478.9 25.1 %copy-start.12 = (f32[2,96,1]{2,1,0:T(8,128)S(1)}, f32[2,96,1]{2,1,0:T(8,128)}, u32[]{:S(2)}) copy-start(f32[2,96,1]{2,1,0:T(8,128)} %copy-done.11) | copy-start | bytes 2308
  478.9 25.8 %copy-start.10 = (f32[2,96,1]{2,1,0:T(8,128)S(1)}, f32[2,96,1]{2,1,0:T(8,128)}, u32[]{:S(2)}) copy-start(f32[2,96,1]{2,1,0:T(8,128)} %copy-done.9) | copy-start | bytes 2308
  478.9 26.5 %copy-start.8 = (f32[2,96,1]{2,1,0:T(8,128)S(1)}, f32[2,96,1]{2,1,0:T(8,128)}, u32[]{:S(2)}) copy-start(f32[2,96,1]{2,1,0:T(8,128)} %copy-done.7) | copy-start | bytes 2308
  478.9 27.2 %copy-start.15 = (f32[96,1]{1,0:T(8,128)S(1)}, f32[96,1]{1,0:T(8,128)}, u32[]{:S(2)}) copy-start(f32[96,1]{1,0:T(8,128)} %copy-done.14) | copy-start | bytes 1156
  479.0 29.0 %copy-start.1 = (f32[2,1000]{1,0:T(2,128)S(1)}, f32[2,1000]{1,0:T(2,128)}, u32[]{:S(2)}) copy-start(f32[2,1000]{1,0:T(2,128)} %param.28) | copy-start | bytes 24004

commit v6 on v5

--- a/solution.py
+++ b/solution.py
@@ -539,9 +539,9 @@
 
 def forward_kernel(
     groups, places_of, picked, places, ids, w_qkv, w_proj, w_fc1, w_fc2, w_mod, small, biases,
-    out, full, mods, ids_all, hidden_t, condition, x_h, proj_h, att_h, branch_a_h, middle_h, branch_b_h,
+    out, full, mods, ids_all, hidden_t, condition, time2_w, x_h, proj_h, att_h, branch_a_h, middle_h, branch_b_h,
     w_in, w_out, x_v, proj_v, att_v, branch_a, middle, branch_b, mixed, active,
-    mod_part, mod_y, mod_z, packed, raw, time1_w, time2_w, raw_sem, out_sem,
+    mod_part, mod_y, mod_z, packed, raw, time1_w, raw_sem, out_sem,
     w_sem, save_sem, i_s, i_r, z_s, z_r, y_s, y_r, x_s, x_r, c_s, c_r, keep_sem, my_s, my_r, mz_s, mz_r,
 ):
     tokens = picked.shape[0]
@@ -820,12 +820,13 @@
         jax.ShapeDtypeStruct((everyone,) + ids.shape, wide),
         jax.ShapeDtypeStruct((everyone * ids.shape[0], D), wide),
         jax.ShapeDtypeStruct((everyone * ids.shape[0], D), wide),
+        jax.ShapeDtypeStruct((D, D), low),
     ]
     return pl.pallas_call(
         partial(forward_kernel, groups, places_of),
         out_shape=outs + [jax.ShapeDtypeStruct((layers,) + shape, kind) for shape, kind in keep],
         in_specs=[vmem] * 3 + [anywhere] * 4 + [vmem] * 3,
-        out_specs=[anywhere, anywhere, vmem, vmem, vmem, vmem] + [anywhere] * len(keep),
+        out_specs=[anywhere, anywhere, vmem, vmem, vmem, vmem, vmem] + [anywhere] * len(keep),
         scratch_shapes=[
             pltpu.VMEM((layers, 4 + FF_BLOCKS, owners, shard, D), low),
             pltpu.VMEM((layers, FF_BLOCKS, D // deep, deep, D), low),
@@ -840,7 +841,6 @@
             pltpu.VMEM((layers, height, width), low),
             pltpu.VMEM((3, 2, shard, D), wide),
             pltpu.VMEM((FREQ, D), low),
-            pltpu.VMEM((D, D), low),
             dma((3, 2)),
             dma,
             dma((layers, 4 + 2 * FF_BLOCKS)),
@@ -1726,10 +1726,10 @@
             indices = [layer * per + first_square + j for j in range(count)]
 
             def put(j, value, col_new=col_new, layer=layer):
-                col_new[layer, :, pl.ds(j * D, D)] = value
+                col_new[pl.ds(layer, 1), pl.ds(j * D, D)] = value
 
             row_mean, rate, sides = scale_of(
-                indices, col_old[layer], put, layer * len(KINDS) + kind, float(weight.shape[1] * dps)
+                indices, col_old[pl.ds(layer, 1)], put, layer * len(KINDS) + kind, float(weight.shape[1] * dps)
             )
             for step in range(weight.shape[1] // half):
                 rows = pl.ds(step * half, half)
@@ -1769,7 +1769,7 @@
     for weight, row, col in kinds + [(w_mod, row_mod, col_mod)]:
         weights.append(weight)
         rows.append(row[..., None])
-        cols.append(col[..., None, :])
+        cols.append(col.reshape(-1, col.shape[-1]))
         outs += [
             jax.ShapeDtypeStruct(weight.shape, wide),
             jax.ShapeDtypeStruct(weight.shape, wide),
@@ -1814,7 +1814,7 @@
     )(finals, picked, stats, silu_rows, *weights, *rows_new, *cols)
     groups = [results[4 * i : 4 * i + 4] for i in range(len(weights))]
     return cond_all, mod_b_grad, [
-        (new, grad, row[..., 0], col.reshape(col.shape[:-2] + col.shape[-1:]), rounded)
+        (new, grad, row[..., 0], col.reshape(row.shape[:-2] + col.shape[-1:]), rounded)
         for (new, grad, col, rounded), row in zip(groups, rows_new)
     ]
 
@@ -1918,7 +1918,7 @@
             places_of[piece_name] = (rows_at, height)
             rows_at += height
         biases = pieces["block_b"].reshape(LAYERS, -1, 1, D)
-        x_last, packed_full, mods, all_ids, hidden_t, condition, *kept_blocks = run_forward(
+        x_last, packed_full, mods, all_ids, hidden_t, condition, time2_low, *kept_blocks = run_forward(
             picked,
             places,
             tile,

time: 515 us -> 497 us (0.965)
  local copies, waits for them, and re-layouts: 40.4 us -> 26 us
    unnamed x74 -> x58, local copies, waits for them, and re-layouts: 15.1 us -> 8.28 us
where the time goes in v6:
time: 497 us; the launch traced here: 490 us
  Pallas kernels  433 us (87%)
  local copies, waits for them, and re-layouts  26 us (5%)
  other arithmetic  25.2 us (5%)
    pallas_call x1, Pallas kernels, run_backward(): pl.pallas_call(partial(backward_kernel, groups, count_all), out_shape=[ja...  225 us
    pallas_call x1, Pallas kernels, run_forward(): pl.pallas_call(partial(forward_kernel, groups, places_of), out_shape=outs...  158 us
    pallas_call x1, Pallas kernels, run_update(): pl.pallas_call(statistics_kernel, out_shape=[jax.ShapeDtypeStruct((dps, i...  31.9 us
    pallas_call x1, Pallas kernels, run_update(): pl.pallas_call(update_kernel, out_shape=outs, in_specs=[vmem] * (4 + 3 *...  17.6 us

profile of v6, /device:TPU:0, one launch (start us, length us, event | category | flops | bytes accessed | tf_op | source)
XLA Modules:
  0.0 490.2 jit_solution(11827577174651563723)
XLA Ops:
  0.7 1.9 multiply_sine_fusion.1
  2.6 1.1 pad_maximum_fusion.places
  3.7 0.9 reduce.4
  4.6 0.8 fusion.18
  5.5 0.2 slice_reduce_fusion.1
  6.0 0.9 reduce.2
  7.0 0.7 broadcast_select_fusion.1
  7.8 0.7 slice.74
  8.5 1.9 slice_bitcast_fusion.small
  10.8 0.6 pad.12.ids
  11.4 157.5 %blocks_forward.1 = (f32[512,768]{1,0:T(8,128)}, bf16[2,8,1152,768]{3,2,1,0:T(8,128)(2,1)}, f32[2,14,1,768]{3,2,1,0:T(1,128)}, f32[32,8,128]{2,1,0:T(8,128)}, f3...) custom-call(bf16[512,256]{1,0:T(8,128)(2,1)} %bitcast.47, ...), custom_call_target="tpu_custom_call" | custom-call | tf_op jit(solution)/shard_map/blocks_forward/pallas_call | solution.py:825
  168.9 0.9 broadcast_select_fusion
  169.8 0.8 slice.107
  170.6 0.2 convert_element_type.104
  170.8 0.7 pad.13.head_w
  171.5 0.7 slice.76
  172.2 0.5 pad_bitcast_fusion.head_b
  172.7 225.4 %blocks_backward.1 = (f32[2,2,576,768]{3,2,1,0:T(8,128)}, bf16[4,2,4,32,768]{4,3,2,1,0:T(8,128)(2,1)}, f32[64,768]{1,0:T(8,128)}) custom-call(f32[512,768]{1,0:T(8,128)} %get-tuple-element.75.x_last, f32[2,14,1,768]{3,2,1,0:T(1,128)} %get-tuple-element.76.mods, f32[2,8,1,768]{3,2,1,0:T(1,128)} %bitcast.51, bf16[512,256]{1,0:T(8,128)(2,1)} %bitcast.48, ...), custom_call_target="tpu_custom_call" | custom-call | tf_op jit(solution)/shard_map/blocks_backward/pallas_call | solution.py:1475
  398.1 1.2 slice.92
  399.3 0.1 reshape.289
  399.6 0.2 copy.92.row_fc2
  399.8 0.1 copy.89.row_qkv
  400.3 1.4 copy-done.3
  401.7 31.9 %statistics.1 = (f32[8,64,128]{2,1,0:T(8,128)S(1)}, f32[14,768]{1,0:T(8,128)S(1)}, bf16[14,64,768]{2,1,0:T(8,128)(2,1)S(1)}, f32[88,768]{1,0:T(8,128)S(1)}, f32[...) custom-call(f32[2,2,576,768]{3,2,1,0:T(8,128)} %get-tuple-element.85, ...), custom_call_target="tpu_custom_call" | custom-call | tf_op jit(solution)/shard_map/statistics/pallas_call | solution.py:1782
  433.6 0.7 copy-done.4
  434.4 1.1 copy-done.6
  435.5 0.6 copy-done.7
  436.1 0.6 copy-done.9
  436.7 0.6 copy-done.11
  437.4 0.7 copy-done.13
  438.1 0.6 copy-done.14
  438.7 0.2 copy.95
  438.9 0.1 reshape.291
  439.1 0.9 slice_convert_fusion.1
  440.1 0.3 fusion.16.refs_6_
  440.4 0.2 reshape.294
  440.6 0.1 convert_reduce_fusion
  440.9 0.1 convert_element_type.117
  441.0 1.2 slice.93
  442.4 0.5 fusion.33.refs_4_
  442.9 0.2 broadcast_in_dim.101.refs_5_
  443.2 0.1 reshape.293
  443.3 1.8 convert_reduce_fusion.1
  445.1 0.2 fusion.9
  445.3 0.3 fusion.12.refs_2_
  445.6 0.9 fusion.32
  446.5 0.9 copy.102
  447.4 1.2 reshape.295.refs_8_
  448.6 0.7 slice.80.refs_1_
  449.3 0.7 slice.88.refs_9_
  450.0 0.2 line_up.1
  450.3 1.7 copy-done.19
  452.0 4.5 multiply_reduce_fusion
  457.2 1.5 multiply_reduce_fusion.1
  459.4 6.2 %fusion.29 = (bf16[861712]{0:T(1024)(128)(2,1)}, f32[861712]{0:T(1024)}) fusion(f32[861712]{0:T(1024)S(1)} %copy-done.18, f32[]{:T(128)S(6)} %max_shard_map.7, f32[861712]{0:T(1024)} %get-tuple-element.126, f32[861712]{0:T(1024)} %get-tuple-element.125, f32[]{:T(128)S(6)} %mul_shard_map.3), kind=kLoop, calls=%fused_computation.77 | loop fusion | flops 4308560 | bytes 15510824 | tf_op jit(solution)/shard_map/convert_element_type | solution.py:2190
  465.6 0.6 reshape.290.col_mod
  466.3 17.6 %update_weights.1 = (f32[2,96,2304]{2,1,0:T(8,128)}, f32[2,96,2304]{2,1,0:T(8,128)}, f32[2,2304]{1,0:T(2,128)}, bf16[2,96,2304]{2,1,0:T(8,128)(2,1)}, f32[2,96,7...) custom-call(f32[2,2,576,768]{3,2,1,0:T(8,128)} %get-tuple-element.85, ...), custom_call_target="tpu_custom_call" | custom-call | tf_op jit(solution)/shard_map/update_weights/pallas_call | solution.py:1807
  483.8 1.5 reduce.10
  485.3 0.8 reduce.8
  486.1 0.7 reduce.5
  486.8 0.7 reduce.6
  487.5 0.7 reduce.7
  488.1 0.6 reduce.9
  488.8 1.3 slice.77
  (79 shorter events, 1.9 us)
Async XLA Ops:
  0.7 4.0 copy-start
  0.7 7.1 %copy-start.17 = (f32[861712]{0:T(1024)S(1)}, f32[861712]{0:T(1024)}, u32[]{:S(2)}) copy-start(f32[861712]{0:T(1024)} %param.44) | copy-start | bytes 10340548
  7.7 2.7 copy-start.26
  7.7 2.8 copy-start.27
  7.7 2.9 copy-start.28
  172.7 226.9 %copy-start.21 = (f32[2,384]{1,0:T(2,128)S(1)}, f32[2,384]{1,0:T(2,128)}, u32[]{:S(2)}) copy-start(f32[2,384]{1,0:T(2,128)} %param.40) | copy-start | bytes 9220
  172.7 227.1 %copy-start.22 = (f32[2,96]{1,0:T(2,128)S(1)}, f32[2,96]{1,0:T(2,128)}, u32[]{:S(2)}) copy-start(f32[2,96]{1,0:T(2,128)} %param.34) | copy-start | bytes 2308
  172.7 227.3 %copy-start.23 = (f32[2,96]{1,0:T(2,128)S(1)}, f32[2,96]{1,0:T(2,128)}, u32[]{:S(2)}) copy-start(f32[2,96]{1,0:T(2,128)} %param.36) | copy-start | bytes 2308
  172.7 227.4 %copy-start.24 = (f32[2,96]{1,0:T(2,128)S(1)}, f32[2,96]{1,0:T(2,128)}, u32[]{:S(2)}) copy-start(f32[2,96]{1,0:T(2,128)} %param.38) | copy-start | bytes 2308
  172.7 227.5 %copy-start.25 = (f32[96]{0:T(128)S(1)}, f32[96]{0:T(128)}, u32[]{:S(2)}) copy-start(f32[96]{0:T(128)} %param.42) | copy-start | bytes 1156
  172.7 227.6 %copy-start.2 = (f32[2,96,768]{2,1,0:T(8,128)S(1)}, f32[2,96,768]{2,1,0:T(8,128)}, u32[]{:S(2)}) copy-start(f32[2,96,768]{2,1,0:T(8,128)} %w_proj.5) | copy-start | bytes 1769476
  399.6 34.0 %copy-start.16 = (bf16[64,96]{1,0:T(8,128)(2,1)}, bf16[64,96]{1,0:T(8,128)(2,1)S(1)}, u32[]{:S(2)}) copy-start(bf16[64,96]{1,0:T(8,128)(2,1)S(1)} %fusion.11.silu_rows) | copy-start | bytes 36868
  400.3 1.4 copy-start.3
  433.6 0.8 copy-start.4
  434.4 1.1 copy-start.6
  435.5 0.6 copy-start.7
  436.1 0.6 copy-start.9
  436.7 0.6 copy-start.11
  437.4 0.7 copy-start.13
  438.1 0.6 copy-start.14
  450.0 2.0 copy-start.19
  452.0 5.2 %copy-start.18 = (f32[861712]{0:T(1024)S(1)}, f32[861712]{0:T(1024)}, u32[]{:S(2)}) copy-start(f32[861712]{0:T(1024)} %param.44) | copy-start | bytes 10340548
  459.4 6.2 %copy-start.20 = (f32[10752]{0:T(1024)S(1)}, f32[10752]{0:T(1024)}, u32[]{:S(2)}) copy-start(f32[10752]{0:T(1024)} %param.43) | copy-start | bytes 129028
  466.2 19.1 %copy-start.5 = (f32[2,384,1]{2,1,0:T(8,128)S(1)}, f32[2,384,1]{2,1,0:T(8,128)}, u32[]{:S(2)}) copy-start(f32[2,384,1]{2,1,0:T(8,128)} %copy-done.4) | copy-start | bytes 9220
  466.2 19.9 %copy-start.12 = (f32[2,96,1]{2,1,0:T(8,128)S(1)}, f32[2,96,1]{2,1,0:T(8,128)}, u32[]{:S(2)}) copy-start(f32[2,96,1]{2,1,0:T(8,128)} %copy-done.11) | copy-start | bytes 2308
  466.2 20.5 %copy-start.10 = (f32[2,96,1]{2,1,0:T(8,128)S(1)}, f32[2,96,1]{2,1,0:T(8,128)}, u32[]{:S(2)}) copy-start(f32[2,96,1]{2,1,0:T(8,128)} %copy-done.9) | copy-start | bytes 2308
  466.2 21.2 %copy-start.8 = (f32[2,96,1]{2,1,0:T(8,128)S(1)}, f32[2,96,1]{2,1,0:T(8,128)}, u32[]{:S(2)}) copy-start(f32[2,96,1]{2,1,0:T(8,128)} %copy-done.7) | copy-start | bytes 2308
  466.2 21.9 %copy-start.15 = (f32[96,1]{1,0:T(8,128)S(1)}, f32[96,1]{1,0:T(8,128)}, u32[]{:S(2)}) copy-start(f32[96,1]{1,0:T(8,128)} %copy-done.14) | copy-start | bytes 1156
  466.3 23.8 %copy-start.1 = (f32[2,1000]{1,0:T(2,128)S(1)}, f32[2,1000]{1,0:T(2,128)}, u32[]{:S(2)}) copy-start(f32[2,1000]{1,0:T(2,128)} %param.28) | copy-start | bytes 24004
